TPU v7x, 256 devices: a whole 4x4x8 slice. The times are simulated.
256 devices in a mesh: lat: 32 (over x_hi, z, core), lon: 8 (over x_lo, y).
Axes of the slice: x: 4 (x_hi: 2, x_lo: 2; x = x_hi * 2 + x_lo), y: 4, z: 8, core: 2. Of those that a mesh axis runs over, the one named last changes fastest.
Arguments:
- input_field: bfloat16 [1, 384, 192, 1024], P(None, 'lat', None, 'lon'), may hold values from -6 to 6
- basis_values: float32 [384, 5, 5, 9], replicated, may hold values from -1.75 to 1.75
- support_reach: int32 [384, 5], replicated, may hold values from 0 to 2
- mix_weight: bfloat16 [4, 9, 48, 48], replicated, may hold values from -0.3125 to 0.3125
- filter_weight: float32 [384, 192], replicated, may hold values from -6 to 6
- cotangent: bfloat16 [1, 384, 192, 1024], P(None, 'lat', None, 'lon'), may hold values from -6 to 6
Outputs:
- block_out: bfloat16 [1, 384, 192, 1024], P(None, 'lat', None, 'lon')
- grad_field: bfloat16 [1, 384, 192, 1024], P(None, 'lat', None, 'lon')
Inputs may be any that keep to these rules, and one draw needn't show every extreme that they name: support_reach[i, a] is how many longitude cells on each side the filter reaches at latitude offset a - 2 from row i.
All inputs are finite; a program needn't handle non-finite values.
Results may differ from a plain program's by a relative error of at most 0.011.
Values may be sent and summed in bfloat16 or wider, within the bound.
No kernel may reach another device: no remote copies, remote signals or barrier semaphores. Data moves between devices by JAX's collectives and lax.ppermute only.
A program may use at most 192 MiB of HBM per device.

v0:
```python
import math

import jax
import jax.numpy as jnp
from jax import lax
from jax.sharding import PartitionSpec as P

huge_value = 2.0**60
tiny_value = 2.0 ** (-60)
log_step = 41.58883083359672


def padded_2(block, sides, width):
    for axis, dim in sides:
        count = lax.axis_size(axis)
        forward = [(i, i + 1) for i in range(count - 1)]
        forward.append((count - 1, 0))
        backward = [(target, source) for source, target in forward]
        low = lax.ppermute(
            lax.slice_in_dim(block, block.shape[dim] - width, None, axis=dim), axis, forward
        )
        high = lax.ppermute(lax.slice_in_dim(block, 0, width, axis=dim), axis, backward)
        block = jnp.concatenate([low, block, high], axis=dim)
    return block


def colatitude(nlat_total):
    return math.pi * (jnp.arange(nlat_total, dtype=jnp.float32) + 0.5) / nlat_total


def quadrature(nlat_total, nlon_total):
    return 2.0 * math.pi * math.pi / nlat_total * jnp.sin(colatitude(nlat_total)) / nlon_total


def order_scale(orders):
    return jnp.where(orders == 0, 1.0, 2.0).astype(jnp.float32)


def lon_table(degree_count, nlon_total):
    product = (
        jnp.arange(nlon_total, dtype=jnp.int32)[:, None]
        * jnp.arange(degree_count, dtype=jnp.int32)[None, :]
    )
    phase_angle = 2.0 * math.pi / nlon_total * (product % nlon_total).astype(jnp.float32)
    cosine = jnp.cos(phase_angle).astype(jnp.bfloat16)
    sine_part = jnp.sin(phase_angle).astype(jnp.bfloat16)
    return jnp.stack([cosine, -sine_part], axis=1)


def legendre(orders, degree_count, nlat_total):
    colat_angle = colatitude(nlat_total)
    cosine = jnp.cos(colat_angle)[None, :]
    log_sine = jnp.log(jnp.sin(colat_angle))[None, :]
    counter = jnp.arange(1, degree_count, dtype=jnp.float32)
    running = jnp.cumsum(jnp.log((2.0 * counter - 1.0) / (2.0 * counter)))
    cumulative = jnp.concatenate([jnp.zeros((1,), jnp.float32), running])
    select = (orders[:, None] == jnp.arange(degree_count, dtype=jnp.int32)[None, :]).astype(
        jnp.float32
    )
    norm_log = jnp.sum(select * cumulative[None, :], axis=1)
    order_real = orders.astype(jnp.float32)[:, None]
    base_log = (
        0.5 * jnp.log((2.0 * order_real + 1.0) / (4.0 * math.pi))
        + 0.5 * norm_log[:, None]
        + order_real * log_sine
    )
    empty_state = jnp.zeros((orders.shape[0], nlat_total), jnp.float32)

    def advance(carry, degree):
        latest, earlier, exponent = carry
        degree_real = degree.astype(jnp.float32)
        forward_gain = jnp.sqrt(
            jnp.maximum(4.0 * degree_real * degree_real - 1.0, 1.0)
            / jnp.maximum(degree_real * degree_real - order_real * order_real, 1.0)
        )
        back_gain = jnp.sqrt(
            jnp.maximum((degree_real - 1.0) ** 2 - order_real * order_real, 0.0)
            / jnp.maximum(4.0 * (degree_real - 1.0) ** 2 - 1.0, 1.0)
        )
        fresh = forward_gain * (cosine * latest - back_gain * earlier)
        start_here = degree == orders[:, None]
        fresh = jnp.where(start_here, 1.0, fresh)
        fresh = jnp.where(degree >= orders[:, None], fresh, 0.0)
        grown = jnp.abs(fresh) > huge_value
        fresh = jnp.where(grown, fresh * tiny_value, fresh)
        earlier_next = jnp.where(grown, latest * tiny_value, latest)
        exponent = exponent + grown.astype(jnp.float32)
        result_value = fresh * jnp.exp(base_log + exponent * log_step)
        return ((fresh, earlier_next, exponent), result_value.astype(jnp.bfloat16))

    degrees = jnp.arange(degree_count, dtype=jnp.int32)
    unused_carry, table = lax.scan(
        advance, (empty_state, empty_state, empty_state), degrees, unroll=32
    )
    return table


def stencil_weights(basis_values, support_reach):
    rim_width = basis_values.shape[1] // 2
    offsets = jnp.abs(jnp.arange(basis_values.shape[2], dtype=jnp.int32) - rim_width)
    inside = (offsets[None, None, :] <= support_reach[:, :, None]).astype(jnp.float32)
    return basis_values * inside[:, :, :, None]


def with_rims(grid_in, rim_width, row_start, nlat_total):
    padded = padded_2(grid_in, (("lat", 1), ("lon", 3)), rim_width)
    row_ids = row_start - rim_width + jnp.arange(padded.shape[1], dtype=jnp.int32)
    keep_rows = ((row_ids >= 0) & (row_ids < nlat_total)).astype(grid_in.dtype)
    return padded * keep_rows[None, :, None, None]


def basis_response(padded, weights_rows, basis_index, row_count, col_count):
    span_count = weights_rows.shape[1]
    total = jnp.zeros((padded.shape[0], row_count, padded.shape[2], col_count), jnp.float32)
    for lat_shift in range(span_count):
        for lon_shift in range(span_count):
            factor = weights_rows[:, lat_shift, lon_shift, basis_index][None, :, None, None]
            window = padded[
                :, lat_shift : lat_shift + row_count, :, lon_shift : lon_shift + col_count
            ]
            total = total + factor * window.astype(jnp.float32)
    return total


def adjoint_response(padded, weights_padded, basis_index, row_count, col_count):
    span_count = weights_padded.shape[1]
    last_shift = span_count - 1
    total = jnp.zeros((padded.shape[0], row_count, padded.shape[2], col_count), jnp.float32)
    for lat_shift in range(span_count):
        for lon_shift in range(span_count):
            first_row = last_shift - lat_shift
            first_col = last_shift - lon_shift
            factor = weights_padded[
                first_row : first_row + row_count, lat_shift, lon_shift, basis_index
            ][None, :, None, None]
            window = padded[
                :, first_row : first_row + row_count, :, first_col : first_col + col_count
            ]
            total = total + factor * window.astype(jnp.float32)
    return total


def spectral(grid_in, lon_tab, table, gains, pre_rows, pre_orders, post_rows, post_orders):
    circles = lax.all_to_all(grid_in, "lon", split_axis=2, concat_axis=3, tiled=True)
    samples, row_count, chan_part, nlon_total = circles.shape
    degree_count = lon_tab.shape[2]
    lon_spec = jnp.dot(
        circles.reshape(-1, nlon_total),
        lon_tab.reshape(nlon_total, 2 * degree_count),
        preferred_element_type=jnp.float32,
    )
    lon_spec = lon_spec.reshape(samples, row_count, chan_part, 2, degree_count)
    lon_spec = (
        lon_spec * pre_rows[None, :, None, None, None] * pre_orders[None, None, None, None, :]
    ).astype(jnp.bfloat16)
    columns = lax.all_to_all(lon_spec, "lat", split_axis=4, concat_axis=1, tiled=True)
    coeffs = jnp.einsum("stcrm,lmt->scrml", columns, table, preferred_element_type=jnp.float32)
    filtered = (coeffs * jnp.transpose(gains)[None, :, None, None, :]).astype(jnp.bfloat16)
    synthesis = jnp.einsum("scrml,lmt->stcrm", filtered, table, preferred_element_type=jnp.float32)
    synthesis = (
        synthesis * post_rows[None, :, None, None, None] * post_orders[None, None, None, None, :]
    ).astype(jnp.bfloat16)
    returned = lax.all_to_all(synthesis, "lat", split_axis=1, concat_axis=4, tiled=True)
    circle_out = jnp.einsum(
        "sicrm,jrm->sicj", returned, lon_tab, preferred_element_type=jnp.float32
    ).astype(jnp.bfloat16)
    return lax.all_to_all(circle_out, "lon", split_axis=3, concat_axis=2, tiled=True)


def local(input_field, basis_values, support_reach, mix_weight, filter_weight, cotangent):
    samples, row_count, channels, col_count = input_field.shape
    rim_width = basis_values.shape[1] // 2
    groups = mix_weight.shape[0]
    basis_count = mix_weight.shape[1]
    group_width = mix_weight.shape[2]
    degree_count = filter_weight.shape[0]
    lat_count = lax.axis_size("lat")
    lon_count = lax.axis_size("lon")
    nlat_total = row_count * lat_count
    nlon_total = col_count * lon_count
    row_start = lax.axis_index("lat") * row_count
    order_count = degree_count // lat_count
    orders = lax.axis_index("lat") * order_count + jnp.arange(order_count, dtype=jnp.int32)
    chan_count = channels // lon_count
    chan_start = lax.axis_index("lon") * chan_count
    table = legendre(orders, degree_count, nlat_total)
    weights_all = stencil_weights(basis_values, support_reach)
    weights_rows = lax.dynamic_slice_in_dim(weights_all, row_start, row_count, 0)
    padded_field = with_rims(input_field, rim_width, row_start, nlat_total)
    padded_rows = row_count + 2 * rim_width
    padded_cols = col_count + 2 * rim_width
    field_groups = padded_field.reshape(samples, padded_rows, groups, group_width, padded_cols)
    group_outs = []
    for group_index in range(groups):
        piece = field_groups[:, :, group_index]
        responses = jnp.stack(
            [
                basis_response(piece, weights_rows, basis_index, row_count, col_count).astype(
                    jnp.bfloat16
                )
                for basis_index in range(basis_count)
            ],
            axis=2,
        )
        group_outs.append(
            jnp.einsum(
                "sikcj,kco->sioj",
                responses,
                mix_weight[group_index],
                preferred_element_type=jnp.float32,
            )
        )
    conv_out = jnp.stack(group_outs, axis=2).reshape(samples, row_count, channels, col_count)
    activated = jax.nn.gelu(conv_out).astype(jnp.bfloat16)
    gains = lax.dynamic_slice_in_dim(filter_weight, chan_start, chan_count, 1)
    lon_tab = lon_table(degree_count, nlon_total)
    quad_all = quadrature(nlat_total, nlon_total)
    quad_rows = lax.dynamic_slice_in_dim(quad_all, row_start, row_count, 0)
    order_all = order_scale(jnp.arange(degree_count, dtype=jnp.int32))
    order_mine = order_scale(orders)
    ones_rows = jnp.ones((row_count,), jnp.float32)
    ones_lat = jnp.ones((nlat_total,), jnp.float32)
    ones_degrees = jnp.ones((degree_count,), jnp.float32)
    ones_mine = jnp.ones((order_count,), jnp.float32)
    branch = spectral(
        activated, lon_tab, table, gains, quad_rows, ones_degrees, ones_lat, order_mine
    )
    block_out = (input_field.astype(jnp.float32) + branch.astype(jnp.float32)).astype(jnp.bfloat16)
    cot_act = spectral(cotangent, lon_tab, table, gains, ones_rows, order_all, quad_all, ones_mine)
    slope = jax.vjp(jax.nn.gelu, conv_out)[1](cot_act.astype(jnp.float32))[0]
    cot_conv = slope.astype(jnp.bfloat16)
    padded_cot = with_rims(cot_conv, rim_width, row_start, nlat_total)
    grouped = padded_cot.reshape(samples, padded_rows, groups, group_width, padded_cols)
    weights_padded = lax.dynamic_slice_in_dim(
        jnp.pad(weights_all, ((rim_width, rim_width), (0, 0), (0, 0), (0, 0))),
        row_start,
        padded_rows,
        0,
    )
    group_grads = []
    for group_index in range(groups):
        mixed = jnp.einsum(
            "spoj,kco->spkcj",
            grouped[:, :, group_index],
            mix_weight[group_index],
            preferred_element_type=jnp.float32,
        ).astype(jnp.bfloat16)
        total = adjoint_response(mixed[:, :, 0], weights_padded, 0, row_count, col_count)
        for basis_index in range(1, basis_count):
            total = total + adjoint_response(
                mixed[:, :, basis_index], weights_padded, basis_index, row_count, col_count
            )
        group_grads.append(total)
    cot_field = jnp.stack(group_grads, axis=2).reshape(samples, row_count, channels, col_count)
    grad_field = (cotangent.astype(jnp.float32) + cot_field).astype(jnp.bfloat16)
    return (block_out, grad_field)


def solution(mesh):
    placed = (P(None, "lat", None, "lon"), P(), P(), P(), P(), P(None, "lat", None, "lon"))
    return jax.shard_map(
        local,
        mesh=mesh,
        in_specs=placed,
        out_specs=(P(None, "lat", None, "lon"), P(None, "lat", None, "lon")),
        check_vma=False,
    )
```

profile of v0, /device:TPU:2, one launch (start us, length us, event | category | flops | bytes accessed | tf_op | source)
XLA Modules:
  0.0 1127.0 jit_solution(13000094417426307145)
XLA Ops:
  17.0 6.7 fusion.498
  23.7 6.6 cosine_convert_fusion
  51.2 582.1 %while.23 = (s32[]{:T(128)}, f32[12,384]{1,0:T(8,128)S(1)}, f32[12,384]{1,0:T(8,128)S(1)}, f32[12,384]{1,0:T(8,128)S(1)}, bf16[12,32,12,384]{3,2,1,0:T(8,128)(2,...) while((s32[]{:T(128)}, f32[12,384]{1,0:T(8,128)S(1)}, ...), condition=%wide.region_4.5_spmd.clone.clone.clone.clone, body=%wide.region_3.4_spmd.clone.clone.clone.clone.sunk | while | flops 6867042 | bytes 4686698 | solution.py:92
  722.9 6.8 all-to-all-start.5
  740.7 7.3 all-to-all-done.5
  748.0 8.8 reshape.3804
  760.5 7.1 fusion.453
  792.3 7.6 all-to-all-done.6
  800.0 8.6 reshape.3806
  867.4 6.7 all-to-all-start
  884.7 6.6 add_add_fusion
  891.3 7.2 add_add_fusion.1
  898.9 7.2 add_add_fusion.2
  906.5 17.9 %add_bitcast_fusion = f32[1,12,1,48,128]{4,3,1,2,0:T(8,128)} fusion(f32[1,12,48,128]{3,2,1,0:T(8,128)S(1)} %add_add_fusion, bf16[1,16,48,132]{3,2,1,0:T(8,128)(2,1)S(1)} %get-tuple-element.824, bf16[1,16,48,132]{3,2,1,0:T(8,128)(2,1)S(1)} %get-tuple-element.825, bf16[1,16,48,132]{3,2,1,0:T(8,128)(2,1)S(1)} %get-tuple-element.826, ...), kind=kLoop, calls=%fused_computation.2732 | loop fusion | flops 33177600 | bytes 22715424 | tf_op jit(solution)/shard_map/stack | solution.py:254
  924.3 7.2 add_add_fusion.3
  944.9 8.7 reshape.3797
  958.5 27.6 %add_bitcast_fusion.1 = f32[1,12,1,48,128]{4,3,1,2,0:T(8,128)} fusion(f32[1,12,48,128]{3,2,1,0:T(8,128)} %add_add_fusion.1, bf16[1,16,48,132]{3,2,1,0:T(8,128)(2,1)} %get-tuple-element.815, bf16[1,16,48,132]{3,2,1,0:T(8,128)(2,1)} %get-tuple-element.816, bf16[1,16,48,132]{3,2,1,0:T(8,128)(2,1)} %get-tuple-element.817, ...), kind=kLoop, calls=%fused_computation.2736 | loop fusion | flops 33177600 | bytes 22715424 | tf_op jit(solution)/shard_map/stack | solution.py:254
  986.1 9.6 reshape.3798
  1002.4 7.8 fusion.454
  1016.3 8.7 reshape.3799
  1025.1 10.4 all-to-all-start.2
  1035.5 20.2 %add_bitcast_fusion.2 = f32[1,12,1,48,128]{4,3,1,2,0:T(8,128)} fusion(f32[1,12,48,128]{3,2,1,0:T(8,128)} %add_add_fusion.2, bf16[1,16,48,132]{3,2,1,0:T(8,128)(2,1)S(1)} %get-tuple-element.806, bf16[1,16,48,132]{3,2,1,0:T(8,128)(2,1)S(1)} %get-tuple-element.807, bf16[1,16,48,132]{3,2,1,0:T(8,128)(2,1)} %get-tuple-element.808, ...), kind=kLoop, calls=%fused_computation.2740 | loop fusion | flops 33177600 | bytes 22715424 | tf_op jit(solution)/shard_map/stack | solution.py:254
  1055.8 9.4 reshape.3800
  1089.3 16.8 %add_bitcast_fusion.3 = f32[1,12,1,48,128]{4,3,1,2,0:T(8,128)S(1)} fusion(f32[1,12,48,128]{3,2,1,0:T(8,128)S(1)} %copy-done.17, bf16[1,16,48,132]{3,2,1,0:T(8,128)(2,1)S(1)} %get-tuple-element.803, bf16[1,16,48,132]{3,2,1,0:T(8,128)(2,1)S(1)} %get-tuple-element.804, bf16[1,16,48,132]{3,2,1,0:T(8,128)(2,1)S(1)} %get-tuple-element.797, ...), kind=kLoop, calls=%fused_computation.2744 | loop fusion | flops 33177600 | bytes 22715424 | tf_op jit(solution)/shard_map/stack | solution.py:254
  (2416 shorter events, 631.1 us)
Async XLA Ops:
  0.6 634.2 %copy-start = (f32[384,192]{0,1:T(8,128)S(1)}, f32[384,192]{0,1:T(8,128)}, u32[]{:S(2)}) copy-start(f32[384,192]{0,1:T(8,128)} %param.12) | copy-start | bytes 884740
  3.1 706.9 %all-to-all-start.4 = ((bf16[1,12,192,128]{3,1,0,2:T(8,128)(2,1)}), bf16[1,12,192,128]{3,1,0,2:T(8,128)(2,1)}, u32[]{:S(2)}, u32[]{:S(2)}) async-start(bf16[1,12,192,128]{3,1,0,2:T(8,128)(2,1)} %copy.431), calls=%async_computation.4 | async-start | bytes 1572864 | tf_op jit(solution)/shard_map/all_to_all | solution.py:144
  9.5 21.4 %copy-start.494 = (s32[384,5]{0,1:T(8,128)S(1)}, s32[384,5]{0,1:T(8,128)}, u32[]{:S(2)}) copy-start(s32[384,5]{0,1:T(8,128)} %param.10) | copy-start | bytes 23044
  9.5 21.5 %copy-start.20 = (f32[384,5,5,9]{0,2,3,1:T(8,128)S(1)}, f32[384,5,5,9]{0,2,3,1:T(8,128)}, u32[]{:S(2)}) copy-start(f32[384,5,5,9]{0,2,3,1:T(8,128)} %param.9) | copy-start | bytes 1036804
  11.2 624.3 %collective-permute-start = (bf16[1,2,192,128]{3,2,1,0:T(8,128)(2,1)}, bf16[1,2,192,128]{3,2,1,0:T(8,128)(2,1)S(1)}, u32[]{:S(2)}, u32[]{:S(2)}) collective-permute-start(bf16[1,2,192,128]{3,2,1,0:T(8,128)(2,1)} %get-tuple-element.847), channel_id=1, source_target_pairs={{0,8},{8,16},{16,24},{24,32},{32,40},{40,48},{48,56},{56,64},{64,7... | collective-permute-start | bytes 294920 | tf_op jit(solution)/shard_map/ppermute | solution.py:19
  11.2 625.5 %collective-permute-start.1 = (bf16[1,2,192,128]{3,2,1,0:T(8,128)(2,1)}, bf16[1,2,192,128]{3,2,1,0:T(8,128)(2,1)S(1)}, u32[]{:S(2)}, u32[]{:S(2)}) collective-permute-start(bf16[1,2,192,128]{3,2,1,0:T(8,128)(2,1)} %get-tuple-element.846), channel_id=1, source_target_pairs={{8,0},{16,8},{24,16},{32,24},{40,32},{48,40},{56,48},{64,56},{72,6... | collective-permute-start | bytes 294920 | tf_op jit(solution)/shard_map/ppermute | solution.py:22
  634.8 125.6 %copy-start.25 = (f32[24,384]{1,0:T(8,128)}, f32[24,384]{1,0:T(8,128)S(1)}, u32[]{:S(2)}) copy-start(f32[24,384]{1,0:T(8,128)S(1)} %fusion.1420) | copy-start | bytes 110596
  639.6 6.8 collective-permute-start.3
  644.5 6.1 collective-permute-start.2
  722.9 25.1 %all-to-all-start.5 = ((bf16[32,2,3456]{2,1,0:T(2,128)(2,1)}), bf16[32,2,3456]{2,1,0:T(2,128)(2,1)}, u32[]{:S(2)}, u32[]{:S(2)}) async-start(bf16[32,2,3456]{2,1,0:T(2,128)(2,1)} %reshape.3803), calls=%async_computation.5 | async-start | bytes 884736 | tf_op jit(solution)/shard_map/all_to_all | solution.py:156
  776.6 23.4 %all-to-all-start.6 = ((bf16[32,2,3456]{2,1,0:T(2,128)(2,1)}), bf16[32,2,3456]{2,1,0:T(2,128)(2,1)}, u32[]{:S(2)}, u32[]{:S(2)}) async-start(bf16[32,2,3456]{2,1,0:T(2,128)(2,1)} %reshape.3805), calls=%async_computation.6 | async-start | bytes 884736 | tf_op jit(solution)/shard_map/all_to_all | solution.py:163
  824.7 13.8 %all-to-all-start.7 = ((bf16[8,2,18432]{2,1,0:T(2,128)(2,1)}), bf16[8,2,18432]{2,1,0:T(2,128)(2,1)S(1)}, u32[]{:S(2)}, u32[]{:S(2)}) async-start(bf16[8,2,18432]{2,1,0:T(2,128)(2,1)} %reshape.3807), calls=%async_computation.7 | async-start | bytes 1179648 | tf_op jit(solution)/shard_map/all_to_all | solution.py:167
  852.3 2.3 collective-permute-start.5
  852.4 7.7 collective-permute-start.4
  861.6 12.5 %collective-permute-start.7 = (bf16[1,16,192,2]{2,1,3,0:T(8,128)(2,1)S(1)}, bf16[1,16,192,2]{2,1,3,0:T(8,128)(2,1)S(1)}, u32[]{:S(2)}, u32[]{:S(2)}) collective-permute-start(bf16[1,16,192,2]{2,1,3,0:T(8,128)(2,1)S(1)} %copy.452), channel_id=1, source_target_pairs={{1,0},{2,1},{3,2},{4,3},{5,4},{6,5},{7,6},{0,7},{9,8},{10,9},{11,1... | collective-permute-start | bytes 36872 | tf_op jit(solution)/shard_map/ppermute | solution.py:22
  863.6 11.1 collective-permute-start.6
  867.4 64.1 %all-to-all-start = ((bf16[1,12,192,128]{3,1,0,2:T(8,128)(2,1)}), bf16[1,12,192,128]{3,1,0,2:T(8,128)(2,1)}, u32[]{:S(2)}, u32[]{:S(2)}) async-start(bf16[1,12,192,128]{3,1,0,2:T(8,128)(2,1)} %copy.416), calls=%async_computation | async-start | bytes 1572864 | tf_op jit(solution)/shard_map/all_to_all | solution.py:144
  953.7 32.4 %all-to-all-start.1 = ((bf16[32,2,3456]{2,1,0:T(2,128)(2,1)}), bf16[32,2,3456]{2,1,0:T(2,128)(2,1)}, u32[]{:S(2)}, u32[]{:S(2)}) async-start(bf16[32,2,3456]{2,1,0:T(2,128)(2,1)} %reshape.3797), calls=%async_computation.1 | async-start | bytes 884736 | tf_op jit(solution)/shard_map/all_to_all | solution.py:156
  1025.1 30.7 %all-to-all-start.2 = ((bf16[32,2,3456]{2,1,0:T(2,128)(2,1)}), bf16[32,2,3456]{2,1,0:T(2,128)(2,1)}, u32[]{:S(2)}, u32[]{:S(2)}) async-start(bf16[32,2,3456]{2,1,0:T(2,128)(2,1)} %reshape.3799), calls=%async_computation.2 | async-start | bytes 884736 | tf_op jit(solution)/shard_map/all_to_all | solution.py:163
  1076.3 12.6 %copy-start.38 = (f32[12]{0:T(128)S(1)}, f32[12]{0:T(128)}, u32[]{:S(2)}) copy-start(f32[12]{0:T(128)} %get-tuple-element.1250) | copy-start | bytes 148
  1083.1 25.2 %all-to-all-start.3 = ((bf16[8,2,18432]{2,1,0:T(2,128)(2,1)}), bf16[8,2,18432]{2,1,0:T(2,128)(2,1)S(1)}, u32[]{:S(2)}, u32[]{:S(2)}) async-start(bf16[8,2,18432]{2,1,0:T(2,128)(2,1)} %reshape.3801), calls=%async_computation.3 | async-start | bytes 1179648 | tf_op jit(solution)/shard_map/all_to_all | solution.py:167
  1089.3 16.8 %copy-start.16 = (f32[1,12,1,48,128]{4,3,1,2,0:T(8,128)S(1)}, f32[1,12,1,48,128]{4,3,1,2,0:T(8,128)}, u32[]{:S(2)}) copy-start(f32[1,12,1,48,128]{4,3,1,2,0:T(8,128)} %add_bitcast_fusion) | copy-start | bytes 884740
  1089.3 16.8 %copy-start.18 = (f32[1,12,1,48,128]{4,3,1,2,0:T(8,128)S(1)}, f32[1,12,1,48,128]{4,3,1,2,0:T(8,128)}, u32[]{:S(2)}) copy-start(f32[1,12,1,48,128]{4,3,1,2,0:T(8,128)} %add_bitcast_fusion.1) | copy-start | bytes 884740
  1089.3 16.8 %copy-start.19 = (f32[1,12,1,48,128]{4,3,1,2,0:T(8,128)S(1)}, f32[1,12,1,48,128]{4,3,1,2,0:T(8,128)}, u32[]{:S(2)}) copy-start(f32[1,12,1,48,128]{4,3,1,2,0:T(8,128)} %add_bitcast_fusion.2) | copy-start | bytes 884740
  (491 other events, 1929.7 us)
where the time goes:
time: 1150 us; the launch traced here: 1130 us
  other arithmetic  511 us (44%)
  loops' own time  256 us (22%)
  local copies, waits for them, and re-layouts  224 us (19%)
  starting transfers between devices  63.6 us (6%)
  matrix products  36.3 us (3%)
  waiting for transfers between devices  27.5 us (2%)
    another operation x1, loops' own time, legendre(): lax.scan(advance, (empty_state, empty_state, empty_state), degrees, unrol...  256 us
    eq x384, other arithmetic, advance(): start_here = degree == orders[:, None]  247 us
    unnamed x1014, local copies, waits for them, and re-layouts  94.8 us
    another operation x5, other arithmetic, local(): jnp.stack(group_grads, axis=2)  82.6 us
    unnamed x35, other arithmetic  62.6 us
    while x372, other arithmetic  43 us
    add x4, other arithmetic, local(): total + adjoint_response(mixed[:, :, basis_index], weights_padded, basis_...  28.1 us
  transfers between devices with their start and end apart: 16, of which 6 were waited for; matrix products, arithmetic and copies ran while one was open for 51% of the time, Pallas kernels for 0%

commit v1 on v0

v1 whole, which is shorter than its diff:
```python
import functools
import math

import jax
import jax.numpy as jnp
import numpy as np
from jax import lax
from jax.experimental import pallas as pl
from jax.experimental.pallas import tpu as pltpu
from jax.sharding import PartitionSpec as P

huge_value = 2.0**60
tiny_value = 2.0 ** (-60)
log_step = 41.58883083359672

f32 = jnp.float32
bf16 = jnp.bfloat16

NT = (((1,), (1,)), ((), ()))
NN = (((1,), (0,)), ((), ()))
TN = (((0,), (0,)), ((), ()))


def dot(a, b, dims=NN):
    return lax.dot_general(a, b, dims, preferred_element_type=f32)


def params(mib=20):
    return pltpu.CompilerParams(vmem_limit_bytes=mib * 1024 * 1024)


def vmem(count):
    return [pl.BlockSpec(memory_space=pltpu.VMEM)] * count


def cost(flops, nbytes):
    return pl.CostEstimate(flops=int(flops), bytes_accessed=int(nbytes), transcendentals=0)


def legendre_kernel(
    m_count, idx_ref, rise_ref, fall_ref, norm_ref, cos_ref, logsin_ref, table_ref, flip_ref, keep
):
    m_pad, lat = norm_ref.shape[0], cos_ref.shape[1]
    degrees = table_ref.shape[1]
    wide = lat // 128
    first = idx_ref[0] * m_count
    order = first + lax.broadcasted_iota(jnp.int32, (m_pad, 128), 0)
    order_real = order.astype(f32)
    square = order_real * order_real
    cosine = [
        jnp.broadcast_to(cos_ref[:, p * 128 : (p + 1) * 128], (m_pad, 128)) for p in range(wide)
    ]
    base = [
        norm_ref[...] + order_real * logsin_ref[:, p * 128 : (p + 1) * 128] for p in range(wide)
    ]

    def block(number, carry):
        latest, earlier, exponent, gain_b = carry
        latest, earlier, exponent = list(latest), list(earlier), list(exponent)
        for step in range(16):
            degree = number * 16 + step
            if step % 4 == 0:
                scale = []
                for p in range(wide):
                    grown = jnp.abs(latest[p]) > huge_value
                    latest[p] = jnp.where(grown, latest[p] * tiny_value, latest[p])
                    earlier[p] = jnp.where(grown, earlier[p] * tiny_value, earlier[p])
                    exponent[p] = jnp.where(grown, exponent[p] + 1.0, exponent[p])
                    scale.append(jnp.exp(base[p] + exponent[p] * log_step))
            d = degree.astype(f32)
            width = d * d - square
            inverse = lax.rsqrt(jnp.maximum(width, 1.0))
            gain_a = rise_ref[degree] * inverse
            both = gain_a * gain_b
            start_here = order == degree
            for p in range(wide):
                fresh = (gain_a * cosine[p]) * latest[p] - both * earlier[p]
                fresh = jnp.where(start_here, 1.0, fresh)
                earlier[p] = latest[p]
                latest[p] = fresh
                keep[p, step * m_pad : (step + 1) * m_pad, :] = fresh * scale[p]
            gain_b = fall_ref[degree] * (jnp.maximum(width, 0.0) * inverse)
        for m in range(m_count):
            rows = jnp.concatenate(
                [keep[part, pl.ds(m, 16, stride=m_pad), :] for part in range(wide)], axis=1
            )
            table_ref[m, pl.ds(pl.multiple_of(number * 16, 16), 16), :] = rows.astype(bf16)
        return tuple(latest), tuple(earlier), tuple(exponent), gain_b

    zero = jnp.zeros((m_pad, 128), f32)
    zeros = (zero,) * wide
    lax.fori_loop(0, degrees // 16, block, (zeros, zeros, zeros, zero))

    def turn(m, carry):
        flip_ref[m] = jnp.transpose(table_ref[m])
        return carry

    lax.fori_loop(0, m_count, turn, 0)


def legendre_tables(lat_index, degrees, lat_count, row_count, m_count):
    nlat = lat_count * row_count
    m_pad = 16
    place = np.arange(nlat)
    t = (place % lat_count) * row_count + place // lat_count
    theta = math.pi * (t + 0.5) / nlat
    counter = np.arange(1, degrees, dtype=np.float64)
    running = np.concatenate([[0.0], np.cumsum(np.log((2 * counter - 1) / (2 * counter)))])
    m = np.arange(degrees)
    norm = 0.5 * np.log((2 * m + 1) / (4 * math.pi)) + 0.5 * running
    norms = np.zeros((lat_count, m_pad, 1), np.float32)
    norms[:, :m_count, 0] = norm.reshape(lat_count, m_count)
    norm_mine = lax.dynamic_index_in_dim(jnp.asarray(norms), lat_index, 0, keepdims=False)
    rise = np.sqrt(np.maximum(4.0 * m * m - 1.0, 1.0)).astype(np.float32)
    fall = (1.0 / np.sqrt(np.maximum(4.0 * m * m - 1.0, 1.0))).astype(np.float32)
    shape = jax.ShapeDtypeStruct((m_count, degrees, nlat), bf16)
    flip = jax.ShapeDtypeStruct((m_count, nlat, degrees), bf16)
    return pl.pallas_call(
        functools.partial(legendre_kernel, m_count),
        out_shape=(shape, flip),
        in_specs=[pl.BlockSpec(memory_space=pltpu.SMEM)] * 3 + vmem(3),
        out_specs=tuple(vmem(2)),
        scratch_shapes=[pltpu.VMEM((nlat // 128, 16 * m_pad, 128), f32)],
        compiler_params=params(),
        cost_estimate=cost(2e9, 7e6),
        name="legendre_tables",
    )(
        lat_index[None],
        jnp.asarray(rise),
        jnp.asarray(fall),
        norm_mine,
        jnp.asarray(np.cos(theta)[None].astype(np.float32)),
        jnp.asarray(np.log(np.sin(theta))[None].astype(np.float32)),
    )


def lon_kernel(near_cos_ref, near_sin_ref, far_ref, tab_ref):
    blocks = tab_ref.shape[1] // 128
    for b in range(blocks):
        tab_ref[:, b * 128 : (b + 1) * 128] = (
            near_cos_ref[...] * far_ref[:, b : b + 1]
            - near_sin_ref[...] * far_ref[:, blocks + b : blocks + b + 1]
        ).astype(bf16)


def lon_table(degrees, nlon, owners):
    per = degrees // owners
    row = np.arange(2 * degrees)
    m_np = row // (2 * per) * per + row % per
    m = jnp.asarray(m_np.astype(np.int32))
    shift = jnp.asarray(((row // per % 2) * (nlon // 4)).astype(np.int32))
    low = jnp.arange(128, dtype=jnp.int32)
    angle = (m[:, None] * low[None, :] + shift[:, None]) % nlon
    phase = 2.0 * math.pi / nlon * angle.astype(f32)
    far = 2.0 * math.pi * ((m_np[:, None] * np.arange(nlon // 128)[None] * 128) % nlon) / nlon
    far = np.concatenate([np.cos(far), np.sin(far)], axis=1).astype(np.float32)
    return pl.pallas_call(
        lon_kernel,
        out_shape=jax.ShapeDtypeStruct((2 * degrees, nlon), bf16),
        in_specs=vmem(3),
        out_specs=vmem(1)[0],
        compiler_params=params(),
        cost_estimate=cost(1e8, 3e6),
        name="lon_table",
    )(jnp.cos(phase), jnp.sin(phase), jnp.asarray(far))


def pack_rows(z, k_count):
    third = k_count // 3
    rest = [z[j * third : (j + 1) * third, 256:288] for j in range(3)]
    rest.append(jnp.zeros((third, 32), f32))
    return jnp.concatenate([z[:, 0:128], z[:, 128:256], jnp.concatenate(rest, axis=1)], axis=0)


def analysis_kernel(k_count, cotangent_pass, *refs):
    circ_ref, tab_ref, quad_ref = refs[:3]
    out_ref, keep = refs[-2:]
    sectors = circ_ref.shape[0]
    lines = keep.shape[1]
    owners = out_ref.shape[0]
    height = 2 * k_count + k_count // 3
    if len(circ_ref.shape) == 3:
        parts = [circ_ref[s, 0:lines, :] for s in range(sectors)]
    else:
        parts = [circ_ref[s].astype(f32).reshape(lines, -1).astype(bf16) for s in range(sectors)]
    circ = jnp.concatenate(parts, axis=1)
    z = dot(tab_ref[...], circ, NT)
    if cotangent_pass:
        row = lax.broadcasted_iota(jnp.int32, z.shape, 0)
        z = z * jnp.where((row == 0) | (row == k_count // 2), 1.0, 2.0)
    else:
        z = z * quad_ref[...]
    keep[...] = z
    for e in range(owners):
        piece = keep[e * k_count : (e + 1) * k_count, :]
        out_ref[e, 0:height, :] = pack_rows(piece, k_count).astype(bf16)
        if len(refs) > 5:
            out_ref[e, height:, :] = refs[3][e]


def analysis(circ, lines, tab, quad_lanes, owners, cotangent_pass, beside=()):
    k_count = tab.shape[0] // owners
    height = (2 * k_count + k_count // 3) * (1 + len(beside))
    return pl.pallas_call(
        functools.partial(analysis_kernel, k_count, cotangent_pass),
        out_shape=jax.ShapeDtypeStruct((owners, height, 128), bf16),
        in_specs=vmem(3 + len(beside)),
        out_specs=vmem(1)[0],
        scratch_shapes=[pltpu.VMEM((tab.shape[0], lines), f32)],
        compiler_params=params(),
        cost_estimate=cost(2 * tab.shape[0] * tab.shape[1] * lines, 3e6),
        name="analysis",
    )(circ, tab, quad_lanes, *beside)


def filter_kernel(
    m_count, chans, cotangent_pass, idx_ref, recv_ref, table_ref, flip_ref, gain_ref, post_ref,
    out_ref, took, give
):
    places, height, _ = out_ref.shape
    k_count = 2 * m_count
    third = k_count // 3
    nlat = table_ref.shape[1]
    rows = nlat // places
    lane = lax.broadcasted_iota(jnp.int32, (places, 128), 1)

    def load(d, carry):
        at = pl.ds(pl.multiple_of(d * height, 8), height)
        took[at, :] = recv_ref[d, 0:height, :].astype(f32)
        return carry

    lax.fori_loop(0, places, load, 0, unroll=4)
    give[2 * k_count * places :, :] = jnp.zeros((third * places, 128), f32)

    def one(mm, carry):
        blocks = []
        for r in range(2):
            k = r * m_count + mm
            b0 = took[pl.ds(k, places, stride=height), :]
            b1 = took[pl.ds(k_count + k, places, stride=height), :]
            b2 = took[pl.ds(2 * k_count + k % third, places, stride=height), :]
            b2 = pltpu.roll(b2, (128 - 32 * (k // third)) % 128, 1)
            blocks.append((b0, b1, b2))
        columns = []
        for i in range(rows):
            start = i * chans
            first, last = start // 128, (start + chans - 1) // 128
            total = None
            for q, b in enumerate(blocks):
                if first == last:
                    source = b[first]
                else:
                    source = jnp.where(lane < 64, b[last], b[first])
                shift = (q * chans - start) % 128
                source = pltpu.roll(source, shift, 1) if shift else source
                total = source if total is None else jnp.where(lane < chans, total, source)
            columns.append(total)
        x = jnp.concatenate(columns, axis=0).astype(bf16)
        coeffs = dot(table_ref[mm], x)
        filtered = (coeffs * gain_ref[...]).astype(bf16)
        y = dot(flip_ref[mm], filtered)
        if cotangent_pass:
            y = y * post_ref[...]
        else:
            y = y * jnp.where(idx_ref[0] * m_count + mm == 0, 1.0, 2.0).astype(f32)
        for r in range(2):
            k = r * m_count + mm
            outs = [jnp.zeros((places, 128), f32) for _ in range(3)]
            for i in range(rows):
                start = i * chans
                first, last = start // 128, (start + chans - 1) // 128
                shift = (start - r * chans) % 128
                piece = y[i * places : (i + 1) * places, :]
                piece = pltpu.roll(piece, shift, 1) if shift else piece
                for part in range(first, last + 1):
                    lo, hi = start - part * 128, start + chans - part * 128
                    outs[part] = jnp.where((lane >= lo) & (lane < hi), piece, outs[part])
            give[pl.ds(k * places, places), :] = outs[0]
            give[pl.ds((k_count + k) * places, places), :] = outs[1]
            at = pl.ds((2 * k_count + k % third) * places, places)
            give[at, :] = give[at, :] + pltpu.roll(outs[2], 32 * (k // third), 1)
        return carry

    lax.fori_loop(0, m_count, one, 0, unroll=2)

    def store(d, carry):
        out_ref[d] = give[pl.ds(d, height, stride=places), :].astype(bf16)
        return carry

    lax.fori_loop(0, places, store, 0, unroll=4)


def filter_step(lat_index, recv, table, flip, gains, post, chans, cotangent_pass):
    places = recv.shape[0]
    m_count, degrees, nlat = table.shape
    height = 4 * m_count + 2 * m_count // 3
    return pl.pallas_call(
        functools.partial(filter_kernel, m_count, chans, cotangent_pass),
        out_shape=jax.ShapeDtypeStruct((places, height, 128), bf16),
        in_specs=[pl.BlockSpec(memory_space=pltpu.SMEM)] + vmem(5),
        out_specs=vmem(1)[0],
        scratch_shapes=[
            pltpu.VMEM((places * height, 128), f32),
            pltpu.VMEM((places * height, 128), f32),
        ],
        compiler_params=params(),
        cost_estimate=cost(4 * m_count * degrees * nlat * 128, 9e6),
        name="filter_step",
    )(lat_index[None], recv, table, flip, gains, post)


def synthesis_kernel(which, recv_ref, tab_ref, out_ref):
    owners = recv_ref.shape[0]
    k_count = tab_ref.shape[0] // owners
    height = 2 * k_count + k_count // 3
    sectors, rows, chans, cols = out_ref.shape
    left, middle, right = [], [], []
    for e in range(owners):
        v = recv_ref[e, which * height : (which + 1) * height, :].astype(f32)
        left.append(v[0:k_count])
        middle.append(v[k_count : 2 * k_count])
        rest = v[2 * k_count :]
        for j in range(3):
            right.append(pltpu.roll(rest, (128 - 32 * j) % 128, 1) if j else rest)
    flat = [jnp.transpose(jnp.concatenate(part, axis=0)) for part in (left, middle, right)]
    s = jnp.concatenate([flat[0], flat[1], flat[2][0:32]], axis=0).astype(bf16)
    circ = dot(s, tab_ref[...])
    for sector in range(sectors):
        piece = circ[:, sector * cols : (sector + 1) * cols]
        out_ref[sector] = piece.reshape(rows, chans, cols).astype(bf16)


def synthesis(recv, tab, which, shape):
    return pl.pallas_call(
        functools.partial(synthesis_kernel, which),
        out_shape=jax.ShapeDtypeStruct(shape, bf16),
        in_specs=vmem(2),
        out_specs=vmem(1)[0],
        compiler_params=params(),
        cost_estimate=cost(2 * tab.shape[0] * tab.shape[1] * shape[1] * shape[2], 5e6),
        name="synthesis",
    )(recv, tab)


def chunk_blocks(count, edge):
    inner = list(range(edge, count - edge))
    return (
        [list(range(edge))]
        + [inner[k : k + 4] for k in range(0, len(inner), 4)]
        + [list(range(count - edge, count))]
    )


def edge_blocks(flat, edge):
    row = lax.broadcasted_iota(jnp.int32, (16, 128), 0)
    lane = lax.broadcasted_iota(jnp.int32, (16, 128), 1)
    first = []
    last = []
    for chunks in chunk_blocks(flat.shape[0] // 128, edge):
        total = jnp.zeros((16, 128), f32)
        for v, chunk in enumerate(chunks):
            head = (row == 2 * v + lane) & (lane < 2)
            tail = (row - 8 - 2 * v == lane - 126) & (lane >= 126)
            select = jnp.where(head | tail, 1.0, 0.0).astype(bf16)
            total = total + dot(select, flat[chunk * 128 : (chunk + 1) * 128], NT)
        first.append(total[0:8])
        last.append(total[8:16])
    return jnp.concatenate(first, axis=0), jnp.concatenate(last, axis=0)


def start_kernel(edge, idx_ref, cot_ref, field_ref, out_ref):
    sectors, height, cols = out_ref.shape
    rows, channels, _ = cot_ref.shape
    chans = channels // sectors
    body = rows * chans
    field = field_ref[...].reshape(rows * channels, cols)
    first, last = edge_blocks(field, edge)
    for b in range(sectors):
        parts = [cot_ref[i, b * chans : (b + 1) * chans, :].astype(f32) for i in range(rows)]
        right = lax.rem(idx_ref[0] + 1, sectors) == b
        parts.append(jnp.where(right, last, first))
        room = height - body - first.shape[0]
        parts.append(jnp.zeros((room, cols), f32))
        out_ref[b] = jnp.concatenate(parts, axis=0).astype(bf16)


def start_step(lon_index, cot, field, sectors, edge):
    rows, channels, cols = cot.shape
    body = rows * channels // sectors
    blocks = len(chunk_blocks(rows * channels // 128, edge))
    height = -(-(body + 8 * blocks) // 16) * 16
    return pl.pallas_call(
        functools.partial(start_kernel, edge),
        out_shape=jax.ShapeDtypeStruct((sectors, height, cols), bf16),
        in_specs=[pl.BlockSpec(memory_space=pltpu.SMEM)] + vmem(2),
        out_specs=vmem(1)[0],
        compiler_params=params(),
        cost_estimate=cost(1e8, 2e6),
        name="start",
    )(lon_index[None], cot, field)


def conv_body(
    idx_ref, x_ref, low_ref, high_ref, left_ref, right_ref, stencil_ref, mix_ref,
    xs, hs, resp, band, blend, emit
):
    rows, channels, cols = x_ref.shape
    groups, taps, width = mix_ref.shape[0], mix_ref.shape[1] // mix_ref.shape[2], mix_ref.shape[2]
    ext = hs.shape[0] // channels
    rim = (ext - rows) // 2
    span = 2 * rim + 1
    edge = rim * channels // 128
    k_pad = 16
    xs[0 : rim * channels, :] = low_ref[0 : rim * channels].astype(f32)
    xs[rim * channels : (rim + rows) * channels, :] = (
        x_ref[...].astype(f32).reshape(rows * channels, cols)
    )
    xs[(rim + rows) * channels :, :] = high_ref[0 : rim * channels].astype(f32)

    row = lax.broadcasted_iota(jnp.int32, (16, cols), 0)
    lane = lax.broadcasted_iota(jnp.int32, (16, cols), 1)

    def spread(left, right, chunks, base):
        turned = jnp.transpose(jnp.concatenate([left.astype(f32), right.astype(f32)], axis=0))
        turned = turned.astype(bf16)
        for v, chunk in enumerate(chunks):
            ahead = (row - 2 * v == lane - (cols - 2)) & (lane >= cols - 2)
            behind = (row - 8 - 2 * v == lane) & (lane < 2)
            put = jnp.where(ahead | behind, 1.0, 0.0).astype(bf16)
            at = (base + chunk) * 128
            hs[at : at + 128, :] = dot(turned, put)

    lists = chunk_blocks(rows * channels // 128, edge)
    tail = rim * channels
    spread(low_ref[tail : tail + 8], low_ref[tail + 8 : tail + 16], range(edge), 0)
    spread(high_ref[tail : tail + 8], high_ref[tail + 8 : tail + 16], range(edge),
           edge + rows * channels // 128)
    for u, chunks in enumerate(lists):
        at = slice(8 * u, 8 * u + 8)
        spread(left_ref[at], right_ref[at], chunks, edge)

    tap = lax.broadcasted_iota(jnp.int32, (stencil_ref.shape[1], 128), 0)
    slot = lax.broadcasted_iota(jnp.int32, (stencil_ref.shape[1], 128), 1)
    source = idx_ref[0] * rows - rim + slot % ext
    inside = (source >= 0) & (source < idx_ref[1]) & (slot < span * ext)
    for i in range(rows):
        hit = inside & (tap // span == slot // ext) & (slot % ext == i + tap % span)
        place = jnp.where(hit, 1.0, 0.0).astype(bf16)
        band[i * k_pad : (i + 1) * k_pad, :] = dot(
            stencil_ref[i * k_pad : (i + 1) * k_pad, :], place
        ).astype(bf16)

    depth = width * k_pad
    pair_row = lax.broadcasted_iota(jnp.int32, (taps * width, depth), 0)
    pair_lane = lax.broadcasted_iota(jnp.int32, (taps * width, depth), 1)
    place = jnp.where(
        pair_lane == (pair_row % width) * k_pad + pair_row // width, 1.0, 0.0
    ).astype(bf16)
    for g in range(groups):
        blend[g] = dot(mix_ref[g], place, TN).astype(bf16)

    stencil = band[:, 0 : span * ext]

    def column(c):
        x = xs[pl.ds(c, ext, stride=channels), :]
        h = hs[pl.ds(c, ext, stride=channels), :]
        pieces = []
        for s in range(-rim, rim + 1):
            if s == 0:
                pieces.append(x)
                continue
            inside = (lane + s >= 0) & (lane + s < cols)
            shift = (-s) % cols
            pieces.append(
                jnp.where(inside, pltpu.roll(x, shift, 1), pltpu.roll(h, shift, 1))
            )
        return jnp.concatenate([p.astype(bf16) for p in pieces], axis=0)

    for g in range(groups):

        def pair(number, carry):
            c = g * width + 2 * number
            both = jnp.concatenate([column(c), column(c + 1)], axis=1)
            r = dot(stencil, both).astype(bf16)
            at = pl.multiple_of(number * 2 * k_pad, k_pad)
            resp[:, pl.ds(at, k_pad), :] = r[:, 0:cols].reshape(rows, k_pad, cols)
            resp[:, pl.ds(at + k_pad, k_pad), :] = r[:, cols:].reshape(rows, k_pad, cols)
            return carry

        lax.fori_loop(0, width // 2, pair, 0, unroll=8)
        for i in range(0, rows, 2):
            operand = jnp.concatenate([resp[i], resp[i + 1]], axis=1)
            out = dot(blend[g], operand)
            emit(g, i, out[:, 0:cols])
            emit(g, i + 1, out[:, cols:])


def forward_kernel(*refs):
    act_ref, slope_ref = refs[8:10]
    width = refs[7].shape[2]
    chans = act_ref.shape[2]
    root = math.sqrt(2.0 / math.pi)

    def emit(g, i, v):
        square = v * v
        t = jnp.tanh(root * v * (1.0 + 0.044715 * square))
        half = 0.5 * (1.0 + t)
        act = v * half
        slope_ref[i, g * width : (g + 1) * width, :] = half + 0.5 * v * (1.0 - t * t) * (
            root + (root * 3.0 * 0.044715) * square
        )
        for j in range(width // chans):
            act_ref[g * (width // chans) + j, i] = act[j * chans : (j + 1) * chans, :].astype(bf16)

    conv_body(*refs[:8], *refs[10:], emit)


def adjoint_kernel(*refs):
    cot_ref, grad_ref = refs[8:10]
    width = refs[7].shape[2]

    def emit(g, i, v):
        at = slice(g * width, (g + 1) * width)
        grad_ref[i, at, :] = (cot_ref[i, at, :].astype(f32) + v).astype(bf16)

    conv_body(*refs[:8], *refs[10:], emit)


def conv_call(kernel, name, where, x, halo, stencil, mix, extra, outs):
    rows, channels, cols = x.shape
    groups, _, width = mix.shape
    ins = (where, x, *halo, stencil, mix, *extra)
    rim = stencil.shape[1] // 10
    flat = (rows + 2 * rim) * channels
    return pl.pallas_call(
        kernel,
        out_shape=outs,
        in_specs=[pl.BlockSpec(memory_space=pltpu.SMEM)] + vmem(len(ins) - 1),
        out_specs=tuple(vmem(len(outs))),
        scratch_shapes=[
            pltpu.VMEM((flat, cols), f32),
            pltpu.VMEM((flat, cols), f32),
            pltpu.VMEM((rows, width * 16, cols), bf16),
            pltpu.VMEM((rows * 16, 128), bf16),
            pltpu.VMEM((groups, width, width * 16), bf16),
        ],
        compiler_params=params(),
        cost_estimate=cost(1.2e10, 4e6),
        name=name,
    )(*ins)


def shifted(axis, step):
    count = lax.axis_size(axis)
    return [(a, (a + step) % count) for a in range(count)]


def lat_rims(x, left, right, rim):
    rows, channels, cols = x.shape
    low = jnp.concatenate([x[-rim:].reshape(rim * channels, cols), left[-8:], right[-8:]], axis=0)
    high = jnp.concatenate([x[:rim].reshape(rim * channels, cols), left[:8], right[:8]], axis=0)
    low = lax.ppermute(low, "lat", shifted("lat", 1))
    high = lax.ppermute(high, "lat", shifted("lat", -1))
    return low, high, left, right


def slope_kernel(edge, act_ref, slope_ref, out_ref, left_ref, right_ref):
    blocks, rows, chans, cols = act_ref.shape
    channels = blocks * chans

    def one(i, carry):
        parts = [act_ref[b, i].astype(f32) for b in range(blocks)]
        out_ref[i] = (slope_ref[i] * jnp.concatenate(parts, axis=0)).astype(bf16)
        return carry

    lax.fori_loop(0, rows, one, 0)
    first, last = edge_blocks(out_ref[...].reshape(rows * channels, cols), edge)
    left_ref[...] = first.astype(bf16)
    right_ref[...] = last.astype(bf16)


def slope_step(cot_act, slope, edge):
    rows, channels, cols = slope.shape
    blocks = len(chunk_blocks(rows * channels // 128, edge))
    shape = jax.ShapeDtypeStruct((8 * blocks, cols), bf16)
    return pl.pallas_call(
        functools.partial(slope_kernel, edge),
        out_shape=(jax.ShapeDtypeStruct(slope.shape, bf16), shape, shape),
        in_specs=vmem(2),
        out_specs=tuple(vmem(3)),
        compiler_params=params(),
        cost_estimate=cost(1e8, 3e6),
        name="slope_step",
    )(cot_act, slope)


def stencil_rows(weights):
    rows, span, _, k_count = weights.shape
    w = jnp.transpose(weights, (0, 3, 2, 1)).reshape(rows, k_count, span * span)
    w = jnp.pad(w, ((0, 0), (0, 16 - k_count), (0, 0)))
    return w.reshape(rows * 16, span * span).astype(bf16)


def local(input_field, basis_values, support_reach, mix_weight, filter_weight, cotangent):
    _, rows, channels, cols = input_field.shape
    rim = basis_values.shape[1] // 2
    degrees = filter_weight.shape[0]
    groups, k_count, width, _ = mix_weight.shape
    lat_count = lax.axis_size("lat")
    lon_count = lax.axis_size("lon")
    nlat = rows * lat_count
    nlon = cols * lon_count
    lat_index = lax.axis_index("lat")
    lon_index = lax.axis_index("lon")
    m_count = degrees // lat_count
    chans = channels // lon_count
    row_start = lat_index * rows
    field = input_field[0]
    cot = cotangent[0]

    edge = rim * channels // 128
    body = rows * chans

    sent = start_step(lon_index, cot, field, lon_count, edge)
    circ_c = lax.all_to_all(sent, "lon", 0, 0, tiled=True)

    blocks = 8 * len(chunk_blocks(rows * channels // 128, edge))
    strips = circ_c[:, body : body + blocks]
    left = lax.dynamic_index_in_dim(strips, (lon_index + lon_count - 1) % lon_count, 0, False)
    right = lax.dynamic_index_in_dim(strips, (lon_index + 1) % lon_count, 0, False)
    halo = lat_rims(field, left, right, rim)
    offsets = jnp.abs(jnp.arange(2 * rim + 1, dtype=jnp.int32) - rim)
    pad = ((rim, rim), (0, 0), (0, 0), (0, 0))
    basis_ext = lax.dynamic_slice_in_dim(jnp.pad(basis_values, pad), row_start, rows + 2 * rim, 0)
    reach_ext = lax.dynamic_slice_in_dim(
        jnp.pad(support_reach, pad[:2]), row_start, rows + 2 * rim, 0
    )
    inside = offsets[None, None, :] <= reach_ext[:, :, None]
    weights_ext = jnp.where(inside[..., None], basis_ext, 0.0)
    stencil = stencil_rows(weights_ext[rim : rim + rows])
    span = 2 * rim + 1
    flipped = jnp.stack(
        [weights_ext[a : a + rows, span - 1 - a, ::-1, :] for a in range(span)], axis=1
    )
    stencil_adj = stencil_rows(flipped)
    mix = mix_weight.reshape(groups, k_count * width, width)
    mix_adj = jnp.transpose(mix_weight, (0, 1, 3, 2)).reshape(groups, k_count * width, width)
    where = jnp.stack([lat_index, jnp.int32(nlat)]).astype(jnp.int32)
    act, slope = conv_call(
        forward_kernel,
        "conv_forward",
        where,
        field,
        halo,
        stencil,
        mix,
        (),
        (
            jax.ShapeDtypeStruct((lon_count, rows, chans, cols), bf16),
            jax.ShapeDtypeStruct((rows, channels, cols), f32),
        ),
    )

    tab = lon_table(degrees, nlon, lat_count)
    table, flip = legendre_tables(lat_index, degrees, lat_count, rows, m_count)
    theta = math.pi * (np.arange(nlat) + 0.5) / nlat
    quad = 2.0 * math.pi * math.pi / nlat * np.sin(theta) / nlon
    quad_rows = np.repeat(quad.reshape(lat_count, rows), chans, axis=1).astype(np.float32)
    quad_lanes = lax.dynamic_slice_in_dim(jnp.asarray(quad_rows), lat_index, 1, 0)
    post = np.broadcast_to(quad.reshape(lat_count, rows).T.reshape(nlat, 1), (nlat, 128))
    gains = lax.dynamic_slice_in_dim(filter_weight, lon_index * chans, chans, 1)
    gains = jnp.pad(jnp.concatenate([gains] * 2, axis=1), ((0, 0), (0, 128 - 2 * chans)))

    post = jnp.asarray(post.astype(np.float32))
    shape = (lon_count, rows, chans, cols)
    send_1 = analysis(circ_c, body, tab, quad_lanes, lat_count, True)
    recv_1 = lax.all_to_all(send_1, "lat", 0, 0, tiled=True)
    recv_1, act = lax.optimization_barrier((recv_1, act))
    circ_f = lax.all_to_all(act, "lon", 0, 0, tiled=True)
    filtered_c = filter_step(lat_index, recv_1, table, flip, gains, post, chans, True)
    send_2 = analysis(circ_f, body, tab, quad_lanes, lat_count, False, (filtered_c,))
    recv_2 = lax.all_to_all(send_2, "lat", 0, 0, tiled=True)
    cot_act = lax.all_to_all(synthesis(recv_2, tab, 1, shape), "lon", 0, 0, tiled=True)
    filtered_f = filter_step(lat_index, recv_2, table, flip, gains, post, chans, False)
    cot_act, filtered_f = lax.optimization_barrier((cot_act, filtered_f))
    recv_3 = lax.all_to_all(filtered_f, "lat", 0, 0, tiled=True)
    branch = lax.all_to_all(synthesis(recv_3, tab, 0, shape), "lon", 0, 0, tiled=True)

    cot_conv, first_c, last_c = slope_step(cot_act, slope, edge)
    left_c = lax.ppermute(last_c, "lon", shifted("lon", 1))
    right_c = lax.ppermute(first_c, "lon", shifted("lon", -1))
    (grad_field,) = conv_call(
        adjoint_kernel,
        "conv_adjoint",
        where,
        cot_conv,
        lat_rims(cot_conv, left_c, right_c, rim),
        stencil_adj,
        mix_adj,
        (cot,),
        (jax.ShapeDtypeStruct((rows, channels, cols), bf16),),
    )
    branch = jnp.transpose(branch, (1, 0, 2, 3)).reshape(rows, channels, cols)
    block_out = (field.astype(f32) + branch.astype(f32)).astype(bf16)
    return block_out[None], grad_field[None]


def solution(mesh):
    placed = (P(None, "lat", None, "lon"), P(), P(), P(), P(), P(None, "lat", None, "lon"))
    return jax.shard_map(
        local,
        mesh=mesh,
        in_specs=placed,
        out_specs=(P(None, "lat", None, "lon"), P(None, "lat", None, "lon")),
        check_vma=False,
    )
```

time: 1150 us -> 190 us (0.17); the launches traced: 1130 us -> 188 us
  other arithmetic: 511 us -> 5.55 us
  loops' own time: 256 us -> 0 us
  local copies, waits for them, and re-layouts: 224 us -> 36 us
  Pallas kernels: 0 us -> 53 us
  matrix products: 36.3 us -> 0 us
  waiting for transfers between devices: 27.5 us -> 39.9 us
    another operation x1 -> x0, loops' own time: 256 us -> none  [legendre(): lax.scan(advance, (empty_state, empty_state, empty_state), degrees, unrol...]
    eq x384 -> x0, other arithmetic: 247 us -> none  [advance(): start_here = degree == orders[:, None]]
    another operation x13 -> x1, other arithmetic: 91.9 us -> 0.08 us  [local(): where = jnp.stack([lat_index, jnp.int32(nlat)]).astype(jnp.int32)]
    unnamed x1014 -> x100, local copies, waits for them, and re-layouts: 94.8 us -> 24.6 us
    unnamed x35 -> x0, other arithmetic: 62.6 us -> none
    pallas_call x0 -> x12, Pallas kernels: none -> 53 us  [the longest x2 21.3 us: conv_call(): pl.pallas_call(kernel, out_shape=outs, in_specs=[pl.BlockSpec(memory_spac...]
    while x372 -> x0, other arithmetic: 43 us -> none
    convert_element_type x9 -> x1, local copies, waits for them, and re-layouts: 39 us -> 0.1 us  [local(): block_out = (field.astype(f32) + branch.astype(f32)).astype(bf16)]
  transfers between devices with their start and end apart: 16 -> 13, of which waited for: 6 -> 5; matrix products, arithmetic and copies ran while one was open for 51% -> 9% of each run, Pallas kernels for 0% -> 26%
where the time goes in v1:
time: 190 us; the launch traced here: 188 us
  Pallas kernels  53 us (28%)
  starting transfers between devices  52.6 us (28%)
  waiting for transfers between devices  39.9 us (21%)
  local copies, waits for them, and re-layouts  36 us (19%)
  other arithmetic  5.55 us (3%)
    all_to_all x1, waiting for transfers between devices, local(): recv_2 = lax.all_to_all(send_2, 'lat', 0, 0, tiled=True)  24.7 us
    unnamed x100, local copies, waits for them, and re-layouts  24.6 us
    pallas_call x2, Pallas kernels, conv_call(): pl.pallas_call(kernel, out_shape=outs, in_specs=[pl.BlockSpec(memory_spac...  21.3 us
    pallas_call x2, Pallas kernels, filter_step(): pl.pallas_call(functools.partial(filter_kernel, m_count, chans, cotangent...  14.3 us
    ppermute x2, starting transfers between devices, lat_rims(): high = lax.ppermute(high, 'lat', shifted('lat', -1))  10.5 us
    pallas_call x1, Pallas kernels, legendre_tables(): pl.pallas_call(functools.partial(legendre_kernel, m_count), out_shape=(sh...  8.3 us
    all_to_all x1, starting transfers between devices, local(): recv_1 = lax.all_to_all(send_1, 'lat', 0, 0, tiled=True)  6.7 us
    all_to_all x1, starting transfers between devices, local(): circ_c = lax.all_to_all(sent, 'lon', 0, 0, tiled=True)  6.07 us
  transfers between devices with their start and end apart: 13, of which 5 were waited for; matrix products, arithmetic and copies ran while one was open for 9% of the time, Pallas kernels for 26%

profile of v1, /device:TPU:2, one launch (start us, length us, event | category | flops | bytes accessed | tf_op | source)
XLA Modules:
  0.0 188.2 jit_solution(15464831175663785763)
XLA Ops:
  4.1 6.1 %all-to-all-start = ((bf16[8,336,128]{2,1,0:T(8,128)(2,1)}), bf16[8,336,128]{2,1,0:T(8,128)(2,1)S(1)}, u32[]{:S(2)}, u32[]{:S(2)}) async-start(bf16[8,336,128]{2,1,0:T(8,128)(2,1)} %start.1), calls=%async_computation | async-start | bytes 1376256 | tf_op jit(solution)/shard_map/all_to_all | solution.py:625
  13.9 1.7 lon_table.1.refs_1_.tab_ref
  16.4 4.2 %all-to-all-done.refs_0_ = bf16[8,336,128]{2,1,0:T(8,128)(2,1)S(1)} async-done(((bf16[8,336,128]{2,1,0:T(8,128)(2,1)}), bf16[8,336,128]{2,1,0:T(8,128)(2,1)S(1)}, u32[]{:S(2)}, u32[]{:S(2)}) %all-to-all-start) | async-done | bytes 688160 | tf_op jit(solution)/shard_map/all_to_all | solution.py:625
  21.9 6.8 %collective-permute-start.1 = (bf16[400,128]{1,0:T(8,128)(2,1)S(1)}, bf16[400,128]{1,0:T(8,128)(2,1)S(1)}, u32[]{:S(2)}, u32[]{:S(2)}) collective-permute-start(bf16[400,128]{1,0:T(8,128)(2,1)S(1)} %pad_maximum_fusion.1), channel_id=1, source_target_pairs={{0,248},{8,0},{16,8},{24,16},{32,24},{40,32},{48,40},{56,48},{64,5... | collective-permute-start | bytes 307208 | tf_op jit(solution)/shard_map/ppermute | solution.py:563
  30.5 6.7 %all-to-all-start.1 = ((bf16[32,56,128]{2,1,0:T(8,128)(2,1)}), bf16[32,56,128]{2,1,0:T(8,128)(2,1)S(1)}, u32[]{:S(2)}, u32[]{:S(2)}) async-start(bf16[32,56,128]{2,1,0:T(8,128)(2,1)} %copy-done.9), calls=%async_computation.1 | async-start | bytes 917504 | tf_op jit(solution)/shard_map/all_to_all | solution.py:677
  39.0 10.1 %conv_forward.1 = (bf16[8,12,24,128]{3,2,1,0:T(8,128)(2,1)S(1)}, f32[12,192,128]{2,1,0:T(8,128)S(1)}) custom-call(s32[2]{0:T(128)S(1)} %pad_add_fusion.refs_0_, bf16[12,192,128]{2,1,0:T(8,128)(2,1)S(1)} %bitcast.39, bf16[400,128]{1,0:T(8,128)(2,1)S(1)} %collective-permute-done.refs_2_, bf16[400,128]{1,0:T(8,128)(2,1)S(1)} %collective-permute-done.1.refs_3_, ...), custom_call_target="tpu_custom_call" | custom-call | flops 12000000000 | bytes 4000000 | tf_op jit(solution)/shard_map/conv_forward/pallas_call | solution.py:535
  51.0 4.9 %all-to-all-done.1.recv_ref = bf16[32,56,128]{2,1,0:T(8,128)(2,1)S(1)} async-done(((bf16[32,56,128]{2,1,0:T(8,128)(2,1)}), bf16[32,56,128]{2,1,0:T(8,128)(2,1)S(1)}, u32[]{:S(2)}, u32[]{:S(2)}) %all-to-all-start.1) | async-done | bytes 458784 | tf_op jit(solution)/shard_map/all_to_all | solution.py:677
  55.9 4.7 %all-to-all-start.2 = ((bf16[8,12,24,128]{3,2,1,0:T(8,128)(2,1)}), bf16[8,12,24,128]{3,2,1,0:T(8,128)(2,1)S(1)}, u32[]{:S(2)}, u32[]{:S(2)}) async-start(bf16[8,12,24,128]{3,2,1,0:T(8,128)(2,1)} %copy-done.18), calls=%async_computation.2 | async-start | bytes 1179648 | tf_op jit(solution)/shard_map/all_to_all | solution.py:679
  64.6 8.3 %legendre_tables.1 = (bf16[12,384,384]{2,1,0:T(8,128)(2,1)S(1)}, bf16[12,384,384]{2,1,0:T(8,128)(2,1)S(1)}) custom-call(s32[1]{0:T(128)} %bitcast.3.idx_ref, f32[384]{0:T(512)S(1)} %copy-done.34, f32[384]{0:T(512)S(1)} %copy-done.35, f32[16,1]{1,0:T(8,128)S(1)} %copy.31.norm_ref, f32[1,384]{1,0:T(1,128)S(1)} %copy-done.36, f32[1,384]{1,0:T(1,128)S(1)} %copy-done.37), custom_call_target="tpu_custom_call" | custom-call | flops 2000000000 | bytes 7000000 | tf_op jit(solution)/shard_map/legendre_tables/pallas_call | solution.py:118
  72.9 6.7 %filter_step.2.refs_3_ = bf16[32,56,128]{2,1,0:T(8,128)(2,1)S(1)} custom-call(s32[1]{0:T(128)} %bitcast.3.idx_ref, bf16[32,56,128]{2,1,0:T(8,128)(2,1)S(1)} %all-to-all-done.1.recv_ref, bf16[12,384,384]{2,1,0:T(8,128)(2,1)S(1)} %get-tuple-element.16.table_ref, bf16[12,384,384]{2,1,0:T(8,128)(2,1)S(1)} %get-tuple-element.17.flip_ref, ...), custom_call_target="tpu_custom_call" | custom-call | flops 905969664 | bytes 9000000 | tf_op jit(solution)/shard_map/filter_step/pallas_call | solution.py:297
  79.7 1.8 copy-done.1
  81.5 1.8 copy-done.3
  87.0 4.8 %all-to-all-start.3 = ((bf16[32,112,128]{2,1,0:T(8,128)(2,1)}), bf16[32,112,128]{2,1,0:T(8,128)(2,1)S(1)}, u32[]{:S(2)}, u32[]{:S(2)}) async-start(bf16[32,112,128]{2,1,0:T(8,128)(2,1)} %copy-done.5), calls=%async_computation.3 | async-start | bytes 1835008 | tf_op jit(solution)/shard_map/all_to_all | solution.py:682
  94.5 24.7 %all-to-all-done.3.recv_ref = bf16[32,112,128]{2,1,0:T(8,128)(2,1)S(1)} async-done(((bf16[32,112,128]{2,1,0:T(8,128)(2,1)}), bf16[32,112,128]{2,1,0:T(8,128)(2,1)S(1)}, u32[]{:S(2)}, u32[]{:S(2)}) %all-to-all-start.3) | async-done | bytes 917536 | tf_op jit(solution)/shard_map/all_to_all | solution.py:682
  120.9 5.8 %all-to-all-start.4 = ((bf16[8,12,24,128]{3,2,1,0:T(8,128)(2,1)}), bf16[8,12,24,128]{3,2,1,0:T(8,128)(2,1)}, u32[]{:S(2)}, u32[]{:S(2)}) async-start(bf16[8,12,24,128]{3,2,1,0:T(8,128)(2,1)} %copy-done.8), calls=%async_computation.4 | async-start | bytes 1179648 | tf_op jit(solution)/shard_map/all_to_all | solution.py:683
  127.5 2.0 %copy-done.2 = bf16[12,384,384]{2,1,0:T(8,128)(2,1)S(1)} copy-done((bf16[12,384,384]{2,1,0:T(8,128)(2,1)S(1)}, bf16[12,384,384]{2,1,0:T(8,128)(2,1)}, u32[]{:S(2)}) %copy-start.2) | copy-done | bytes 3538968
  129.5 2.0 %copy-done.4 = bf16[12,384,384]{2,1,0:T(8,128)(2,1)S(1)} copy-done((bf16[12,384,384]{2,1,0:T(8,128)(2,1)S(1)}, bf16[12,384,384]{2,1,0:T(8,128)(2,1)}, u32[]{:S(2)}) %copy-start.4) | copy-done | bytes 3538968
  133.3 7.5 %filter_step.3 = bf16[32,56,128]{2,1,0:T(8,128)(2,1)} custom-call(s32[1]{0:T(128)} %bitcast.3.idx_ref, bf16[32,112,128]{2,1,0:T(8,128)(2,1)S(1)} %all-to-all-done.3.recv_ref, bf16[12,384,384]{2,1,0:T(8,128)(2,1)S(1)} %copy-done.2, bf16[12,384,384]{2,1,0:T(8,128)(2,1)S(1)} %copy-done.4, f32[384,128]{1,0:T(8,128)S(1)} %copy-done.13, f32[384,128]{1,0:T(8,128)S(1)} %copy-done.17), custom_call_target="tpu_custom_call" | custom-call | flops 905969664 | bytes 9000000 | tf_op jit(solution)/shard_map/filter_step/pallas_call | solution.py:297
  146.0 3.9 %all-to-all-start.5 = ((bf16[32,56,128]{2,1,0:T(8,128)(2,1)}), bf16[32,56,128]{2,1,0:T(8,128)(2,1)S(1)}, u32[]{:S(2)}, u32[]{:S(2)}) async-start(bf16[32,56,128]{2,1,0:T(8,128)(2,1)} %filter_step.3), calls=%async_computation.5 | async-start | bytes 917504 | tf_op jit(solution)/shard_map/all_to_all | solution.py:686
  150.9 3.1 %collective-permute-start.3 = (bf16[40,128]{1,0:T(8,128)(2,1)S(1)}, bf16[40,128]{1,0:T(8,128)(2,1)S(1)}, u32[]{:S(2)}, u32[]{:S(2)}) collective-permute-start(bf16[40,128]{1,0:T(8,128)(2,1)S(1)} %get-tuple-element.23), channel_id=1, source_target_pairs={{0,7},{1,0},{2,1},{3,2},{4,3},{5,4},{6,5},{7,6},{8,15},{9,8},{10,9... | collective-permute-start | bytes 30728 | tf_op jit(solution)/shard_map/ppermute | solution.py:691
  156.7 3.8 %collective-permute-start.5 = (bf16[400,128]{1,0:T(8,128)(2,1)}, bf16[400,128]{1,0:T(8,128)(2,1)}, u32[]{:S(2)}, u32[]{:S(2)}) collective-permute-start(bf16[400,128]{1,0:T(8,128)(2,1)} %pad_maximum_fusion.3), channel_id=1, source_target_pairs={{0,248},{8,0},{16,8},{24,16},{32,24},{40,32},{48,40},{56,48},{64,5... | collective-permute-start | bytes 307208 | tf_op jit(solution)/shard_map/ppermute | solution.py:563
  163.9 4.7 %all-to-all-done.5.recv_ref = bf16[32,56,128]{2,1,0:T(8,128)(2,1)S(1)} async-done(((bf16[32,56,128]{2,1,0:T(8,128)(2,1)}), bf16[32,56,128]{2,1,0:T(8,128)(2,1)S(1)}, u32[]{:S(2)}, u32[]{:S(2)}) %all-to-all-start.5) | async-done | bytes 458784 | tf_op jit(solution)/shard_map/all_to_all | solution.py:686
  170.3 5.5 %all-to-all-start.6 = ((bf16[8,12,24,128]{3,2,1,0:T(8,128)(2,1)}), bf16[8,12,24,128]{3,2,1,0:T(8,128)(2,1)S(1)}, u32[]{:S(2)}, u32[]{:S(2)}) async-start(bf16[8,12,24,128]{3,2,1,0:T(8,128)(2,1)} %synthesis.3), calls=%async_computation.6 | async-start | bytes 1179648 | tf_op jit(solution)/shard_map/all_to_all | solution.py:687
  175.9 11.1 %conv_adjoint.1 = bf16[12,192,128]{2,1,0:T(8,128)(2,1)} custom-call(s32[2]{0:T(128)S(1)} %copy-done.33, bf16[12,192,128]{2,1,0:T(8,128)(2,1)S(1)} %copy-done.26, bf16[400,128]{1,0:T(8,128)(2,1)} %collective-permute-done.4.refs_2_, bf16[400,128]{1,0:T(8,128)(2,1)} %collective-permute-done.5.refs_3_, bf16[40,128]{1,0:T(8,128)(2,1)S(1)} %copy-done.29, ...), custom_call_target="tpu_custom_call" | custom-call | flops 12000000000 | bytes 4000000 | tf_op jit(solution)/shard_map/conv_adjoint/pallas_call | solution.py:535
  (156 shorter events, 44.4 us)
Async XLA Ops:
  0.6 60.7 %copy-start = (f32[384,192]{0,1:T(8,128)S(1)}, f32[384,192]{0,1:T(8,128)}, u32[]{:S(2)}) copy-start(f32[384,192]{0,1:T(8,128)} %param.20) | copy-start | bytes 884740
  4.1 16.5 %all-to-all-start = ((bf16[8,336,128]{2,1,0:T(8,128)(2,1)}), bf16[8,336,128]{2,1,0:T(8,128)(2,1)S(1)}, u32[]{:S(2)}, u32[]{:S(2)}) async-start(bf16[8,336,128]{2,1,0:T(8,128)(2,1)} %start.1), calls=%async_computation | async-start | bytes 1376256 | tf_op jit(solution)/shard_map/all_to_all | solution.py:625
  15.6 22.3 %copy-start.32 = (s32[2]{0:T(128)}, s32[2]{0:T(128)S(1)}, u32[]{:S(2)}) copy-start(s32[2]{0:T(128)S(1)} %pad_add_fusion.refs_0_) | copy-start | bytes 28
  21.9 16.0 %collective-permute-start = (bf16[400,128]{1,0:T(8,128)(2,1)}, bf16[400,128]{1,0:T(8,128)(2,1)S(1)}, u32[]{:S(2)}, u32[]{:S(2)}) collective-permute-start(bf16[400,128]{1,0:T(8,128)(2,1)} %pad_maximum_fusion), channel_id=1, source_target_pairs={{0,8},{8,16},{16,24},{24,32},{32,40},{40,48},{48,56},{56,64},{64,7... | collective-permute-start | bytes 307208 | tf_op jit(solution)/shard_map/ppermute | solution.py:562
  21.9 16.0 %copy-start.27 = (bf16[12,16,25]{2,1,0:T(8,128)(2,1)S(1)}, bf16[12,16,25]{2,1,0:T(8,128)(2,1)}, u32[]{:S(2)}) copy-start(bf16[12,16,25]{2,1,0:T(8,128)(2,1)} %pad.23.clone) | copy-start | bytes 28804
  21.9 16.0 %collective-permute-start.1 = (bf16[400,128]{1,0:T(8,128)(2,1)S(1)}, bf16[400,128]{1,0:T(8,128)(2,1)S(1)}, u32[]{:S(2)}, u32[]{:S(2)}) collective-permute-start(bf16[400,128]{1,0:T(8,128)(2,1)S(1)} %pad_maximum_fusion.1), channel_id=1, source_target_pairs={{0,248},{8,0},{16,8},{24,16},{32,24},{40,32},{48,40},{56,48},{64,5... | collective-permute-start | bytes 307208 | tf_op jit(solution)/shard_map/ppermute | solution.py:563
  30.5 25.4 %all-to-all-start.1 = ((bf16[32,56,128]{2,1,0:T(8,128)(2,1)}), bf16[32,56,128]{2,1,0:T(8,128)(2,1)S(1)}, u32[]{:S(2)}, u32[]{:S(2)}) async-start(bf16[32,56,128]{2,1,0:T(8,128)(2,1)} %copy-done.9), calls=%async_computation.1 | async-start | bytes 917504 | tf_op jit(solution)/shard_map/all_to_all | solution.py:677
  51.0 13.6 %copy-start.34 = (f32[384]{0:T(512)S(1)}, f32[384]{0:T(512)}, u32[]{:S(2)}) copy-start(f32[384]{0:T(512)} %constant.101.clone.rise_ref) | copy-start | bytes 4612
  51.0 13.6 %copy-start.35 = (f32[384]{0:T(512)S(1)}, f32[384]{0:T(512)}, u32[]{:S(2)}) copy-start(f32[384]{0:T(512)} %constant.102.clone.fall_ref) | copy-start | bytes 4612
  51.0 13.6 %copy-start.36 = (f32[1,384]{1,0:T(1,128)S(1)}, f32[1,384]{1,0:T(1,128)}, u32[]{:S(2)}) copy-start(f32[1,384]{1,0:T(1,128)} %constant.103.clone.cos_ref) | copy-start | bytes 4612
  51.0 13.6 %copy-start.37 = (f32[1,384]{1,0:T(1,128)S(1)}, f32[1,384]{1,0:T(1,128)}, u32[]{:S(2)}) copy-start(f32[1,384]{1,0:T(1,128)} %constant.104.clone.logsin_ref) | copy-start | bytes 4612
  55.9 28.1 %all-to-all-start.2 = ((bf16[8,12,24,128]{3,2,1,0:T(8,128)(2,1)}), bf16[8,12,24,128]{3,2,1,0:T(8,128)(2,1)S(1)}, u32[]{:S(2)}, u32[]{:S(2)}) async-start(bf16[8,12,24,128]{3,2,1,0:T(8,128)(2,1)} %copy-done.18), calls=%async_computation.2 | async-start | bytes 1179648 | tf_op jit(solution)/shard_map/all_to_all | solution.py:679
  64.6 8.3 %copy-start.12 = (f32[384,128]{1,0:T(8,128)}, f32[384,128]{1,0:T(8,128)S(1)}, u32[]{:S(2)}) copy-start(f32[384,128]{1,0:T(8,128)S(1)} %pad.24.gain_ref) | copy-start | bytes 589828
  64.6 8.3 %copy-start.16 = (f32[384,128]{1,0:T(8,128)S(1)}, f32[384,128]{1,0:T(8,128)}, u32[]{:S(2)}) copy-start(f32[384,128]{1,0:T(8,128)} %constant.106.clone.post_ref) | copy-start | bytes 589828
  87.0 32.2 %all-to-all-start.3 = ((bf16[32,112,128]{2,1,0:T(8,128)(2,1)}), bf16[32,112,128]{2,1,0:T(8,128)(2,1)S(1)}, u32[]{:S(2)}, u32[]{:S(2)}) async-start(bf16[32,112,128]{2,1,0:T(8,128)(2,1)} %copy-done.5), calls=%async_computation.3 | async-start | bytes 1835008 | tf_op jit(solution)/shard_map/all_to_all | solution.py:682
  120.9 20.0 %all-to-all-start.4 = ((bf16[8,12,24,128]{3,2,1,0:T(8,128)(2,1)}), bf16[8,12,24,128]{3,2,1,0:T(8,128)(2,1)}, u32[]{:S(2)}, u32[]{:S(2)}) async-start(bf16[8,12,24,128]{3,2,1,0:T(8,128)(2,1)} %copy-done.8), calls=%async_computation.4 | async-start | bytes 1179648 | tf_op jit(solution)/shard_map/all_to_all | solution.py:683
  144.6 18.4 %copy-start.22 = (bf16[4,9,48,48]{3,2,1,0:T(8,128)(2,1)S(1)}, bf16[4,9,48,48]{3,2,1,0:T(8,128)(2,1)}, u32[]{:S(2)}) copy-start(bf16[4,9,48,48]{3,2,1,0:T(8,128)(2,1)} %param.19) | copy-start | bytes 497668
  144.6 9.5 %collective-permute-start.2 = (bf16[40,128]{1,0:T(8,128)(2,1)S(1)}, bf16[40,128]{1,0:T(8,128)(2,1)S(1)}, u32[]{:S(2)}, u32[]{:S(2)}) collective-permute-start(bf16[40,128]{1,0:T(8,128)(2,1)S(1)} %get-tuple-element.22), channel_id=1, source_target_pairs={{0,1},{1,2},{2,3},{3,4},{4,5},{5,6},{6,7},{7,0},{8,9},{9,10},{10,1... | collective-permute-start | bytes 30728 | tf_op jit(solution)/shard_map/ppermute | solution.py:690
  146.0 22.6 %all-to-all-start.5 = ((bf16[32,56,128]{2,1,0:T(8,128)(2,1)}), bf16[32,56,128]{2,1,0:T(8,128)(2,1)S(1)}, u32[]{:S(2)}, u32[]{:S(2)}) async-start(bf16[32,56,128]{2,1,0:T(8,128)(2,1)} %filter_step.3), calls=%async_computation.5 | async-start | bytes 917504 | tf_op jit(solution)/shard_map/all_to_all | solution.py:686
  150.9 4.5 %collective-permute-start.3 = (bf16[40,128]{1,0:T(8,128)(2,1)S(1)}, bf16[40,128]{1,0:T(8,128)(2,1)S(1)}, u32[]{:S(2)}, u32[]{:S(2)}) collective-permute-start(bf16[40,128]{1,0:T(8,128)(2,1)S(1)} %get-tuple-element.23), channel_id=1, source_target_pairs={{0,7},{1,0},{2,1},{3,2},{4,3},{5,4},{6,5},{7,6},{8,15},{9,8},{10,9... | collective-permute-start | bytes 30728 | tf_op jit(solution)/shard_map/ppermute | solution.py:691
  154.0 9.9 %copy-start.28 = (bf16[40,128]{1,0:T(8,128)(2,1)}, bf16[40,128]{1,0:T(8,128)(2,1)S(1)}, u32[]{:S(2)}) copy-start(bf16[40,128]{1,0:T(8,128)(2,1)S(1)} %collective-permute-done.2.refs_4_) | copy-start | bytes 30724
  156.7 19.2 %collective-permute-start.5 = (bf16[400,128]{1,0:T(8,128)(2,1)}, bf16[400,128]{1,0:T(8,128)(2,1)}, u32[]{:S(2)}, u32[]{:S(2)}) collective-permute-start(bf16[400,128]{1,0:T(8,128)(2,1)} %pad_maximum_fusion.3), channel_id=1, source_target_pairs={{0,248},{8,0},{16,8},{24,16},{32,24},{40,32},{48,40},{56,48},{64,5... | collective-permute-start | bytes 307208 | tf_op jit(solution)/shard_map/ppermute | solution.py:563
  161.1 14.7 %collective-permute-start.4 = (bf16[400,128]{1,0:T(8,128)(2,1)}, bf16[400,128]{1,0:T(8,128)(2,1)}, u32[]{:S(2)}, u32[]{:S(2)}) collective-permute-start(bf16[400,128]{1,0:T(8,128)(2,1)} %pad_maximum_fusion.2), channel_id=1, source_target_pairs={{0,8},{8,16},{16,24},{24,32},{32,40},{40,48},{48,56},{56,64},{64,7... | collective-permute-start | bytes 307208 | tf_op jit(solution)/shard_map/ppermute | solution.py:562
  170.3 16.8 %all-to-all-start.6 = ((bf16[8,12,24,128]{3,2,1,0:T(8,128)(2,1)}), bf16[8,12,24,128]{3,2,1,0:T(8,128)(2,1)S(1)}, u32[]{:S(2)}, u32[]{:S(2)}) async-start(bf16[8,12,24,128]{3,2,1,0:T(8,128)(2,1)} %synthesis.3), calls=%async_computation.6 | async-start | bytes 1179648 | tf_op jit(solution)/shard_map/all_to_all | solution.py:687
  (36 other events, 103.8 us)

commit v2 on v1

--- a/solution.py
+++ b/solution.py
@@ -33,12 +33,17 @@
     return [pl.BlockSpec(memory_space=pltpu.VMEM)] * count
 
 
+def hbm(count):
+    return [pl.BlockSpec(memory_space=pl.ANY)] * count
+
+
 def cost(flops, nbytes):
     return pl.CostEstimate(flops=int(flops), bytes_accessed=int(nbytes), transcendentals=0)
 
 
-def legendre_kernel(
-    m_count, idx_ref, rise_ref, fall_ref, norm_ref, cos_ref, logsin_ref, table_ref, flip_ref, keep
+def legendre_fill(
+    m_count, idx_ref, rise_ref, fall_ref, norm_ref, cos_ref, logsin_ref, keep, table_ref, flip_ref,
+    table_out, flip_out, sems
 ):
     m_pad, lat = norm_ref.shape[0], cos_ref.shape[1]
     degrees = table_ref.shape[1]
@@ -92,13 +97,15 @@
     lax.fori_loop(0, degrees // 16, block, (zeros, zeros, zeros, zero))
 
     def turn(m, carry):
+        pltpu.make_async_copy(table_ref.at[m], table_out.at[m], sems.at[0, m]).start()
         flip_ref[m] = jnp.transpose(table_ref[m])
+        pltpu.make_async_copy(flip_ref.at[m], flip_out.at[m], sems.at[1, m]).start()
         return carry
 
     lax.fori_loop(0, m_count, turn, 0)
 
 
-def legendre_tables(lat_index, degrees, lat_count, row_count, m_count):
+def legendre_inputs(lat_index, degrees, lat_count, row_count, m_count):
     nlat = lat_count * row_count
     m_pad = 16
     place = np.arange(nlat)
@@ -113,19 +120,7 @@
     norm_mine = lax.dynamic_index_in_dim(jnp.asarray(norms), lat_index, 0, keepdims=False)
     rise = np.sqrt(np.maximum(4.0 * m * m - 1.0, 1.0)).astype(np.float32)
     fall = (1.0 / np.sqrt(np.maximum(4.0 * m * m - 1.0, 1.0))).astype(np.float32)
-    shape = jax.ShapeDtypeStruct((m_count, degrees, nlat), bf16)
-    flip = jax.ShapeDtypeStruct((m_count, nlat, degrees), bf16)
-    return pl.pallas_call(
-        functools.partial(legendre_kernel, m_count),
-        out_shape=(shape, flip),
-        in_specs=[pl.BlockSpec(memory_space=pltpu.SMEM)] * 3 + vmem(3),
-        out_specs=tuple(vmem(2)),
-        scratch_shapes=[pltpu.VMEM((nlat // 128, 16 * m_pad, 128), f32)],
-        compiler_params=params(),
-        cost_estimate=cost(2e9, 7e6),
-        name="legendre_tables",
-    )(
-        lat_index[None],
+    return (
         jnp.asarray(rise),
         jnp.asarray(fall),
         norm_mine,
@@ -213,9 +208,9 @@
     )(circ, tab, quad_lanes, *beside)
 
 
-def filter_kernel(
-    m_count, chans, cotangent_pass, idx_ref, recv_ref, table_ref, flip_ref, gain_ref, post_ref,
-    out_ref, took, give
+def filter_body(
+    m_count, chans, cotangent_pass, idx_ref, recv_ref, weight_ref, post_ref, out_ref,
+    took, give, gain, table_ref, flip_ref, ready
 ):
     places, height, _ = out_ref.shape
     k_count = 2 * m_count
@@ -231,8 +226,15 @@
 
     lax.fori_loop(0, places, load, 0, unroll=4)
     give[2 * k_count * places :, :] = jnp.zeros((third * places, 128), f32)
-
-    def one(mm, carry):
+    weight = weight_ref[...]
+    room = 256 - weight.shape[1]
+    weight = jnp.concatenate([weight, jnp.zeros((weight.shape[0], room), f32)], axis=1)
+    weight = pltpu.roll(weight, lax.rem(256 - idx_ref[1] * chans, 256), 1)[:, 0:128]
+    place = lax.broadcasted_iota(jnp.int32, weight.shape, 1)
+    weight = jnp.where(place < chans, weight, 0.0)
+    gain[...] = weight + pltpu.roll(weight, chans, 1)
+
+    def one(mm):
         blocks = []
         for r in range(2):
             k = r * m_count + mm
@@ -257,7 +259,7 @@
             columns.append(total)
         x = jnp.concatenate(columns, axis=0).astype(bf16)
         coeffs = dot(table_ref[mm], x)
-        filtered = (coeffs * gain_ref[...]).astype(bf16)
+        filtered = (coeffs * gain[...]).astype(bf16)
         y = dot(flip_ref[mm], filtered)
         if cotangent_pass:
             y = y * post_ref[...]
@@ -279,9 +281,15 @@
             give[pl.ds((k_count + k) * places, places), :] = outs[1]
             at = pl.ds((2 * k_count + k % third) * places, places)
             give[at, :] = give[at, :] + pltpu.roll(outs[2], 32 * (k // third), 1)
+
+    def group(number, carry):
+        for m in range(3):
+            ready(number * 3 + m)
+        for m in range(3):
+            one(number * 3 + m)
         return carry
 
-    lax.fori_loop(0, m_count, one, 0, unroll=2)
+    lax.fori_loop(0, m_count // 3, group, 0)
 
     def store(d, carry):
         out_ref[d] = give[pl.ds(d, height, stride=places), :].astype(bf16)
@@ -290,23 +298,97 @@
     lax.fori_loop(0, places, store, 0, unroll=4)
 
 
-def filter_step(lat_index, recv, table, flip, gains, post, chans, cotangent_pass):
+def legendre_kernel(
+    m_count, idx_ref, rise_ref, fall_ref, norm_ref, cos_ref, logsin_ref, table_out, flip_out,
+    keep, table, flip, sems
+):
+    legendre_fill(
+        m_count, idx_ref, rise_ref, fall_ref, norm_ref, cos_ref, logsin_ref, keep, table, flip,
+        table_out, flip_out, sems,
+    )
+
+    def finish(m, carry):
+        pltpu.make_async_copy(table.at[m], table_out.at[m], sems.at[0, m]).wait()
+        pltpu.make_async_copy(flip.at[m], flip_out.at[m], sems.at[1, m]).wait()
+        return carry
+
+    lax.fori_loop(0, m_count, finish, 0)
+
+
+def legendre_tables(where, legendre, m_count, degrees, nlat):
+    smem = pl.BlockSpec(memory_space=pltpu.SMEM)
+    return pl.pallas_call(
+        functools.partial(legendre_kernel, m_count),
+        out_shape=(
+            jax.ShapeDtypeStruct((m_count, degrees, nlat), bf16),
+            jax.ShapeDtypeStruct((m_count, nlat, degrees), bf16),
+        ),
+        in_specs=[smem] * 3 + vmem(3),
+        out_specs=tuple(hbm(2)),
+        scratch_shapes=[
+            pltpu.VMEM((nlat // 128, 16 * 16, 128), f32),
+            *table_scratch(m_count, degrees, nlat),
+        ],
+        compiler_params=params(60),
+        cost_estimate=cost(2e9, 7e6),
+        name="legendre_tables",
+    )(where, *legendre)
+
+
+def filter_kernel(
+    m_count, chans, cotangent_pass, idx_ref, recv_ref, weight_ref, post_ref, table_in, flip_in,
+    out_ref, took, give, gain, table, flip, sems
+):
+    def begin(m, carry):
+        pltpu.make_async_copy(table_in.at[m], table.at[m], sems.at[0, m]).start()
+        pltpu.make_async_copy(flip_in.at[m], flip.at[m], sems.at[1, m]).start()
+        return carry
+
+    lax.fori_loop(0, m_count, begin, 0)
+
+    def ready(m):
+        pltpu.make_async_copy(table_in.at[m], table.at[m], sems.at[0, m]).wait()
+        pltpu.make_async_copy(flip_in.at[m], flip.at[m], sems.at[1, m]).wait()
+
+    filter_body(
+        m_count, chans, cotangent_pass, idx_ref, recv_ref, weight_ref, post_ref, out_ref,
+        took, give, gain, table, flip, ready,
+    )
+
+
+def filter_scratch(places, height, degrees):
+    return [
+        pltpu.VMEM((places * height, 128), f32),
+        pltpu.VMEM((places * height, 128), f32),
+        pltpu.VMEM((degrees, 128), f32),
+    ]
+
+
+def table_scratch(m_count, degrees, nlat):
+    return [
+        pltpu.VMEM((m_count, degrees, nlat), bf16),
+        pltpu.VMEM((m_count, nlat, degrees), bf16),
+        pltpu.SemaphoreType.DMA((2, m_count)),
+    ]
+
+
+def filter_step(where, recv, weight, post, table, flip, chans, cotangent_pass):
     places = recv.shape[0]
     m_count, degrees, nlat = table.shape
     height = 4 * m_count + 2 * m_count // 3
     return pl.pallas_call(
         functools.partial(filter_kernel, m_count, chans, cotangent_pass),
         out_shape=jax.ShapeDtypeStruct((places, height, 128), bf16),
-        in_specs=[pl.BlockSpec(memory_space=pltpu.SMEM)] + vmem(5),
+        in_specs=[pl.BlockSpec(memory_space=pltpu.SMEM)] + vmem(3) + hbm(2),
         out_specs=vmem(1)[0],
         scratch_shapes=[
-            pltpu.VMEM((places * height, 128), f32),
-            pltpu.VMEM((places * height, 128), f32),
+            *filter_scratch(places, height, degrees),
+            *table_scratch(m_count, degrees, nlat),
         ],
-        compiler_params=params(),
-        cost_estimate=cost(4 * m_count * degrees * nlat * 128, 9e6),
+        compiler_params=params(60),
+        cost_estimate=cost(8e9, 9e6),
         name="filter_step",
-    )(lat_index[None], recv, table, flip, gains, post)
+    )(where, recv, weight, post, table, flip)
 
 
 def synthesis_kernel(which, recv_ref, tab_ref, out_ref):
@@ -400,12 +482,61 @@
     )(lon_index[None], cot, field)
 
 
+def weights_kernel(rim, adjoint, idx_ref, stencil_ref, mix_ref, band, blend):
+    groups, width = mix_ref.shape[0], mix_ref.shape[2]
+    taps = mix_ref.shape[1] // width
+    k_pad = 16
+    ext = stencil_ref.shape[0] // k_pad
+    rows = ext - 2 * rim
+    span = 2 * rim + 1
+
+    tap = lax.broadcasted_iota(jnp.int32, (span * span, 128), 0)
+    slot = lax.broadcasted_iota(jnp.int32, (span * span, 128), 1)
+    source = idx_ref[0] * rows - rim + slot % ext
+    inside = (source >= 0) & (source < idx_ref[1]) & (slot < span * ext)
+    for i in range(rows):
+        total = jnp.zeros((k_pad, 128), f32)
+        for line in range(i, i + span) if adjoint else (i + rim,):
+            if adjoint:
+                hit = (span - 1 - tap // span == slot // ext) & (slot % ext == line)
+                hit = hit & (tap % span == i - line + span - 1)
+            else:
+                hit = (tap // span == slot // ext) & (slot % ext == i + tap % span)
+            place = jnp.where(inside & hit, 1.0, 0.0).astype(bf16)
+            total = total + dot(stencil_ref[line * k_pad : (line + 1) * k_pad, :], place)
+        band[i * k_pad : (i + 1) * k_pad, :] = total.astype(bf16)
+
+    depth = width * k_pad
+    pair_row = lax.broadcasted_iota(jnp.int32, (taps * width, depth), 0)
+    pair_lane = lax.broadcasted_iota(jnp.int32, (taps * width, depth), 1)
+    place = jnp.where(
+        pair_lane == (pair_row % width) * k_pad + pair_row // width, 1.0, 0.0
+    ).astype(bf16)
+    for g in range(groups):
+        blend[g] = dot(mix_ref[g], place, TN).astype(bf16)
+
+
+def conv_weights(where, stencil, mix, rim, adjoint):
+    groups, _, width = mix.shape
+    return pl.pallas_call(
+        functools.partial(weights_kernel, rim, adjoint),
+        out_shape=(
+            jax.ShapeDtypeStruct((stencil.shape[0] - 32 * rim, 128), bf16),
+            jax.ShapeDtypeStruct((groups, width, width * 16), bf16),
+        ),
+        in_specs=[pl.BlockSpec(memory_space=pltpu.SMEM)] + vmem(2),
+        out_specs=tuple(vmem(2)),
+        compiler_params=params(),
+        cost_estimate=cost(4e8, 1e6),
+        name="conv_weights",
+    )(where, stencil, mix)
+
+
 def conv_body(
-    idx_ref, x_ref, low_ref, high_ref, left_ref, right_ref, stencil_ref, mix_ref,
-    xs, hs, resp, band, blend, emit
+    x_ref, low_ref, high_ref, left_ref, right_ref, band_ref, blend_ref, xs, hs, resp, emit
 ):
     rows, channels, cols = x_ref.shape
-    groups, taps, width = mix_ref.shape[0], mix_ref.shape[1] // mix_ref.shape[2], mix_ref.shape[2]
+    groups, width, _ = blend_ref.shape
     ext = hs.shape[0] // channels
     rim = (ext - rows) // 2
     span = 2 * rim + 1
@@ -439,27 +570,7 @@
         at = slice(8 * u, 8 * u + 8)
         spread(left_ref[at], right_ref[at], chunks, edge)
 
-    tap = lax.broadcasted_iota(jnp.int32, (stencil_ref.shape[1], 128), 0)
-    slot = lax.broadcasted_iota(jnp.int32, (stencil_ref.shape[1], 128), 1)
-    source = idx_ref[0] * rows - rim + slot % ext
-    inside = (source >= 0) & (source < idx_ref[1]) & (slot < span * ext)
-    for i in range(rows):
-        hit = inside & (tap // span == slot // ext) & (slot % ext == i + tap % span)
-        place = jnp.where(hit, 1.0, 0.0).astype(bf16)
-        band[i * k_pad : (i + 1) * k_pad, :] = dot(
-            stencil_ref[i * k_pad : (i + 1) * k_pad, :], place
-        ).astype(bf16)
-
-    depth = width * k_pad
-    pair_row = lax.broadcasted_iota(jnp.int32, (taps * width, depth), 0)
-    pair_lane = lax.broadcasted_iota(jnp.int32, (taps * width, depth), 1)
-    place = jnp.where(
-        pair_lane == (pair_row % width) * k_pad + pair_row // width, 1.0, 0.0
-    ).astype(bf16)
-    for g in range(groups):
-        blend[g] = dot(mix_ref[g], place, TN).astype(bf16)
-
-    stencil = band[:, 0 : span * ext]
+    stencil = band_ref[:, 0 : span * ext]
 
     def column(c):
         x = xs[pl.ds(c, ext, stride=channels), :]
@@ -490,14 +601,16 @@
         lax.fori_loop(0, width // 2, pair, 0, unroll=8)
         for i in range(0, rows, 2):
             operand = jnp.concatenate([resp[i], resp[i + 1]], axis=1)
-            out = dot(blend[g], operand)
+            out = dot(blend_ref[g], operand)
             emit(g, i, out[:, 0:cols])
             emit(g, i + 1, out[:, cols:])
 
 
-def forward_kernel(*refs):
-    act_ref, slope_ref = refs[8:10]
-    width = refs[7].shape[2]
+def forward_kernel(rim, *refs):
+    where_ref, stencil_ref, mix_ref = refs[:3]
+    act_ref, slope_ref, xs, hs, resp, band, blend = refs[8:]
+    weights_kernel(rim, False, where_ref, stencil_ref, mix_ref, band, blend)
+    width = blend.shape[1]
     chans = act_ref.shape[2]
     root = math.sqrt(2.0 / math.pi)
 
@@ -512,42 +625,59 @@
         for j in range(width // chans):
             act_ref[g * (width // chans) + j, i] = act[j * chans : (j + 1) * chans, :].astype(bf16)
 
-    conv_body(*refs[:8], *refs[10:], emit)
+    conv_body(*refs[3:8], band, blend, xs, hs, resp, emit)
 
 
 def adjoint_kernel(*refs):
-    cot_ref, grad_ref = refs[8:10]
-    width = refs[7].shape[2]
+    cot_ref, grad_ref = refs[7:9]
+    width = refs[6].shape[1]
 
     def emit(g, i, v):
         at = slice(g * width, (g + 1) * width)
         grad_ref[i, at, :] = (cot_ref[i, at, :].astype(f32) + v).astype(bf16)
 
-    conv_body(*refs[:8], *refs[10:], emit)
-
-
-def conv_call(kernel, name, where, x, halo, stencil, mix, extra, outs):
+    conv_body(*refs[:7], *refs[9:], emit)
+
+
+def conv_scratch(rim, x, width):
     rows, channels, cols = x.shape
+    flat = (rows + 2 * rim) * channels
+    return [
+        pltpu.VMEM((flat, cols), f32),
+        pltpu.VMEM((flat, cols), f32),
+        pltpu.VMEM((rows, width * 16, cols), bf16),
+    ]
+
+
+def conv_forward(where, stencil, mix, rim, x, halo, shape):
     groups, _, width = mix.shape
-    ins = (where, x, *halo, stencil, mix, *extra)
-    rim = stencil.shape[1] // 10
-    flat = (rows + 2 * rim) * channels
-    return pl.pallas_call(
-        kernel,
-        out_shape=outs,
-        in_specs=[pl.BlockSpec(memory_space=pltpu.SMEM)] + vmem(len(ins) - 1),
-        out_specs=tuple(vmem(len(outs))),
+    return pl.pallas_call(
+        functools.partial(forward_kernel, rim),
+        out_shape=(jax.ShapeDtypeStruct(shape, bf16), jax.ShapeDtypeStruct(x.shape, f32)),
+        in_specs=[pl.BlockSpec(memory_space=pltpu.SMEM)] + vmem(7),
+        out_specs=tuple(vmem(2)),
         scratch_shapes=[
-            pltpu.VMEM((flat, cols), f32),
-            pltpu.VMEM((flat, cols), f32),
-            pltpu.VMEM((rows, width * 16, cols), bf16),
-            pltpu.VMEM((rows * 16, 128), bf16),
+            *conv_scratch(rim, x, width),
+            pltpu.VMEM((x.shape[0] * 16, 128), bf16),
             pltpu.VMEM((groups, width, width * 16), bf16),
         ],
         compiler_params=params(),
         cost_estimate=cost(1.2e10, 4e6),
-        name=name,
-    )(*ins)
+        name="conv_forward",
+    )(where, stencil, mix, x, *halo)
+
+
+def conv_adjoint(weights, rim, x, halo, cot):
+    return pl.pallas_call(
+        adjoint_kernel,
+        out_shape=jax.ShapeDtypeStruct(x.shape, bf16),
+        in_specs=vmem(8),
+        out_specs=vmem(1)[0],
+        scratch_shapes=conv_scratch(rim, x, weights[1].shape[1]),
+        compiler_params=params(),
+        cost_estimate=cost(1.2e10, 4e6),
+        name="conv_adjoint",
+    )(x, *halo, *weights, cot)
 
 
 def shifted(axis, step):
@@ -628,7 +758,6 @@
     strips = circ_c[:, body : body + blocks]
     left = lax.dynamic_index_in_dim(strips, (lon_index + lon_count - 1) % lon_count, 0, False)
     right = lax.dynamic_index_in_dim(strips, (lon_index + 1) % lon_count, 0, False)
-    halo = lat_rims(field, left, right, rim)
     offsets = jnp.abs(jnp.arange(2 * rim + 1, dtype=jnp.int32) - rim)
     pad = ((rim, rim), (0, 0), (0, 0), (0, 0))
     basis_ext = lax.dynamic_slice_in_dim(jnp.pad(basis_values, pad), row_start, rows + 2 * rim, 0)
@@ -637,69 +766,46 @@
     )
     inside = offsets[None, None, :] <= reach_ext[:, :, None]
     weights_ext = jnp.where(inside[..., None], basis_ext, 0.0)
-    stencil = stencil_rows(weights_ext[rim : rim + rows])
-    span = 2 * rim + 1
-    flipped = jnp.stack(
-        [weights_ext[a : a + rows, span - 1 - a, ::-1, :] for a in range(span)], axis=1
-    )
-    stencil_adj = stencil_rows(flipped)
+    stencil = stencil_rows(weights_ext)
     mix = mix_weight.reshape(groups, k_count * width, width)
     mix_adj = jnp.transpose(mix_weight, (0, 1, 3, 2)).reshape(groups, k_count * width, width)
     where = jnp.stack([lat_index, jnp.int32(nlat)]).astype(jnp.int32)
-    act, slope = conv_call(
-        forward_kernel,
-        "conv_forward",
-        where,
-        field,
-        halo,
-        stencil,
-        mix,
-        (),
-        (
-            jax.ShapeDtypeStruct((lon_count, rows, chans, cols), bf16),
-            jax.ShapeDtypeStruct((rows, channels, cols), f32),
-        ),
-    )
-
     tab = lon_table(degrees, nlon, lat_count)
-    table, flip = legendre_tables(lat_index, degrees, lat_count, rows, m_count)
+    legendre = legendre_inputs(lat_index, degrees, lat_count, rows, m_count)
     theta = math.pi * (np.arange(nlat) + 0.5) / nlat
     quad = 2.0 * math.pi * math.pi / nlat * np.sin(theta) / nlon
     quad_rows = np.repeat(quad.reshape(lat_count, rows), chans, axis=1).astype(np.float32)
     quad_lanes = lax.dynamic_slice_in_dim(jnp.asarray(quad_rows), lat_index, 1, 0)
     post = np.broadcast_to(quad.reshape(lat_count, rows).T.reshape(nlat, 1), (nlat, 128))
-    gains = lax.dynamic_slice_in_dim(filter_weight, lon_index * chans, chans, 1)
-    gains = jnp.pad(jnp.concatenate([gains] * 2, axis=1), ((0, 0), (0, 128 - 2 * chans)))
-
     post = jnp.asarray(post.astype(np.float32))
+    here = jnp.stack([lat_index, lon_index]).astype(jnp.int32)
     shape = (lon_count, rows, chans, cols)
+
     send_1 = analysis(circ_c, body, tab, quad_lanes, lat_count, True)
+    halo = lat_rims(field, left, right, rim)
+    send_1, halo = lax.optimization_barrier((send_1, halo))
     recv_1 = lax.all_to_all(send_1, "lat", 0, 0, tiled=True)
-    recv_1, act = lax.optimization_barrier((recv_1, act))
+    act, slope = conv_forward(where, stencil, mix, rim, field, halo, shape)
+    act, after = lax.optimization_barrier((act, here))
+    table, flip = legendre_tables(after, legendre, m_count, degrees, nlat)
+    recv_1, act, table, flip = lax.optimization_barrier((recv_1, act, table, flip))
     circ_f = lax.all_to_all(act, "lon", 0, 0, tiled=True)
-    filtered_c = filter_step(lat_index, recv_1, table, flip, gains, post, chans, True)
+    filtered_c = filter_step(here, recv_1, filter_weight, post, table, flip, chans, True)
     send_2 = analysis(circ_f, body, tab, quad_lanes, lat_count, False, (filtered_c,))
     recv_2 = lax.all_to_all(send_2, "lat", 0, 0, tiled=True)
+    stencil, send_2 = lax.optimization_barrier((stencil, send_2))
+    weights_adj = conv_weights(where, stencil, mix_adj, rim, True)
+    recv_2, weights_adj = lax.optimization_barrier((recv_2, weights_adj))
     cot_act = lax.all_to_all(synthesis(recv_2, tab, 1, shape), "lon", 0, 0, tiled=True)
-    filtered_f = filter_step(lat_index, recv_2, table, flip, gains, post, chans, False)
-    cot_act, filtered_f = lax.optimization_barrier((cot_act, filtered_f))
+    filtered_f = filter_step(here, recv_2, filter_weight, post, table, flip, chans, False)
     recv_3 = lax.all_to_all(filtered_f, "lat", 0, 0, tiled=True)
     branch = lax.all_to_all(synthesis(recv_3, tab, 0, shape), "lon", 0, 0, tiled=True)
 
     cot_conv, first_c, last_c = slope_step(cot_act, slope, edge)
     left_c = lax.ppermute(last_c, "lon", shifted("lon", 1))
     right_c = lax.ppermute(first_c, "lon", shifted("lon", -1))
-    (grad_field,) = conv_call(
-        adjoint_kernel,
-        "conv_adjoint",
-        where,
-        cot_conv,
-        lat_rims(cot_conv, left_c, right_c, rim),
-        stencil_adj,
-        mix_adj,
-        (cot,),
-        (jax.ShapeDtypeStruct((rows, channels, cols), bf16),),
-    )
+    halo_c = lat_rims(cot_conv, left_c, right_c, rim)
+    grad_field = conv_adjoint(weights_adj, rim, cot_conv, halo_c, cot)
     branch = jnp.transpose(branch, (1, 0, 2, 3)).reshape(rows, channels, cols)
     block_out = (field.astype(f32) + branch.astype(f32)).astype(bf16)
     return block_out[None], grad_field[None]

time: 190 us -> 179 us (0.942)
  local copies, waits for them, and re-layouts: 36 us -> 20.4 us
  waiting for transfers between devices: 39.9 us -> 30.3 us
  Pallas kernels: 53 us -> 60.7 us
  starting transfers between devices: 52.6 us -> 58.9 us
    unnamed x100 -> x56, local copies, waits for them, and re-layouts: 24.6 us -> 16.4 us
    all_to_all x1, starting transfers between devices: 4.78 us -> 9.69 us  [local(): recv_2 = lax.all_to_all(send_2, 'lat', 0, 0, tiled=True)]
    all_to_all x1, waiting for transfers between devices: 4.86 us -> 0.01 us  [local(): recv_1 = lax.all_to_all(send_1, 'lat', 0, 0, tiled=True)]
    pallas_call x2, Pallas kernels: 14.3 us -> 18.9 us  [filter_step(): pl.pallas_call(functools.partial(filter_kernel, m_count, chans, cotangent...]
    ppermute x1, waiting for transfers between devices: 0.01 us -> 4.41 us  [local(): left_c = lax.ppermute(last_c, 'lon', shifted('lon', 1))]
    all_to_all x1, waiting for transfers between devices: 4.22 us -> 0.01 us  [local(): circ_c = lax.all_to_all(sent, 'lon', 0, 0, tiled=True)]
    all_to_all x1, waiting for transfers between devices: 4.7 us -> 1.28 us  [local(): recv_3 = lax.all_to_all(filtered_f, 'lat', 0, 0, tiled=True)]
    pallas_call x3 -> x4, Pallas kernels: 29.6 us -> 32 us  [the longest x1 10.9 us: conv_forward(): pl.pallas_call(functools.partial(forward_kernel, rim), out_shape=(jax.Sha...]
  transfers between devices with their start and end apart: 13 -> 13, of which waited for: 5 -> 6; matrix products, arithmetic and copies ran while one was open for 9% -> 6% of each run, Pallas kernels for 26% -> 32%
where the time goes in v2:
time: 179 us; the launch traced here: 177 us
  Pallas kernels  60.7 us (34%)
  starting transfers between devices  58.9 us (33%)
  waiting for transfers between devices  30.3 us (17%)
  local copies, waits for them, and re-layouts  20.4 us (11%)
  other arithmetic  6.21 us (3%)
    all_to_all x1, waiting for transfers between devices, local(): recv_2 = lax.all_to_all(send_2, 'lat', 0, 0, tiled=True)  22.4 us
    pallas_call x2, Pallas kernels, filter_step(): pl.pallas_call(functools.partial(filter_kernel, m_count, chans, cotangent...  18.9 us
    unnamed x56, local copies, waits for them, and re-layouts  16.4 us
    ppermute x2, starting transfers between devices, lat_rims(): high = lax.ppermute(high, 'lat', shifted('lat', -1))  11.7 us
    pallas_call x1, Pallas kernels, conv_forward(): pl.pallas_call(functools.partial(forward_kernel, rim), out_shape=(jax.Sha...  10.9 us
    pallas_call x1, Pallas kernels, legendre_tables(): pl.pallas_call(functools.partial(legendre_kernel, m_count), out_shape=(ja...  10 us
    all_to_all x1, starting transfers between devices, local(): recv_2 = lax.all_to_all(send_2, 'lat', 0, 0, tiled=True)  9.69 us
    pallas_call x1, Pallas kernels, conv_adjoint(): pl.pallas_call(adjoint_kernel, out_shape=jax.ShapeDtypeStruct(x.shape, bf...  9.63 us
  transfers between devices with their start and end apart: 13, of which 6 were waited for; matrix products, arithmetic and copies ran while one was open for 6% of the time, Pallas kernels for 32%

profile of v2, /device:TPU:2, one launch (start us, length us, event | category | flops | bytes accessed | tf_op | source)
XLA Modules:
  0.0 177.4 jit_solution(13923319565911033794)
XLA Ops:
  4.1 6.1 %all-to-all-start = ((bf16[8,336,128]{2,1,0:T(8,128)(2,1)}), bf16[8,336,128]{2,1,0:T(8,128)(2,1)S(1)}, u32[]{:S(2)}, u32[]{:S(2)}) async-start(bf16[8,336,128]{2,1,0:T(8,128)(2,1)} %start.1), calls=%async_computation | async-start | bytes 1376256 | tf_op jit(solution)/shard_map/all_to_all | solution.py:755
  10.2 3.0 %fusion.3 = (f32[768,128]{1,0:T(8,128)S(1)}, f32[768,128]{1,0:T(8,128)}) fusion(s32[768]{0:T(1024)S(1)} %copy-done.25, s32[768]{0:T(1024)S(1)} %copy-done.26), kind=kLoop, calls=%fused_computation.9 | loop fusion | flops 1474560 | bytes 792576 | tf_op jit(solution)/shard_map/sin | solution.py:160
  18.5 1.7 lon_table.1.refs_1_.tab_ref
  21.8 6.4 %collective-permute-start.1 = (bf16[400,128]{1,0:T(8,128)(2,1)S(1)}, bf16[400,128]{1,0:T(8,128)(2,1)S(1)}, u32[]{:S(2)}, u32[]{:S(2)}) collective-permute-start(bf16[400,128]{1,0:T(8,128)(2,1)S(1)} %pad_maximum_fusion.1), channel_id=1, source_target_pairs={{0,248},{8,0},{16,8},{24,16},{32,24},{40,32},{48,40},{56,48},{64,5... | collective-permute-start | bytes 307208 | tf_op jit(solution)/shard_map/ppermute | solution.py:693
  28.2 1.8 %analysis.2 = bf16[32,56,128]{2,1,0:T(8,128)(2,1)} custom-call(bf16[8,336,128]{2,1,0:T(8,128)(2,1)S(1)} %all-to-all-done.refs_0_, bf16[768,1024]{1,0:T(8,128)(2,1)S(1)} %lon_table.1.refs_1_.tab_ref, f32[1,288]{1,0:T(1,128)S(1)} %constant_dynamic-slice_fusion.5.refs_2_), custom_call_target="tpu_custom_call" | custom-call | flops 452984832 | bytes 3000000 | tf_op jit(solution)/shard_map/analysis/pallas_call | solution.py:199
  31.1 7.4 %all-to-all-start.1 = ((bf16[32,56,128]{2,1,0:T(8,128)(2,1)}), bf16[32,56,128]{2,1,0:T(8,128)(2,1)S(1)}, u32[]{:S(2)}, u32[]{:S(2)}) async-start(bf16[32,56,128]{2,1,0:T(8,128)(2,1)} %analysis.2), calls=%async_computation.1 | async-start | bytes 917504 | tf_op jit(solution)/shard_map/all_to_all | solution.py:787
  39.5 10.9 %conv_forward.1 = (bf16[8,12,24,128]{3,2,1,0:T(8,128)(2,1)}, f32[12,192,128]{2,1,0:T(8,128)S(1)}) custom-call(s32[2]{0:T(128)S(1)} %pad_add_fusion.1.refs_0_.idx_ref, bf16[256,25]{1,0:T(8,128)(2,1)S(1)} %bitcast.41, bf16[4,432,48]{2,1,0:T(8,128)(2,1)S(1)} %bitcast.38, bf16[12,192,128]{2,1,0:T(8,128)(2,1)S(1)} %bitcast.35, ...), custom_call_target="tpu_custom_call" | custom-call | flops 12000000000 | bytes 4000000 | tf_op jit(solution)/shard_map/conv_forward/pallas_call | solution.py:654
  51.5 10.0 %legendre_tables.1 = (bf16[12,384,384]{2,1,0:T(8,128)(2,1)}, bf16[12,384,384]{2,1,0:T(8,128)(2,1)}) custom-call(s32[2]{0:T(128)} %pad_add_fusion.idx_ref, f32[384]{0:T(512)} %constant.97.clone.rise_ref, f32[384]{0:T(512)} %constant.98.clone.fall_ref, f32[16,1]{1,0:T(8,128)} %copy.24.norm_ref, f32[1,384]{1,0:T(1,128)} %constant.99.clone.cos_ref, ...), custom_call_target="tpu_custom_call" | custom-call | flops 2000000000 | bytes 7000000 | tf_op jit(solution)/shard_map/legendre_tables/pallas_call | solution.py:320
  62.3 5.7 %all-to-all-start.2 = ((bf16[8,12,24,128]{3,2,1,0:T(8,128)(2,1)}), bf16[8,12,24,128]{3,2,1,0:T(8,128)(2,1)S(1)}, u32[]{:S(2)}, u32[]{:S(2)}) async-start(bf16[8,12,24,128]{3,2,1,0:T(8,128)(2,1)} %get-tuple-element.36), calls=%async_computation.2 | async-start | bytes 1179648 | tf_op jit(solution)/shard_map/all_to_all | solution.py:792
  68.0 9.4 %filter_step.2.refs_3_ = bf16[32,56,128]{2,1,0:T(8,128)(2,1)} custom-call(s32[2]{0:T(128)} %pad_add_fusion.idx_ref, bf16[32,56,128]{2,1,0:T(8,128)(2,1)} %copy-done.22, f32[384,192]{1,0:T(8,128)} %copy.25.weight_ref, f32[384,128]{1,0:T(8,128)} %constant.102.clone.post_ref, bf16[12,384,384]{2,1,0:T(8,128)(2,1)} %get-tuple-element.38.table_in, ...), custom_call_target="tpu_custom_call" | custom-call | flops 8000000000 | bytes 9000000 | tf_op jit(solution)/shard_map/filter_step/pallas_call | solution.py:379
  78.8 2.0 %analysis.3 = bf16[32,112,128]{2,1,0:T(8,128)(2,1)} custom-call(bf16[8,12,24,128]{3,2,1,0:T(8,128)(2,1)S(1)} %all-to-all-done.2.refs_0_, bf16[768,1024]{1,0:T(8,128)(2,1)S(1)} %lon_table.1.refs_1_.tab_ref, f32[1,288]{1,0:T(1,128)S(1)} %constant_dynamic-slice_fusion.5.refs_2_, bf16[32,56,128]{2,1,0:T(8,128)(2,1)S(1)} %copy-done.9), custom_call_target="tpu_custom_call" | custom-call | flops 452984832 | bytes 3000000 | tf_op jit(solution)/shard_map/analysis/pallas_call | solution.py:199
  80.8 9.7 %all-to-all-start.3 = ((bf16[32,112,128]{2,1,0:T(8,128)(2,1)}), bf16[32,112,128]{2,1,0:T(8,128)(2,1)S(1)}, u32[]{:S(2)}, u32[]{:S(2)}) async-start(bf16[32,112,128]{2,1,0:T(8,128)(2,1)} %analysis.3), calls=%async_computation.3 | async-start | bytes 1835008 | tf_op jit(solution)/shard_map/all_to_all | solution.py:795
  93.3 1.5 conv_weights.1
  95.5 22.4 %all-to-all-done.3.recv_ref = bf16[32,112,128]{2,1,0:T(8,128)(2,1)S(1)} async-done(((bf16[32,112,128]{2,1,0:T(8,128)(2,1)}), bf16[32,112,128]{2,1,0:T(8,128)(2,1)S(1)}, u32[]{:S(2)}, u32[]{:S(2)}) %all-to-all-start.3) | async-done | bytes 917536 | tf_op jit(solution)/shard_map/all_to_all | solution.py:795
  119.6 5.5 %all-to-all-start.6 = ((bf16[8,12,24,128]{3,2,1,0:T(8,128)(2,1)}), bf16[8,12,24,128]{3,2,1,0:T(8,128)(2,1)S(1)}, u32[]{:S(2)}, u32[]{:S(2)}) async-start(bf16[8,12,24,128]{3,2,1,0:T(8,128)(2,1)} %copy-done.3), calls=%async_computation.6 | async-start | bytes 1179648 | tf_op jit(solution)/shard_map/all_to_all | solution.py:799
  125.1 9.5 %filter_step.3 = bf16[32,56,128]{2,1,0:T(8,128)(2,1)} custom-call(s32[2]{0:T(128)} %pad_add_fusion.idx_ref, bf16[32,112,128]{2,1,0:T(8,128)(2,1)} %copy-done, f32[384,192]{1,0:T(8,128)} %copy.25.weight_ref, f32[384,128]{1,0:T(8,128)} %constant.102.clone.post_ref, bf16[12,384,384]{2,1,0:T(8,128)(2,1)} %get-tuple-element.38.table_in, ...), custom_call_target="tpu_custom_call" | custom-call | flops 8000000000 | bytes 9000000 | tf_op jit(solution)/shard_map/filter_step/pallas_call | solution.py:379
  134.6 3.9 %all-to-all-start.4 = ((bf16[32,56,128]{2,1,0:T(8,128)(2,1)}), bf16[32,56,128]{2,1,0:T(8,128)(2,1)S(1)}, u32[]{:S(2)}, u32[]{:S(2)}) async-start(bf16[32,56,128]{2,1,0:T(8,128)(2,1)} %filter_step.3), calls=%async_computation.4 | async-start | bytes 917504 | tf_op jit(solution)/shard_map/all_to_all | solution.py:801
  140.4 3.1 %collective-permute-start.3 = (bf16[40,128]{1,0:T(8,128)(2,1)S(1)}, bf16[40,128]{1,0:T(8,128)(2,1)S(1)}, u32[]{:S(2)}, u32[]{:S(2)}) collective-permute-start(bf16[40,128]{1,0:T(8,128)(2,1)S(1)} %get-tuple-element.47), channel_id=1, source_target_pairs={{0,7},{1,0},{2,1},{3,2},{4,3},{5,4},{6,5},{7,6},{8,15},{9,8},{10,9... | collective-permute-start | bytes 30728 | tf_op jit(solution)/shard_map/ppermute | solution.py:806
  143.5 1.4 collective-permute-done.3.refs_4_
  144.9 4.4 %collective-permute-done.2.refs_3_ = bf16[40,128]{1,0:T(8,128)(2,1)S(1)} collective-permute-done((bf16[40,128]{1,0:T(8,128)(2,1)S(1)}, bf16[40,128]{1,0:T(8,128)(2,1)S(1)}, u32[]{:S(2)}, u32[]{:S(2)}) %collective-permute-start.2) | collective-permute-done | bytes 10272 | tf_op jit(solution)/shard_map/ppermute | solution.py:805
  150.6 5.4 %collective-permute-start.5 = (bf16[400,128]{1,0:T(8,128)(2,1)}, bf16[400,128]{1,0:T(8,128)(2,1)S(1)}, u32[]{:S(2)}, u32[]{:S(2)}) collective-permute-start(bf16[400,128]{1,0:T(8,128)(2,1)} %pad_maximum_fusion.3), channel_id=1, source_target_pairs={{0,248},{8,0},{16,8},{24,16},{32,24},{40,32},{48,40},{56,48},{64,5... | collective-permute-start | bytes 307208 | tf_op jit(solution)/shard_map/ppermute | solution.py:693
  157.2 1.6 synthesis.2
  158.9 5.7 %all-to-all-start.5 = ((bf16[8,12,24,128]{3,2,1,0:T(8,128)(2,1)}), bf16[8,12,24,128]{3,2,1,0:T(8,128)(2,1)S(1)}, u32[]{:S(2)}, u32[]{:S(2)}) async-start(bf16[8,12,24,128]{3,2,1,0:T(8,128)(2,1)} %synthesis.2), calls=%async_computation.5 | async-start | bytes 1179648 | tf_op jit(solution)/shard_map/all_to_all | solution.py:802
  166.6 9.6 %conv_adjoint.1 = bf16[12,192,128]{2,1,0:T(8,128)(2,1)} custom-call(bf16[12,192,128]{2,1,0:T(8,128)(2,1)S(1)} %copy-done.14, bf16[400,128]{1,0:T(8,128)(2,1)S(1)} %collective-permute-done.4.refs_1_, bf16[400,128]{1,0:T(8,128)(2,1)S(1)} %collective-permute-done.5.refs_2_, bf16[40,128]{1,0:T(8,128)(2,1)S(1)} %collective-permute-done.2.refs_3_, ...), custom_call_target="tpu_custom_call" | custom-call | flops 12000000000 | bytes 4000000 | tf_op jit(solution)/shard_map/conv_adjoint/pallas_call | solution.py:671
  (99 shorter events, 28.4 us)
Async XLA Ops:
  2.8 7.4 %copy-start.25 = (s32[768]{0:T(1024)S(1)}, s32[768]{0:T(1024)}, u32[]{:S(2)}) copy-start(s32[768]{0:T(1024)} %constant.94.clone) | copy-start | bytes 9220
  2.8 7.4 %copy-start.26 = (s32[768]{0:T(1024)S(1)}, s32[768]{0:T(1024)}, u32[]{:S(2)}) copy-start(s32[768]{0:T(1024)} %constant.93.clone) | copy-start | bytes 9220
  4.1 9.1 %copy-start.24 = (s32[384,5]{0,1:T(8,128)S(1)}, s32[384,5]{0,1:T(8,128)}, u32[]{:S(2)}) copy-start(s32[384,5]{0,1:T(8,128)} %param.18) | copy-start | bytes 23044
  4.1 9.2 %copy-start.21 = (f32[384,5,5,9]{0,2,3,1:T(8,128)S(1)}, f32[384,5,5,9]{0,2,3,1:T(8,128)}, u32[]{:S(2)}) copy-start(f32[384,5,5,9]{0,2,3,1:T(8,128)} %param.17) | copy-start | bytes 1036804
  4.1 17.6 %all-to-all-start = ((bf16[8,336,128]{2,1,0:T(8,128)(2,1)}), bf16[8,336,128]{2,1,0:T(8,128)(2,1)S(1)}, u32[]{:S(2)}, u32[]{:S(2)}) async-start(bf16[8,336,128]{2,1,0:T(8,128)(2,1)} %start.1), calls=%async_computation | async-start | bytes 1376256 | tf_op jit(solution)/shard_map/all_to_all | solution.py:755
  10.1 4.9 %copy-start.23 = (f32[384,192]{0,1:T(8,128)S(1)}, f32[384,192]{0,1:T(8,128)}, u32[]{:S(2)}) copy-start(f32[384,192]{0,1:T(8,128)} %param.20) | copy-start | bytes 884740
  18.5 3.1 %copy-start.2 = (bf16[1,12,192,128]{3,2,1,0:T(8,128)(2,1)S(1)}, bf16[1,12,192,128]{3,2,1,0:T(8,128)(2,1)}, u32[]{:S(2)}) copy-start(bf16[1,12,192,128]{3,2,1,0:T(8,128)(2,1)} %param.16) | copy-start | bytes 1769476
  21.7 8.7 %collective-permute-start = (bf16[400,128]{1,0:T(8,128)(2,1)S(1)}, bf16[400,128]{1,0:T(8,128)(2,1)S(1)}, u32[]{:S(2)}, u32[]{:S(2)}) collective-permute-start(bf16[400,128]{1,0:T(8,128)(2,1)S(1)} %pad_maximum_fusion), channel_id=1, source_target_pairs={{0,8},{8,16},{16,24},{24,32},{32,40},{40,48},{48,56},{56,64},{64,7... | collective-permute-start | bytes 307208 | tf_op jit(solution)/shard_map/ppermute | solution.py:692
  21.8 16.7 %copy-start.10 = (bf16[4,9,48,48]{3,2,1,0:T(8,128)(2,1)S(1)}, bf16[4,9,48,48]{3,2,1,0:T(8,128)(2,1)}, u32[]{:S(2)}) copy-start(bf16[4,9,48,48]{3,2,1,0:T(8,128)(2,1)} %param.19) | copy-start | bytes 497668
  21.8 16.7 %copy-start.15 = (bf16[16,16,25]{2,1,0:T(8,128)(2,1)S(1)}, bf16[16,16,25]{2,1,0:T(8,128)(2,1)}, u32[]{:S(2)}) copy-start(bf16[16,16,25]{2,1,0:T(8,128)(2,1)} %pad.15.clone) | copy-start | bytes 38404
  21.8 8.6 %collective-permute-start.1 = (bf16[400,128]{1,0:T(8,128)(2,1)S(1)}, bf16[400,128]{1,0:T(8,128)(2,1)S(1)}, u32[]{:S(2)}, u32[]{:S(2)}) collective-permute-start(bf16[400,128]{1,0:T(8,128)(2,1)S(1)} %pad_maximum_fusion.1), channel_id=1, source_target_pairs={{0,248},{8,0},{16,8},{24,16},{32,24},{40,32},{48,40},{56,48},{64,5... | collective-permute-start | bytes 307208 | tf_op jit(solution)/shard_map/ppermute | solution.py:693
  31.1 30.4 %all-to-all-start.1 = ((bf16[32,56,128]{2,1,0:T(8,128)(2,1)}), bf16[32,56,128]{2,1,0:T(8,128)(2,1)S(1)}, u32[]{:S(2)}, u32[]{:S(2)}) async-start(bf16[32,56,128]{2,1,0:T(8,128)(2,1)} %analysis.2), calls=%async_computation.1 | async-start | bytes 917504 | tf_op jit(solution)/shard_map/all_to_all | solution.py:787
  62.3 15.5 %all-to-all-start.2 = ((bf16[8,12,24,128]{3,2,1,0:T(8,128)(2,1)}), bf16[8,12,24,128]{3,2,1,0:T(8,128)(2,1)S(1)}, u32[]{:S(2)}, u32[]{:S(2)}) async-start(bf16[8,12,24,128]{3,2,1,0:T(8,128)(2,1)} %get-tuple-element.36), calls=%async_computation.2 | async-start | bytes 1179648 | tf_op jit(solution)/shard_map/all_to_all | solution.py:792
  80.8 37.1 %all-to-all-start.3 = ((bf16[32,112,128]{2,1,0:T(8,128)(2,1)}), bf16[32,112,128]{2,1,0:T(8,128)(2,1)S(1)}, u32[]{:S(2)}, u32[]{:S(2)}) async-start(bf16[32,112,128]{2,1,0:T(8,128)(2,1)} %analysis.3), calls=%async_computation.3 | async-start | bytes 1835008 | tf_op jit(solution)/shard_map/all_to_all | solution.py:795
  119.6 15.0 %all-to-all-start.6 = ((bf16[8,12,24,128]{3,2,1,0:T(8,128)(2,1)}), bf16[8,12,24,128]{3,2,1,0:T(8,128)(2,1)S(1)}, u32[]{:S(2)}, u32[]{:S(2)}) async-start(bf16[8,12,24,128]{3,2,1,0:T(8,128)(2,1)} %copy-done.3), calls=%async_computation.6 | async-start | bytes 1179648 | tf_op jit(solution)/shard_map/all_to_all | solution.py:799
  134.6 22.6 %all-to-all-start.4 = ((bf16[32,56,128]{2,1,0:T(8,128)(2,1)}), bf16[32,56,128]{2,1,0:T(8,128)(2,1)S(1)}, u32[]{:S(2)}, u32[]{:S(2)}) async-start(bf16[32,56,128]{2,1,0:T(8,128)(2,1)} %filter_step.3), calls=%async_computation.4 | async-start | bytes 917504 | tf_op jit(solution)/shard_map/all_to_all | solution.py:801
  138.5 1.3 copy-start.6
  140.4 10.2 %copy-start.13 = (bf16[12,192,128]{2,1,0:T(8,128)(2,1)}, bf16[12,192,128]{2,1,0:T(8,128)(2,1)S(1)}, u32[]{:S(2)}) copy-start(bf16[12,192,128]{2,1,0:T(8,128)(2,1)S(1)} %get-tuple-element.45.refs_0_) | copy-start | bytes 1769476
  140.4 4.5 %collective-permute-start.3 = (bf16[40,128]{1,0:T(8,128)(2,1)S(1)}, bf16[40,128]{1,0:T(8,128)(2,1)S(1)}, u32[]{:S(2)}, u32[]{:S(2)}) collective-permute-start(bf16[40,128]{1,0:T(8,128)(2,1)S(1)} %get-tuple-element.47), channel_id=1, source_target_pairs={{0,7},{1,0},{2,1},{3,2},{4,3},{5,4},{6,5},{7,6},{8,15},{9,8},{10,9... | collective-permute-start | bytes 30728 | tf_op jit(solution)/shard_map/ppermute | solution.py:806
  143.5 5.8 %collective-permute-start.2 = (bf16[40,128]{1,0:T(8,128)(2,1)S(1)}, bf16[40,128]{1,0:T(8,128)(2,1)S(1)}, u32[]{:S(2)}, u32[]{:S(2)}) collective-permute-start(bf16[40,128]{1,0:T(8,128)(2,1)S(1)} %get-tuple-element.46), channel_id=1, source_target_pairs={{0,1},{1,2},{2,3},{3,4},{4,5},{5,6},{6,7},{7,0},{8,9},{9,10},{10,1... | collective-permute-start | bytes 30728 | tf_op jit(solution)/shard_map/ppermute | solution.py:805
  150.0 14.6 %collective-permute-start.4 = (bf16[400,128]{1,0:T(8,128)(2,1)}, bf16[400,128]{1,0:T(8,128)(2,1)S(1)}, u32[]{:S(2)}, u32[]{:S(2)}) collective-permute-start(bf16[400,128]{1,0:T(8,128)(2,1)} %pad_maximum_fusion.2), channel_id=1, source_target_pairs={{0,8},{8,16},{16,24},{24,32},{32,40},{40,48},{48,56},{56,64},{64,7... | collective-permute-start | bytes 307208 | tf_op jit(solution)/shard_map/ppermute | solution.py:692
  150.6 14.0 %copy-start.8 = (bf16[1,12,192,128]{3,2,1,0:T(8,128)(2,1)S(1)}, bf16[1,12,192,128]{3,2,1,0:T(8,128)(2,1)}, u32[]{:S(2)}) copy-start(bf16[1,12,192,128]{3,2,1,0:T(8,128)(2,1)} %param.21) | copy-start | bytes 1769476
  150.6 14.0 %collective-permute-start.5 = (bf16[400,128]{1,0:T(8,128)(2,1)}, bf16[400,128]{1,0:T(8,128)(2,1)S(1)}, u32[]{:S(2)}, u32[]{:S(2)}) collective-permute-start(bf16[400,128]{1,0:T(8,128)(2,1)} %pad_maximum_fusion.3), channel_id=1, source_target_pairs={{0,248},{8,0},{16,8},{24,16},{32,24},{40,32},{48,40},{56,48},{64,5... | collective-permute-start | bytes 307208 | tf_op jit(solution)/shard_map/ppermute | solution.py:693
  158.9 17.4 %all-to-all-start.5 = ((bf16[8,12,24,128]{3,2,1,0:T(8,128)(2,1)}), bf16[8,12,24,128]{3,2,1,0:T(8,128)(2,1)S(1)}, u32[]{:S(2)}, u32[]{:S(2)}) async-start(bf16[8,12,24,128]{3,2,1,0:T(8,128)(2,1)} %synthesis.2), calls=%async_computation.5 | async-start | bytes 1179648 | tf_op jit(solution)/shard_map/all_to_all | solution.py:802
  (16 other events, 14.9 us)

commit v3 on v2

--- a/solution.py
+++ b/solution.py
@@ -41,11 +41,11 @@
     return pl.CostEstimate(flops=int(flops), bytes_accessed=int(nbytes), transcendentals=0)
 
 
-def legendre_fill(
-    m_count, idx_ref, rise_ref, fall_ref, norm_ref, cos_ref, logsin_ref, keep, table_ref, flip_ref,
-    table_out, flip_out, sems
+def legendre_kernel(
+    m_count, idx_ref, rise_ref, fall_ref, norm_ref, cos_ref, logsin_ref, table_out,
+    keep, table_ref, sems
 ):
-    m_pad, lat = norm_ref.shape[0], cos_ref.shape[1]
+    m_pad, lat = 16, cos_ref.shape[1]
     degrees = table_ref.shape[1]
     wide = lat // 128
     first = idx_ref[0] * m_count
@@ -55,9 +55,17 @@
     cosine = [
         jnp.broadcast_to(cos_ref[:, p * 128 : (p + 1) * 128], (m_pad, 128)) for p in range(wide)
     ]
+    local_row = lax.broadcasted_iota(jnp.int32, (m_pad, 128), 0)
+    norm = jnp.zeros((m_pad, 128), f32)
+    for m in range(m_count):
+        norm = jnp.where(local_row == m, norm_ref[first + m], norm)
     base = [
-        norm_ref[...] + order_real * logsin_ref[:, p * 128 : (p + 1) * 128] for p in range(wide)
+        norm + order_real * logsin_ref[:, p * 128 : (p + 1) * 128] for p in range(wide)
     ]
+
+    def copy_out(number):
+        at = pl.ds(pl.multiple_of(number * 16, 16), 16)
+        return pltpu.make_async_copy(table_ref.at[:, at], table_out.at[:, at], sems.at[number])
 
     def block(number, carry):
         latest, earlier, exponent, gain_b = carry
@@ -90,24 +98,22 @@
                 [keep[part, pl.ds(m, 16, stride=m_pad), :] for part in range(wide)], axis=1
             )
             table_ref[m, pl.ds(pl.multiple_of(number * 16, 16), 16), :] = rows.astype(bf16)
+        copy_out(number).start()
         return tuple(latest), tuple(earlier), tuple(exponent), gain_b
 
     zero = jnp.zeros((m_pad, 128), f32)
     zeros = (zero,) * wide
     lax.fori_loop(0, degrees // 16, block, (zeros, zeros, zeros, zero))
 
-    def turn(m, carry):
-        pltpu.make_async_copy(table_ref.at[m], table_out.at[m], sems.at[0, m]).start()
-        flip_ref[m] = jnp.transpose(table_ref[m])
-        pltpu.make_async_copy(flip_ref.at[m], flip_out.at[m], sems.at[1, m]).start()
+    def finish(number, carry):
+        copy_out(number).wait()
         return carry
 
-    lax.fori_loop(0, m_count, turn, 0)
-
-
-def legendre_inputs(lat_index, degrees, lat_count, row_count, m_count):
+    lax.fori_loop(0, degrees // 16, finish, 0)
+
+
+def legendre_inputs(degrees, lat_count, row_count):
     nlat = lat_count * row_count
-    m_pad = 16
     place = np.arange(nlat)
     t = (place % lat_count) * row_count + place // lat_count
     theta = math.pi * (t + 0.5) / nlat
@@ -115,15 +121,12 @@
     running = np.concatenate([[0.0], np.cumsum(np.log((2 * counter - 1) / (2 * counter)))])
     m = np.arange(degrees)
     norm = 0.5 * np.log((2 * m + 1) / (4 * math.pi)) + 0.5 * running
-    norms = np.zeros((lat_count, m_pad, 1), np.float32)
-    norms[:, :m_count, 0] = norm.reshape(lat_count, m_count)
-    norm_mine = lax.dynamic_index_in_dim(jnp.asarray(norms), lat_index, 0, keepdims=False)
     rise = np.sqrt(np.maximum(4.0 * m * m - 1.0, 1.0)).astype(np.float32)
     fall = (1.0 / np.sqrt(np.maximum(4.0 * m * m - 1.0, 1.0))).astype(np.float32)
     return (
         jnp.asarray(rise),
         jnp.asarray(fall),
-        norm_mine,
+        jnp.asarray(norm.astype(np.float32)),
         jnp.asarray(np.cos(theta)[None].astype(np.float32)),
         jnp.asarray(np.log(np.sin(theta))[None].astype(np.float32)),
     )
@@ -168,7 +171,7 @@
 
 
 def analysis_kernel(k_count, cotangent_pass, *refs):
-    circ_ref, tab_ref, quad_ref = refs[:3]
+    circ_ref, tab_ref = refs[:2]
     out_ref, keep = refs[-2:]
     sectors = circ_ref.shape[0]
     lines = keep.shape[1]
@@ -184,32 +187,32 @@
         row = lax.broadcasted_iota(jnp.int32, z.shape, 0)
         z = z * jnp.where((row == 0) | (row == k_count // 2), 1.0, 2.0)
     else:
-        z = z * quad_ref[...]
+        z = z * refs[2][...]
     keep[...] = z
     for e in range(owners):
         piece = keep[e * k_count : (e + 1) * k_count, :]
         out_ref[e, 0:height, :] = pack_rows(piece, k_count).astype(bf16)
-        if len(refs) > 5:
+        if not cotangent_pass:
             out_ref[e, height:, :] = refs[3][e]
 
 
-def analysis(circ, lines, tab, quad_lanes, owners, cotangent_pass, beside=()):
+def analysis(circ, lines, tab, owners, *field_pass):
     k_count = tab.shape[0] // owners
-    height = (2 * k_count + k_count // 3) * (1 + len(beside))
-    return pl.pallas_call(
-        functools.partial(analysis_kernel, k_count, cotangent_pass),
+    height = (2 * k_count + k_count // 3) * (2 if field_pass else 1)
+    return pl.pallas_call(
+        functools.partial(analysis_kernel, k_count, not field_pass),
         out_shape=jax.ShapeDtypeStruct((owners, height, 128), bf16),
-        in_specs=vmem(3 + len(beside)),
+        in_specs=vmem(2 + len(field_pass)),
         out_specs=vmem(1)[0],
         scratch_shapes=[pltpu.VMEM((tab.shape[0], lines), f32)],
         compiler_params=params(),
         cost_estimate=cost(2 * tab.shape[0] * tab.shape[1] * lines, 3e6),
         name="analysis",
-    )(circ, tab, quad_lanes, *beside)
+    )(circ, tab, *field_pass)
 
 
 def filter_body(
-    m_count, chans, cotangent_pass, idx_ref, recv_ref, weight_ref, post_ref, out_ref,
+    m_count, chans, cotangent_pass, idx_ref, lon_ref, recv_ref, weight_ref, post_ref, out_ref,
     took, give, gain, table_ref, flip_ref, ready
 ):
     places, height, _ = out_ref.shape
@@ -229,7 +232,7 @@
     weight = weight_ref[...]
     room = 256 - weight.shape[1]
     weight = jnp.concatenate([weight, jnp.zeros((weight.shape[0], room), f32)], axis=1)
-    weight = pltpu.roll(weight, lax.rem(256 - idx_ref[1] * chans, 256), 1)[:, 0:128]
+    weight = pltpu.roll(weight, lax.rem(256 - lon_ref[0] * chans, 256), 1)[:, 0:128]
     place = lax.broadcasted_iota(jnp.int32, weight.shape, 1)
     weight = jnp.where(place < chans, weight, 0.0)
     gain[...] = weight + pltpu.roll(weight, chans, 1)
@@ -298,46 +301,57 @@
     lax.fori_loop(0, places, store, 0, unroll=4)
 
 
-def legendre_kernel(
-    m_count, idx_ref, rise_ref, fall_ref, norm_ref, cos_ref, logsin_ref, table_out, flip_out,
-    keep, table, flip, sems
-):
-    legendre_fill(
-        m_count, idx_ref, rise_ref, fall_ref, norm_ref, cos_ref, logsin_ref, keep, table, flip,
-        table_out, flip_out, sems,
-    )
-
-    def finish(m, carry):
-        pltpu.make_async_copy(table.at[m], table_out.at[m], sems.at[0, m]).wait()
-        pltpu.make_async_copy(flip.at[m], flip_out.at[m], sems.at[1, m]).wait()
-        return carry
-
-    lax.fori_loop(0, m_count, finish, 0)
-
-
-def legendre_tables(where, legendre, m_count, degrees, nlat):
+def legendre_table(where, legendre, m_count, degrees, nlat):
     smem = pl.BlockSpec(memory_space=pltpu.SMEM)
     return pl.pallas_call(
         functools.partial(legendre_kernel, m_count),
-        out_shape=(
-            jax.ShapeDtypeStruct((m_count, degrees, nlat), bf16),
-            jax.ShapeDtypeStruct((m_count, nlat, degrees), bf16),
-        ),
-        in_specs=[smem] * 3 + vmem(3),
-        out_specs=tuple(hbm(2)),
+        out_shape=jax.ShapeDtypeStruct((m_count, degrees, nlat), bf16),
+        in_specs=[smem] * 4 + vmem(2),
+        out_specs=hbm(1)[0],
         scratch_shapes=[
             pltpu.VMEM((nlat // 128, 16 * 16, 128), f32),
-            *table_scratch(m_count, degrees, nlat),
+            pltpu.VMEM((m_count, degrees, nlat), bf16),
+            pltpu.SemaphoreType.DMA((degrees // 16,)),
         ],
         compiler_params=params(60),
-        cost_estimate=cost(2e9, 7e6),
-        name="legendre_tables",
+        cost_estimate=cost(2e9, 4e6),
+        name="legendre_table",
     )(where, *legendre)
 
 
+def flip_kernel(table_in, flip_out, table, flip, sems):
+    orders = table.shape[0]
+    for m in range(orders):
+        pltpu.make_async_copy(table_in.at[m], table.at[m], sems.at[0, m]).start()
+
+    def turn(m, carry):
+        pltpu.make_async_copy(table_in.at[m], table.at[m], sems.at[0, m]).wait()
+        flip[m] = jnp.transpose(table[m])
+        pltpu.make_async_copy(flip.at[m], flip_out.at[m], sems.at[1, m]).start()
+        return carry
+
+    lax.fori_loop(0, orders, turn, 0)
+    for m in range(orders):
+        pltpu.make_async_copy(flip.at[m], flip_out.at[m], sems.at[1, m]).wait()
+
+
+def flipped_table(table):
+    m_count, degrees, nlat = table.shape
+    return pl.pallas_call(
+        flip_kernel,
+        out_shape=jax.ShapeDtypeStruct((m_count, nlat, degrees), bf16),
+        in_specs=hbm(1),
+        out_specs=hbm(1)[0],
+        scratch_shapes=table_scratch(m_count, degrees, nlat),
+        compiler_params=params(60),
+        cost_estimate=cost(1e8, 7e6),
+        name="flip_table",
+    )(table)
+
+
 def filter_kernel(
-    m_count, chans, cotangent_pass, idx_ref, recv_ref, weight_ref, post_ref, table_in, flip_in,
-    out_ref, took, give, gain, table, flip, sems
+    m_count, chans, cotangent_pass, idx_ref, lon_ref, recv_ref, weight_ref, post_ref, table_in,
+    flip_in, out_ref, took, give, gain, table, flip, sems
 ):
     def begin(m, carry):
         pltpu.make_async_copy(table_in.at[m], table.at[m], sems.at[0, m]).start()
@@ -351,7 +365,7 @@
         pltpu.make_async_copy(flip_in.at[m], flip.at[m], sems.at[1, m]).wait()
 
     filter_body(
-        m_count, chans, cotangent_pass, idx_ref, recv_ref, weight_ref, post_ref, out_ref,
+        m_count, chans, cotangent_pass, idx_ref, lon_ref, recv_ref, weight_ref, post_ref, out_ref,
         took, give, gain, table, flip, ready,
     )
 
@@ -372,14 +386,14 @@
     ]
 
 
-def filter_step(where, recv, weight, post, table, flip, chans, cotangent_pass):
+def filter_step(where, lon, recv, weight, post, table, flip, chans, cotangent_pass):
     places = recv.shape[0]
     m_count, degrees, nlat = table.shape
     height = 4 * m_count + 2 * m_count // 3
     return pl.pallas_call(
         functools.partial(filter_kernel, m_count, chans, cotangent_pass),
         out_shape=jax.ShapeDtypeStruct((places, height, 128), bf16),
-        in_specs=[pl.BlockSpec(memory_space=pltpu.SMEM)] + vmem(3) + hbm(2),
+        in_specs=[pl.BlockSpec(memory_space=pltpu.SMEM)] * 2 + vmem(3) + hbm(2),
         out_specs=vmem(1)[0],
         scratch_shapes=[
             *filter_scratch(places, height, degrees),
@@ -388,7 +402,7 @@
         compiler_params=params(60),
         cost_estimate=cost(8e9, 9e6),
         name="filter_step",
-    )(where, recv, weight, post, table, flip)
+    )(where, lon, recv, weight, post, table, flip)
 
 
 def synthesis_kernel(which, recv_ref, tab_ref, out_ref):
@@ -476,13 +490,13 @@
         out_shape=jax.ShapeDtypeStruct((sectors, height, cols), bf16),
         in_specs=[pl.BlockSpec(memory_space=pltpu.SMEM)] + vmem(2),
         out_specs=vmem(1)[0],
-        compiler_params=params(),
+        compiler_params=params(60),
         cost_estimate=cost(1e8, 2e6),
         name="start",
     )(lon_index[None], cot, field)
 
 
-def weights_kernel(rim, adjoint, idx_ref, stencil_ref, mix_ref, band, blend):
+def weights_kernel(rim, nlat, adjoint, idx_ref, stencil_ref, mix_ref, band, blend):
     groups, width = mix_ref.shape[0], mix_ref.shape[2]
     taps = mix_ref.shape[1] // width
     k_pad = 16
@@ -493,7 +507,7 @@
     tap = lax.broadcasted_iota(jnp.int32, (span * span, 128), 0)
     slot = lax.broadcasted_iota(jnp.int32, (span * span, 128), 1)
     source = idx_ref[0] * rows - rim + slot % ext
-    inside = (source >= 0) & (source < idx_ref[1]) & (slot < span * ext)
+    inside = (source >= 0) & (source < nlat) & (slot < span * ext)
     for i in range(rows):
         total = jnp.zeros((k_pad, 128), f32)
         for line in range(i, i + span) if adjoint else (i + rim,):
@@ -516,10 +530,10 @@
         blend[g] = dot(mix_ref[g], place, TN).astype(bf16)
 
 
-def conv_weights(where, stencil, mix, rim, adjoint):
+def conv_weights(where, stencil, mix, rim, nlat, adjoint):
     groups, _, width = mix.shape
     return pl.pallas_call(
-        functools.partial(weights_kernel, rim, adjoint),
+        functools.partial(weights_kernel, rim, nlat, adjoint),
         out_shape=(
             jax.ShapeDtypeStruct((stencil.shape[0] - 32 * rim, 128), bf16),
             jax.ShapeDtypeStruct((groups, width, width * 16), bf16),
@@ -580,11 +594,8 @@
             if s == 0:
                 pieces.append(x)
                 continue
-            inside = (lane + s >= 0) & (lane + s < cols)
-            shift = (-s) % cols
-            pieces.append(
-                jnp.where(inside, pltpu.roll(x, shift, 1), pltpu.roll(h, shift, 1))
-            )
+            beyond = lane < s if s > 0 else lane >= cols + s
+            pieces.append(pltpu.roll(jnp.where(beyond, h, x), (-s) % cols, 1))
         return jnp.concatenate([p.astype(bf16) for p in pieces], axis=0)
 
     for g in range(groups):
@@ -606,10 +617,10 @@
             emit(g, i + 1, out[:, cols:])
 
 
-def forward_kernel(rim, *refs):
+def forward_kernel(rim, nlat, *refs):
     where_ref, stencil_ref, mix_ref = refs[:3]
     act_ref, slope_ref, xs, hs, resp, band, blend = refs[8:]
-    weights_kernel(rim, False, where_ref, stencil_ref, mix_ref, band, blend)
+    weights_kernel(rim, nlat, False, where_ref, stencil_ref, mix_ref, band, blend)
     width = blend.shape[1]
     chans = act_ref.shape[2]
     root = math.sqrt(2.0 / math.pi)
@@ -636,7 +647,7 @@
         at = slice(g * width, (g + 1) * width)
         grad_ref[i, at, :] = (cot_ref[i, at, :].astype(f32) + v).astype(bf16)
 
-    conv_body(*refs[:7], *refs[9:], emit)
+    conv_body(*refs[:7], *refs[9:12], emit)
 
 
 def conv_scratch(rim, x, width):
@@ -649,10 +660,10 @@
     ]
 
 
-def conv_forward(where, stencil, mix, rim, x, halo, shape):
+def conv_forward(where, stencil, mix, rim, nlat, x, halo, shape):
     groups, _, width = mix.shape
     return pl.pallas_call(
-        functools.partial(forward_kernel, rim),
+        functools.partial(forward_kernel, rim, nlat),
         out_shape=(jax.ShapeDtypeStruct(shape, bf16), jax.ShapeDtypeStruct(x.shape, f32)),
         in_specs=[pl.BlockSpec(memory_space=pltpu.SMEM)] + vmem(7),
         out_specs=tuple(vmem(2)),
@@ -769,35 +780,39 @@
     stencil = stencil_rows(weights_ext)
     mix = mix_weight.reshape(groups, k_count * width, width)
     mix_adj = jnp.transpose(mix_weight, (0, 1, 3, 2)).reshape(groups, k_count * width, width)
-    where = jnp.stack([lat_index, jnp.int32(nlat)]).astype(jnp.int32)
+    where = lat_index[None]
     tab = lon_table(degrees, nlon, lat_count)
-    legendre = legendre_inputs(lat_index, degrees, lat_count, rows, m_count)
+    legendre = legendre_inputs(degrees, lat_count, rows)
     theta = math.pi * (np.arange(nlat) + 0.5) / nlat
     quad = 2.0 * math.pi * math.pi / nlat * np.sin(theta) / nlon
     quad_rows = np.repeat(quad.reshape(lat_count, rows), chans, axis=1).astype(np.float32)
-    quad_lanes = lax.dynamic_slice_in_dim(jnp.asarray(quad_rows), lat_index, 1, 0)
     post = np.broadcast_to(quad.reshape(lat_count, rows).T.reshape(nlat, 1), (nlat, 128))
     post = jnp.asarray(post.astype(np.float32))
-    here = jnp.stack([lat_index, lon_index]).astype(jnp.int32)
+    here = lat_index[None]
     shape = (lon_count, rows, chans, cols)
 
-    send_1 = analysis(circ_c, body, tab, quad_lanes, lat_count, True)
+    table = legendre_table(here, legendre, m_count, degrees, nlat)
+    circ_c, table = lax.optimization_barrier((circ_c, table))
+    send_1 = analysis(circ_c, body, tab, lat_count)
     halo = lat_rims(field, left, right, rim)
     send_1, halo = lax.optimization_barrier((send_1, halo))
     recv_1 = lax.all_to_all(send_1, "lat", 0, 0, tiled=True)
-    act, slope = conv_forward(where, stencil, mix, rim, field, halo, shape)
-    act, after = lax.optimization_barrier((act, here))
-    table, flip = legendre_tables(after, legendre, m_count, degrees, nlat)
+    act, slope = conv_forward(where, stencil, mix, rim, nlat, field, halo, shape)
+    act, table, filter_weight, later = lax.optimization_barrier(
+        (act, table, filter_weight, lat_index)
+    )
+    quad_lanes = lax.dynamic_slice_in_dim(jnp.asarray(quad_rows), later, 1, 0)
+    flip = flipped_table(table)
     recv_1, act, table, flip = lax.optimization_barrier((recv_1, act, table, flip))
     circ_f = lax.all_to_all(act, "lon", 0, 0, tiled=True)
-    filtered_c = filter_step(here, recv_1, filter_weight, post, table, flip, chans, True)
-    send_2 = analysis(circ_f, body, tab, quad_lanes, lat_count, False, (filtered_c,))
+    filtered_c = filter_step(here, lon_index[None], recv_1, filter_weight, post, table, flip, chans, True)
+    send_2 = analysis(circ_f, body, tab, lat_count, quad_lanes, filtered_c)
     recv_2 = lax.all_to_all(send_2, "lat", 0, 0, tiled=True)
     stencil, send_2 = lax.optimization_barrier((stencil, send_2))
-    weights_adj = conv_weights(where, stencil, mix_adj, rim, True)
+    weights_adj = conv_weights(where, stencil, mix_adj, rim, nlat, True)
     recv_2, weights_adj = lax.optimization_barrier((recv_2, weights_adj))
     cot_act = lax.all_to_all(synthesis(recv_2, tab, 1, shape), "lon", 0, 0, tiled=True)
-    filtered_f = filter_step(here, recv_2, filter_weight, post, table, flip, chans, False)
+    filtered_f = filter_step(here, lon_index[None], recv_2, filter_weight, post, table, flip, chans, False)
     recv_3 = lax.all_to_all(filtered_f, "lat", 0, 0, tiled=True)
     branch = lax.all_to_all(synthesis(recv_3, tab, 0, shape), "lon", 0, 0, tiled=True)
 

time: 179 us -> 173 us (0.966)
  local copies, waits for them, and re-layouts: 20.4 us -> 15.3 us
  other arithmetic: 6.21 us -> 4.18 us
    unnamed x56 -> x47, local copies, waits for them, and re-layouts: 16.4 us -> 11.4 us
    optimization_barrier x0 -> x1, local copies, waits for them, and re-layouts: none -> 1.87 us  [local(): lax.optimization_barrier((act, table, filter_weight, lat_index))]
    pallas_call x5 -> x6, Pallas kernels: 26.2 us -> 26.2 us  [the longest x1 10.1 us: conv_forward(): pl.pallas_call(functools.partial(forward_kernel, rim, nlat), out_shape=(j...]
  transfers between devices with their start and end apart: 13 -> 13, of which waited for: 6 -> 6; matrix products, arithmetic and copies ran while one was open for 6% -> 4% of each run, Pallas kernels for 32% -> 33%
where the time goes in v3:
time: 173 us; the launch traced here: 172 us
  Pallas kernels  61.6 us (36%)
  starting transfers between devices  59 us (34%)
  waiting for transfers between devices  30.7 us (18%)
  local copies, waits for them, and re-layouts  15.3 us (9%)
  other arithmetic  4.18 us (2%)
    all_to_all x1, waiting for transfers between devices, local(): recv_2 = lax.all_to_all(send_2, 'lat', 0, 0, tiled=True)  23 us
    pallas_call x2, Pallas kernels, filter_step(): pl.pallas_call(functools.partial(filter_kernel, m_count, chans, cotangent...  18.9 us
    ppermute x2, starting transfers between devices, lat_rims(): high = lax.ppermute(high, 'lat', shifted('lat', -1))  11.7 us
    unnamed x47, local copies, waits for them, and re-layouts  11.4 us
    pallas_call x1, Pallas kernels, conv_forward(): pl.pallas_call(functools.partial(forward_kernel, rim, nlat), out_shape=(j...  10.1 us
    all_to_all x1, starting transfers between devices, local(): recv_2 = lax.all_to_all(send_2, 'lat', 0, 0, tiled=True)  9.65 us
    pallas_call x1, Pallas kernels, conv_adjoint(): pl.pallas_call(adjoint_kernel, out_shape=jax.ShapeDtypeStruct(x.shape, bf...  9.29 us
    pallas_call x1, Pallas kernels, legendre_table(): pl.pallas_call(functools.partial(legendre_kernel, m_count), out_shape=jax...  7.8 us
  transfers between devices with their start and end apart: 13, of which 6 were waited for; matrix products, arithmetic and copies ran while one was open for 4% of the time, Pallas kernels for 33%

profile of v3, /device:TPU:2, one launch (start us, length us, event | category | flops | bytes accessed | tf_op | source)
XLA Modules:
  0.0 171.8 jit_solution(5637357274002918736)
XLA Ops:
  0.6 2.5 %start.1 = bf16[8,336,128]{2,1,0:T(8,128)(2,1)} custom-call(s32[1]{0:T(128)} %bitcast.1.idx_ref.lon_ref, bf16[12,192,128]{2,1,0:T(8,128)(2,1)} %bitcast.34, bf16[12,192,128]{2,1,0:T(8,128)(2,1)} %bitcast.32), custom_call_target="tpu_custom_call" | custom-call | flops 100000000 | bytes 2000000 | tf_op jit(solution)/shard_map/start/pallas_call | solution.py:488
  3.2 6.1 %all-to-all-start = ((bf16[8,336,128]{2,1,0:T(8,128)(2,1)}), bf16[8,336,128]{2,1,0:T(8,128)(2,1)S(1)}, u32[]{:S(2)}, u32[]{:S(2)}) async-start(bf16[8,336,128]{2,1,0:T(8,128)(2,1)} %start.1), calls=%async_computation | async-start | bytes 1376256 | tf_op jit(solution)/shard_map/all_to_all | solution.py:766
  9.9 1.6 fusion.3
  11.5 1.7 lon_table.1.refs_1_.tab_ref
  13.2 7.8 %legendre_table.1.table_in = bf16[12,384,384]{2,1,0:T(8,128)(2,1)} custom-call(s32[1]{0:T(128)} %bitcast.idx_ref.refs_0_, f32[384]{0:T(512)} %constant.90.clone.rise_ref, f32[384]{0:T(512)} %constant.91.clone.fall_ref, f32[384]{0:T(512)} %constant.92.clone.norm_ref, f32[1,384]{1,0:T(1,128)} %constant.93.clone.cos_ref, f32[1,384]{1,0:T(1,128)} %constant.94.clone.logsin_ref), custom_call_target="tpu_custom_call" | custom-call | flops 2000000000 | bytes 4000000 | tf_op jit(solution)/shard_map/legendre_table/pallas_call | solution.py:306
  21.3 6.4 %collective-permute-start.1 = (bf16[400,128]{1,0:T(8,128)(2,1)S(1)}, bf16[400,128]{1,0:T(8,128)(2,1)S(1)}, u32[]{:S(2)}, u32[]{:S(2)}) collective-permute-start(bf16[400,128]{1,0:T(8,128)(2,1)S(1)} %pad_maximum_fusion.1), channel_id=1, source_target_pairs={{0,248},{8,0},{16,8},{24,16},{32,24},{40,32},{48,40},{56,48},{64,5... | collective-permute-start | bytes 307208 | tf_op jit(solution)/shard_map/ppermute | solution.py:704
  27.6 1.8 %analysis.2 = bf16[32,56,128]{2,1,0:T(8,128)(2,1)} custom-call(bf16[8,336,128]{2,1,0:T(8,128)(2,1)S(1)} %all-to-all-done.refs_0_, bf16[768,1024]{1,0:T(8,128)(2,1)S(1)} %lon_table.1.refs_1_.tab_ref), custom_call_target="tpu_custom_call" | custom-call | flops 452984832 | bytes 3000000 | tf_op jit(solution)/shard_map/analysis/pallas_call | solution.py:202
  30.5 7.6 %all-to-all-start.1 = ((bf16[32,56,128]{2,1,0:T(8,128)(2,1)}), bf16[32,56,128]{2,1,0:T(8,128)(2,1)S(1)}, u32[]{:S(2)}, u32[]{:S(2)}) async-start(bf16[32,56,128]{2,1,0:T(8,128)(2,1)} %analysis.2), calls=%async_computation.1 | async-start | bytes 917504 | tf_op jit(solution)/shard_map/all_to_all | solution.py:799
  39.1 10.1 %conv_forward.1 = (bf16[8,12,24,128]{3,2,1,0:T(8,128)(2,1)}, f32[12,192,128]{2,1,0:T(8,128)S(1)}) custom-call(s32[1]{0:T(128)} %bitcast.idx_ref.refs_0_, bf16[256,25]{1,0:T(8,128)(2,1)S(1)} %bitcast.39, bf16[4,432,48]{2,1,0:T(8,128)(2,1)S(1)} %bitcast.36, bf16[12,192,128]{2,1,0:T(8,128)(2,1)S(1)} %bitcast.33, ...), custom_call_target="tpu_custom_call" | custom-call | flops 12000000000 | bytes 4000000 | tf_op jit(solution)/shard_map/conv_forward/pallas_call | solution.py:665
  50.3 1.9 %copy.23.weight_ref = f32[384,192]{1,0:T(8,128)} copy(f32[384,192]{0,1:T(8,128)} %param.20) | data formatting | bytes 589824 | tf_op jit(solution)/shard_map/optimization_barrier | solution.py:801
  52.2 3.6 %flip_table.1.flip_in = bf16[12,384,384]{2,1,0:T(8,128)(2,1)} custom-call(bf16[12,384,384]{2,1,0:T(8,128)(2,1)} %legendre_table.1.table_in), custom_call_target="tpu_custom_call" | custom-call | flops 100000000 | bytes 7000000 | tf_op jit(solution)/shard_map/flip_table/pallas_call | solution.py:340
  57.4 5.7 %all-to-all-start.2 = ((bf16[8,12,24,128]{3,2,1,0:T(8,128)(2,1)}), bf16[8,12,24,128]{3,2,1,0:T(8,128)(2,1)S(1)}, u32[]{:S(2)}, u32[]{:S(2)}) async-start(bf16[8,12,24,128]{3,2,1,0:T(8,128)(2,1)} %get-tuple-element.38), calls=%async_computation.2 | async-start | bytes 1179648 | tf_op jit(solution)/shard_map/all_to_all | solution.py:807
  63.1 9.4 %filter_step.2.refs_3_ = bf16[32,56,128]{2,1,0:T(8,128)(2,1)} custom-call(s32[1]{0:T(128)} %bitcast.idx_ref.refs_0_, s32[1]{0:T(128)} %bitcast.1.idx_ref.lon_ref, bf16[32,56,128]{2,1,0:T(8,128)(2,1)} %copy-done.19, f32[384,192]{1,0:T(8,128)} %copy.23.weight_ref, f32[384,128]{1,0:T(8,128)} %constant.95.clone.post_ref, ...), custom_call_target="tpu_custom_call" | custom-call | flops 8000000000 | bytes 9000000 | tf_op jit(solution)/shard_map/filter_step/pallas_call | solution.py:393
  73.6 2.0 %analysis.3 = bf16[32,112,128]{2,1,0:T(8,128)(2,1)} custom-call(bf16[8,12,24,128]{3,2,1,0:T(8,128)(2,1)S(1)} %all-to-all-done.2.refs_0_, bf16[768,1024]{1,0:T(8,128)(2,1)S(1)} %lon_table.1.refs_1_.tab_ref, f32[1,288]{1,0:T(1,128)S(1)} %constant_dynamic-slice_fusion.4.refs_2_, bf16[32,56,128]{2,1,0:T(8,128)(2,1)S(1)} %copy-done.6), custom_call_target="tpu_custom_call" | custom-call | flops 452984832 | bytes 3000000 | tf_op jit(solution)/shard_map/analysis/pallas_call | solution.py:202
  75.6 9.6 %all-to-all-start.3 = ((bf16[32,112,128]{2,1,0:T(8,128)(2,1)}), bf16[32,112,128]{2,1,0:T(8,128)(2,1)S(1)}, u32[]{:S(2)}, u32[]{:S(2)}) async-start(bf16[32,112,128]{2,1,0:T(8,128)(2,1)} %analysis.3), calls=%async_computation.3 | async-start | bytes 1835008 | tf_op jit(solution)/shard_map/all_to_all | solution.py:810
  89.7 23.0 %all-to-all-done.3.recv_ref = bf16[32,112,128]{2,1,0:T(8,128)(2,1)S(1)} async-done(((bf16[32,112,128]{2,1,0:T(8,128)(2,1)}), bf16[32,112,128]{2,1,0:T(8,128)(2,1)S(1)}, u32[]{:S(2)}, u32[]{:S(2)}) %all-to-all-start.3) | async-done | bytes 917536 | tf_op jit(solution)/shard_map/all_to_all | solution.py:810
  114.4 5.5 %all-to-all-start.6 = ((bf16[8,12,24,128]{3,2,1,0:T(8,128)(2,1)}), bf16[8,12,24,128]{3,2,1,0:T(8,128)(2,1)S(1)}, u32[]{:S(2)}, u32[]{:S(2)}) async-start(bf16[8,12,24,128]{3,2,1,0:T(8,128)(2,1)} %copy-done.2), calls=%async_computation.6 | async-start | bytes 1179648 | tf_op jit(solution)/shard_map/all_to_all | solution.py:814
  119.9 9.5 %filter_step.3 = bf16[32,56,128]{2,1,0:T(8,128)(2,1)} custom-call(s32[1]{0:T(128)} %bitcast.idx_ref.refs_0_, s32[1]{0:T(128)} %bitcast.1.idx_ref.lon_ref, bf16[32,112,128]{2,1,0:T(8,128)(2,1)} %copy-done, f32[384,192]{1,0:T(8,128)} %copy.23.weight_ref, f32[384,128]{1,0:T(8,128)} %constant.95.clone.post_ref, bf16[12,384,384]{2,1,0:T(8,128)(2,1)} %legendre_table.1.table_in, ...), custom_call_target="tpu_custom_call" | custom-call | flops 8000000000 | bytes 9000000 | tf_op jit(solution)/shard_map/filter_step/pallas_call | solution.py:393
  129.4 3.9 %all-to-all-start.4 = ((bf16[32,56,128]{2,1,0:T(8,128)(2,1)}), bf16[32,56,128]{2,1,0:T(8,128)(2,1)S(1)}, u32[]{:S(2)}, u32[]{:S(2)}) async-start(bf16[32,56,128]{2,1,0:T(8,128)(2,1)} %filter_step.3), calls=%async_computation.4 | async-start | bytes 917504 | tf_op jit(solution)/shard_map/all_to_all | solution.py:816
  135.1 3.1 %collective-permute-start.3 = (bf16[40,128]{1,0:T(8,128)(2,1)S(1)}, bf16[40,128]{1,0:T(8,128)(2,1)S(1)}, u32[]{:S(2)}, u32[]{:S(2)}) collective-permute-start(bf16[40,128]{1,0:T(8,128)(2,1)S(1)} %get-tuple-element.51), channel_id=1, source_target_pairs={{0,7},{1,0},{2,1},{3,2},{4,3},{5,4},{6,5},{7,6},{8,15},{9,8},{10,9... | collective-permute-start | bytes 30728 | tf_op jit(solution)/shard_map/ppermute | solution.py:821
  139.6 4.4 %collective-permute-done.2.refs_3_ = bf16[40,128]{1,0:T(8,128)(2,1)S(1)} collective-permute-done((bf16[40,128]{1,0:T(8,128)(2,1)S(1)}, bf16[40,128]{1,0:T(8,128)(2,1)S(1)}, u32[]{:S(2)}, u32[]{:S(2)}) %collective-permute-start.2) | collective-permute-done | bytes 10272 | tf_op jit(solution)/shard_map/ppermute | solution.py:820
  145.3 5.4 %collective-permute-start.5 = (bf16[400,128]{1,0:T(8,128)(2,1)}, bf16[400,128]{1,0:T(8,128)(2,1)S(1)}, u32[]{:S(2)}, u32[]{:S(2)}) collective-permute-start(bf16[400,128]{1,0:T(8,128)(2,1)} %pad_maximum_fusion.3), channel_id=1, source_target_pairs={{0,248},{8,0},{16,8},{24,16},{32,24},{40,32},{48,40},{56,48},{64,5... | collective-permute-start | bytes 307208 | tf_op jit(solution)/shard_map/ppermute | solution.py:704
  153.6 5.7 %all-to-all-start.5 = ((bf16[8,12,24,128]{3,2,1,0:T(8,128)(2,1)}), bf16[8,12,24,128]{3,2,1,0:T(8,128)(2,1)S(1)}, u32[]{:S(2)}, u32[]{:S(2)}) async-start(bf16[8,12,24,128]{3,2,1,0:T(8,128)(2,1)} %synthesis.2), calls=%async_computation.5 | async-start | bytes 1179648 | tf_op jit(solution)/shard_map/all_to_all | solution.py:817
  161.4 9.3 %conv_adjoint.1 = bf16[12,192,128]{2,1,0:T(8,128)(2,1)} custom-call(bf16[12,192,128]{2,1,0:T(8,128)(2,1)S(1)} %copy-done.11, bf16[400,128]{1,0:T(8,128)(2,1)S(1)} %collective-permute-done.4.refs_1_, bf16[400,128]{1,0:T(8,128)(2,1)S(1)} %collective-permute-done.5.refs_2_, bf16[40,128]{1,0:T(8,128)(2,1)S(1)} %collective-permute-done.2.refs_3_, ...), custom_call_target="tpu_custom_call" | custom-call | flops 12000000000 | bytes 4000000 | tf_op jit(solution)/shard_map/conv_adjoint/pallas_call | solution.py:682
  (88 shorter events, 23.3 us)
Async XLA Ops:
  3.2 6.1 %copy-start.20 = (s32[384,5]{0,1:T(8,128)S(1)}, s32[384,5]{0,1:T(8,128)}, u32[]{:S(2)}) copy-start(s32[384,5]{0,1:T(8,128)} %param.18) | copy-start | bytes 23044
  3.2 6.3 %copy-start.18 = (f32[384,5,5,9]{0,2,3,1:T(8,128)S(1)}, f32[384,5,5,9]{0,2,3,1:T(8,128)}, u32[]{:S(2)}) copy-start(f32[384,5,5,9]{0,2,3,1:T(8,128)} %param.17) | copy-start | bytes 1036804
  3.2 6.7 %copy-start.21 = (s32[768]{0:T(1024)S(1)}, s32[768]{0:T(1024)}, u32[]{:S(2)}) copy-start(s32[768]{0:T(1024)} %constant.88.clone) | copy-start | bytes 9220
  3.2 6.7 %copy-start.22 = (s32[768]{0:T(1024)S(1)}, s32[768]{0:T(1024)}, u32[]{:S(2)}) copy-start(s32[768]{0:T(1024)} %constant.87.clone) | copy-start | bytes 9220
  3.2 17.9 %all-to-all-start = ((bf16[8,336,128]{2,1,0:T(8,128)(2,1)}), bf16[8,336,128]{2,1,0:T(8,128)(2,1)S(1)}, u32[]{:S(2)}, u32[]{:S(2)}) async-start(bf16[8,336,128]{2,1,0:T(8,128)(2,1)} %start.1), calls=%async_computation | async-start | bytes 1376256 | tf_op jit(solution)/shard_map/all_to_all | solution.py:766
  9.2 2.3 %copy-start.9 = (f32[768,16]{1,0:T(8,128)S(1)}, f32[768,16]{1,0:T(8,128)}, u32[]{:S(2)}) copy-start(f32[768,16]{1,0:T(8,128)} %constant.89.clone.far_ref) | copy-start | bytes 147460
  9.9 28.3 %copy-start.12 = (bf16[16,16,25]{2,1,0:T(8,128)(2,1)}, bf16[16,16,25]{2,1,0:T(8,128)(2,1)S(1)}, u32[]{:S(2)}) copy-start(bf16[16,16,25]{2,1,0:T(8,128)(2,1)S(1)} %pad.15.clone) | copy-start | bytes 38404
  13.2 7.8 %copy-start.1 = (bf16[1,12,192,128]{3,2,1,0:T(8,128)(2,1)S(1)}, bf16[1,12,192,128]{3,2,1,0:T(8,128)(2,1)}, u32[]{:S(2)}) copy-start(bf16[1,12,192,128]{3,2,1,0:T(8,128)(2,1)} %param.16) | copy-start | bytes 1769476
  21.1 8.7 %collective-permute-start = (bf16[400,128]{1,0:T(8,128)(2,1)S(1)}, bf16[400,128]{1,0:T(8,128)(2,1)S(1)}, u32[]{:S(2)}, u32[]{:S(2)}) collective-permute-start(bf16[400,128]{1,0:T(8,128)(2,1)S(1)} %pad_maximum_fusion), channel_id=1, source_target_pairs={{0,8},{8,16},{16,24},{24,32},{32,40},{40,48},{48,56},{56,64},{64,7... | collective-permute-start | bytes 307208 | tf_op jit(solution)/shard_map/ppermute | solution.py:703
  21.3 16.9 %copy-start.7 = (bf16[4,9,48,48]{3,2,1,0:T(8,128)(2,1)S(1)}, bf16[4,9,48,48]{3,2,1,0:T(8,128)(2,1)}, u32[]{:S(2)}) copy-start(bf16[4,9,48,48]{3,2,1,0:T(8,128)(2,1)} %param.19) | copy-start | bytes 497668
  21.3 8.6 %collective-permute-start.1 = (bf16[400,128]{1,0:T(8,128)(2,1)S(1)}, bf16[400,128]{1,0:T(8,128)(2,1)S(1)}, u32[]{:S(2)}, u32[]{:S(2)}) collective-permute-start(bf16[400,128]{1,0:T(8,128)(2,1)S(1)} %pad_maximum_fusion.1), channel_id=1, source_target_pairs={{0,248},{8,0},{16,8},{24,16},{32,24},{40,32},{48,40},{56,48},{64,5... | collective-permute-start | bytes 307208 | tf_op jit(solution)/shard_map/ppermute | solution.py:704
  30.5 26.1 %all-to-all-start.1 = ((bf16[32,56,128]{2,1,0:T(8,128)(2,1)}), bf16[32,56,128]{2,1,0:T(8,128)(2,1)S(1)}, u32[]{:S(2)}, u32[]{:S(2)}) async-start(bf16[32,56,128]{2,1,0:T(8,128)(2,1)} %analysis.2), calls=%async_computation.1 | async-start | bytes 917504 | tf_op jit(solution)/shard_map/all_to_all | solution.py:799
  57.4 15.1 %all-to-all-start.2 = ((bf16[8,12,24,128]{3,2,1,0:T(8,128)(2,1)}), bf16[8,12,24,128]{3,2,1,0:T(8,128)(2,1)S(1)}, u32[]{:S(2)}, u32[]{:S(2)}) async-start(bf16[8,12,24,128]{3,2,1,0:T(8,128)(2,1)} %get-tuple-element.38), calls=%async_computation.2 | async-start | bytes 1179648 | tf_op jit(solution)/shard_map/all_to_all | solution.py:807
  75.6 37.1 %all-to-all-start.3 = ((bf16[32,112,128]{2,1,0:T(8,128)(2,1)}), bf16[32,112,128]{2,1,0:T(8,128)(2,1)S(1)}, u32[]{:S(2)}, u32[]{:S(2)}) async-start(bf16[32,112,128]{2,1,0:T(8,128)(2,1)} %analysis.3), calls=%async_computation.3 | async-start | bytes 1835008 | tf_op jit(solution)/shard_map/all_to_all | solution.py:810
  114.4 15.0 %all-to-all-start.6 = ((bf16[8,12,24,128]{3,2,1,0:T(8,128)(2,1)}), bf16[8,12,24,128]{3,2,1,0:T(8,128)(2,1)S(1)}, u32[]{:S(2)}, u32[]{:S(2)}) async-start(bf16[8,12,24,128]{3,2,1,0:T(8,128)(2,1)} %copy-done.2), calls=%async_computation.6 | async-start | bytes 1179648 | tf_op jit(solution)/shard_map/all_to_all | solution.py:814
  129.4 22.6 %all-to-all-start.4 = ((bf16[32,56,128]{2,1,0:T(8,128)(2,1)}), bf16[32,56,128]{2,1,0:T(8,128)(2,1)S(1)}, u32[]{:S(2)}, u32[]{:S(2)}) async-start(bf16[32,56,128]{2,1,0:T(8,128)(2,1)} %filter_step.3), calls=%async_computation.4 | async-start | bytes 917504 | tf_op jit(solution)/shard_map/all_to_all | solution.py:816
  133.3 1.3 copy-start.4
  135.1 10.2 %copy-start.10 = (bf16[12,192,128]{2,1,0:T(8,128)(2,1)}, bf16[12,192,128]{2,1,0:T(8,128)(2,1)S(1)}, u32[]{:S(2)}) copy-start(bf16[12,192,128]{2,1,0:T(8,128)(2,1)S(1)} %get-tuple-element.49.refs_0_) | copy-start | bytes 1769476
  135.1 4.5 %collective-permute-start.3 = (bf16[40,128]{1,0:T(8,128)(2,1)S(1)}, bf16[40,128]{1,0:T(8,128)(2,1)S(1)}, u32[]{:S(2)}, u32[]{:S(2)}) collective-permute-start(bf16[40,128]{1,0:T(8,128)(2,1)S(1)} %get-tuple-element.51), channel_id=1, source_target_pairs={{0,7},{1,0},{2,1},{3,2},{4,3},{5,4},{6,5},{7,6},{8,15},{9,8},{10,9... | collective-permute-start | bytes 30728 | tf_op jit(solution)/shard_map/ppermute | solution.py:821
  138.2 5.8 %collective-permute-start.2 = (bf16[40,128]{1,0:T(8,128)(2,1)S(1)}, bf16[40,128]{1,0:T(8,128)(2,1)S(1)}, u32[]{:S(2)}, u32[]{:S(2)}) collective-permute-start(bf16[40,128]{1,0:T(8,128)(2,1)S(1)} %get-tuple-element.50), channel_id=1, source_target_pairs={{0,1},{1,2},{2,3},{3,4},{4,5},{5,6},{6,7},{7,0},{8,9},{9,10},{10,1... | collective-permute-start | bytes 30728 | tf_op jit(solution)/shard_map/ppermute | solution.py:820
  144.7 14.7 %collective-permute-start.4 = (bf16[400,128]{1,0:T(8,128)(2,1)}, bf16[400,128]{1,0:T(8,128)(2,1)S(1)}, u32[]{:S(2)}, u32[]{:S(2)}) collective-permute-start(bf16[400,128]{1,0:T(8,128)(2,1)} %pad_maximum_fusion.2), channel_id=1, source_target_pairs={{0,8},{8,16},{16,24},{24,32},{32,40},{40,48},{48,56},{56,64},{64,7... | collective-permute-start | bytes 307208 | tf_op jit(solution)/shard_map/ppermute | solution.py:703
  145.3 14.0 %copy-start.5 = (bf16[1,12,192,128]{3,2,1,0:T(8,128)(2,1)S(1)}, bf16[1,12,192,128]{3,2,1,0:T(8,128)(2,1)}, u32[]{:S(2)}) copy-start(bf16[1,12,192,128]{3,2,1,0:T(8,128)(2,1)} %param.21) | copy-start | bytes 1769476
  145.3 14.0 %collective-permute-start.5 = (bf16[400,128]{1,0:T(8,128)(2,1)}, bf16[400,128]{1,0:T(8,128)(2,1)S(1)}, u32[]{:S(2)}, u32[]{:S(2)}) collective-permute-start(bf16[400,128]{1,0:T(8,128)(2,1)} %pad_maximum_fusion.3), channel_id=1, source_target_pairs={{0,248},{8,0},{16,8},{24,16},{32,24},{40,32},{48,40},{56,48},{64,5... | collective-permute-start | bytes 307208 | tf_op jit(solution)/shard_map/ppermute | solution.py:704
  153.6 17.1 %all-to-all-start.5 = ((bf16[8,12,24,128]{3,2,1,0:T(8,128)(2,1)}), bf16[8,12,24,128]{3,2,1,0:T(8,128)(2,1)S(1)}, u32[]{:S(2)}, u32[]{:S(2)}) async-start(bf16[8,12,24,128]{3,2,1,0:T(8,128)(2,1)} %synthesis.2), calls=%async_computation.5 | async-start | bytes 1179648 | tf_op jit(solution)/shard_map/all_to_all | solution.py:817
  (12 other events, 10.8 us)

commit v4 on v3

--- a/solution.py
+++ b/solution.py
@@ -229,13 +229,10 @@
 
     lax.fori_loop(0, places, load, 0, unroll=4)
     give[2 * k_count * places :, :] = jnp.zeros((third * places, 128), f32)
-    weight = weight_ref[...]
-    room = 256 - weight.shape[1]
-    weight = jnp.concatenate([weight, jnp.zeros((weight.shape[0], room), f32)], axis=1)
-    weight = pltpu.roll(weight, lax.rem(256 - lon_ref[0] * chans, 256), 1)[:, 0:128]
-    place = lax.broadcasted_iota(jnp.int32, weight.shape, 1)
-    weight = jnp.where(place < chans, weight, 0.0)
-    gain[...] = weight + pltpu.roll(weight, chans, 1)
+    at = pl.ds(pl.multiple_of(lon_ref[0] * chans, 8), chans)
+    weight = weight_ref[at, :]
+    room = jnp.zeros((128 - 2 * chans, weight.shape[1]), f32)
+    gain[...] = jnp.transpose(jnp.concatenate([weight, weight, room], axis=0))
 
     def one(mm):
         blocks = []
@@ -390,6 +387,7 @@
     places = recv.shape[0]
     m_count, degrees, nlat = table.shape
     height = 4 * m_count + 2 * m_count // 3
+    weight = jnp.transpose(weight)
     return pl.pallas_call(
         functools.partial(filter_kernel, m_count, chans, cotangent_pass),
         out_shape=jax.ShapeDtypeStruct((places, height, 128), bf16),

time: 173 us -> 171 us (0.988)
  waiting for transfers between devices: 30.7 us -> 32.6 us
  local copies, waits for them, and re-layouts: 15.3 us -> 13.5 us
  starting transfers between devices: 59 us -> 57.2 us
    all_to_all x1, waiting for transfers between devices: 0.22 us -> 2.09 us  [local(): recv_1 = lax.all_to_all(send_1, 'lat', 0, 0, tiled=True)]
    optimization_barrier x1 -> x0, local copies, waits for them, and re-layouts: 1.87 us -> none  [local(): lax.optimization_barrier((act, table, filter_weight, lat_index))]
    all_to_all x1, starting transfers between devices: 9.65 us -> 7.81 us  [local(): recv_2 = lax.all_to_all(send_2, 'lat', 0, 0, tiled=True)]
  transfers between devices with their start and end apart: 13 -> 13, of which waited for: 6 -> 6; matrix products, arithmetic and copies ran while one was open for 4% -> 3% of each run, Pallas kernels for 33% -> 33%
where the time goes in v4:
time: 171 us; the launch traced here: 170 us
  Pallas kernels  61.5 us (36%)
  starting transfers between devices  57.2 us (33%)
  waiting for transfers between devices  32.6 us (19%)
  local copies, waits for them, and re-layouts  13.5 us (8%)
  other arithmetic  4.18 us (2%)
    all_to_all x1, waiting for transfers between devices, local(): recv_2 = lax.all_to_all(send_2, 'lat', 0, 0, tiled=True)  23 us
    pallas_call x2, Pallas kernels, filter_step(): pl.pallas_call(functools.partial(filter_kernel, m_count, chans, cotangent...  18.8 us
    ppermute x2, starting transfers between devices, lat_rims(): high = lax.ppermute(high, 'lat', shifted('lat', -1))  11.7 us
    unnamed x47, local copies, waits for them, and re-layouts  11.5 us
    pallas_call x1, Pallas kernels, conv_forward(): pl.pallas_call(functools.partial(forward_kernel, rim, nlat), out_shape=(j...  10.1 us
    pallas_call x1, Pallas kernels, conv_adjoint(): pl.pallas_call(adjoint_kernel, out_shape=jax.ShapeDtypeStruct(x.shape, bf...  9.3 us
    all_to_all x1, starting transfers between devices, local(): recv_2 = lax.all_to_all(send_2, 'lat', 0, 0, tiled=True)  7.81 us
    pallas_call x1, Pallas kernels, legendre_table(): pl.pallas_call(functools.partial(legendre_kernel, m_count), out_shape=jax...  7.8 us
  transfers between devices with their start and end apart: 13, of which 6 were waited for; matrix products, arithmetic and copies ran while one was open for 3% of the time, Pallas kernels for 33%

profile of v4, /device:TPU:2, one launch (start us, length us, event | category | flops | bytes accessed | tf_op | source)
XLA Modules:
  0.0 169.9 jit_solution(16347178000247349936)
XLA Ops:
  0.6 2.5 %start.1 = bf16[8,336,128]{2,1,0:T(8,128)(2,1)} custom-call(s32[1]{0:T(128)} %bitcast.1.idx_ref.lon_ref, bf16[12,192,128]{2,1,0:T(8,128)(2,1)} %bitcast.35, bf16[12,192,128]{2,1,0:T(8,128)(2,1)} %bitcast.33), custom_call_target="tpu_custom_call" | custom-call | flops 100000000 | bytes 2000000 | tf_op jit(solution)/shard_map/start/pallas_call | solution.py:486
  3.2 6.1 %all-to-all-start = ((bf16[8,336,128]{2,1,0:T(8,128)(2,1)}), bf16[8,336,128]{2,1,0:T(8,128)(2,1)S(1)}, u32[]{:S(2)}, u32[]{:S(2)}) async-start(bf16[8,336,128]{2,1,0:T(8,128)(2,1)} %start.1), calls=%async_computation | async-start | bytes 1376256 | tf_op jit(solution)/shard_map/all_to_all | solution.py:764
  9.9 1.6 fusion.3
  11.5 1.7 %lon_table.1.refs_1_.tab_ref = bf16[768,1024]{1,0:T(8,128)(2,1)S(1)} custom-call(f32[768,128]{1,0:T(8,128)S(1)} %get-tuple-element.69.near_cos_ref, f32[768,128]{1,0:T(8,128)S(1)} %get-tuple-element.68.near_sin_ref, f32[768,16]{1,0:T(8,128)S(1)} %copy-done.9), custom_call_target="tpu_custom_call" | custom-call | flops 100000000 | bytes 3000000 | tf_op jit(solution)/shard_map/lon_table/pallas_call | solution.py:155
  13.2 7.8 %legendre_table.1.table_in = bf16[12,384,384]{2,1,0:T(8,128)(2,1)} custom-call(s32[1]{0:T(128)} %bitcast.idx_ref.refs_0_, f32[384]{0:T(512)} %constant.90.clone.rise_ref, f32[384]{0:T(512)} %constant.91.clone.fall_ref, f32[384]{0:T(512)} %constant.92.clone.norm_ref, f32[1,384]{1,0:T(1,128)} %constant.93.clone.cos_ref, f32[1,384]{1,0:T(1,128)} %constant.94.clone.logsin_ref), custom_call_target="tpu_custom_call" | custom-call | flops 2000000000 | bytes 4000000 | tf_op jit(solution)/shard_map/legendre_table/pallas_call | solution.py:303
  21.3 6.4 %collective-permute-start.1 = (bf16[400,128]{1,0:T(8,128)(2,1)S(1)}, bf16[400,128]{1,0:T(8,128)(2,1)S(1)}, u32[]{:S(2)}, u32[]{:S(2)}) collective-permute-start(bf16[400,128]{1,0:T(8,128)(2,1)S(1)} %pad_maximum_fusion.1), channel_id=1, source_target_pairs={{0,248},{8,0},{16,8},{24,16},{32,24},{40,32},{48,40},{56,48},{64,5... | collective-permute-start | bytes 307208 | tf_op jit(solution)/shard_map/ppermute | solution.py:702
  27.6 1.8 %analysis.2 = bf16[32,56,128]{2,1,0:T(8,128)(2,1)} custom-call(bf16[8,336,128]{2,1,0:T(8,128)(2,1)S(1)} %all-to-all-done.refs_0_, bf16[768,1024]{1,0:T(8,128)(2,1)S(1)} %lon_table.1.refs_1_.tab_ref), custom_call_target="tpu_custom_call" | custom-call | flops 452984832 | bytes 3000000 | tf_op jit(solution)/shard_map/analysis/pallas_call | solution.py:202
  30.5 7.6 %all-to-all-start.1 = ((bf16[32,56,128]{2,1,0:T(8,128)(2,1)}), bf16[32,56,128]{2,1,0:T(8,128)(2,1)S(1)}, u32[]{:S(2)}, u32[]{:S(2)}) async-start(bf16[32,56,128]{2,1,0:T(8,128)(2,1)} %analysis.2), calls=%async_computation.1 | async-start | bytes 917504 | tf_op jit(solution)/shard_map/all_to_all | solution.py:797
  39.1 10.1 %conv_forward.1 = (bf16[8,12,24,128]{3,2,1,0:T(8,128)(2,1)}, f32[12,192,128]{2,1,0:T(8,128)S(1)}) custom-call(s32[1]{0:T(128)} %bitcast.idx_ref.refs_0_, bf16[256,25]{1,0:T(8,128)(2,1)S(1)} %bitcast.40, bf16[4,432,48]{2,1,0:T(8,128)(2,1)S(1)} %bitcast.37, bf16[12,192,128]{2,1,0:T(8,128)(2,1)S(1)} %bitcast.34, ...), custom_call_target="tpu_custom_call" | custom-call | flops 12000000000 | bytes 4000000 | tf_op jit(solution)/shard_map/conv_forward/pallas_call | solution.py:663
  50.3 3.6 %flip_table.1.flip_in = bf16[12,384,384]{2,1,0:T(8,128)(2,1)} custom-call(bf16[12,384,384]{2,1,0:T(8,128)(2,1)} %legendre_table.1.table_in), custom_call_target="tpu_custom_call" | custom-call | flops 100000000 | bytes 7000000 | tf_op jit(solution)/shard_map/flip_table/pallas_call | solution.py:337
  54.6 2.1 %all-to-all-done.1.recv_ref = bf16[32,56,128]{2,1,0:T(8,128)(2,1)S(1)} async-done(((bf16[32,56,128]{2,1,0:T(8,128)(2,1)}), bf16[32,56,128]{2,1,0:T(8,128)(2,1)S(1)}, u32[]{:S(2)}, u32[]{:S(2)}) %all-to-all-start.1) | async-done | bytes 458784 | tf_op jit(solution)/shard_map/all_to_all | solution.py:797
  57.4 5.7 %all-to-all-start.2 = ((bf16[8,12,24,128]{3,2,1,0:T(8,128)(2,1)}), bf16[8,12,24,128]{3,2,1,0:T(8,128)(2,1)S(1)}, u32[]{:S(2)}, u32[]{:S(2)}) async-start(bf16[8,12,24,128]{3,2,1,0:T(8,128)(2,1)} %get-tuple-element.38), calls=%async_computation.2 | async-start | bytes 1179648 | tf_op jit(solution)/shard_map/all_to_all | solution.py:805
  63.1 9.4 %filter_step.2.refs_3_ = bf16[32,56,128]{2,1,0:T(8,128)(2,1)} custom-call(s32[1]{0:T(128)} %bitcast.idx_ref.refs_0_, s32[1]{0:T(128)} %bitcast.1.idx_ref.lon_ref, bf16[32,56,128]{2,1,0:T(8,128)(2,1)} %copy-done.19, f32[192,384]{1,0:T(8,128)} %bitcast.47, f32[384,128]{1,0:T(8,128)} %constant.95.clone.post_ref, bf16[12,384,384]{2,1,0:T(8,128)(2,1)} %legendre_table.1.table_in, ...), custom_call_target="tpu_custom_call" | custom-call | flops 8000000000 | bytes 9000000 | tf_op jit(solution)/shard_map/filter_step/pallas_call | solution.py:391
  73.5 2.0 %analysis.3 = bf16[32,112,128]{2,1,0:T(8,128)(2,1)} custom-call(bf16[8,12,24,128]{3,2,1,0:T(8,128)(2,1)S(1)} %all-to-all-done.2.refs_0_, bf16[768,1024]{1,0:T(8,128)(2,1)S(1)} %lon_table.1.refs_1_.tab_ref, f32[1,288]{1,0:T(1,128)S(1)} %constant_dynamic-slice_fusion.4.refs_2_, bf16[32,56,128]{2,1,0:T(8,128)(2,1)S(1)} %copy-done.6), custom_call_target="tpu_custom_call" | custom-call | flops 452984832 | bytes 3000000 | tf_op jit(solution)/shard_map/analysis/pallas_call | solution.py:202
  75.5 7.8 %all-to-all-start.3 = ((bf16[32,112,128]{2,1,0:T(8,128)(2,1)}), bf16[32,112,128]{2,1,0:T(8,128)(2,1)S(1)}, u32[]{:S(2)}, u32[]{:S(2)}) async-start(bf16[32,112,128]{2,1,0:T(8,128)(2,1)} %analysis.3), calls=%async_computation.3 | async-start | bytes 1835008 | tf_op jit(solution)/shard_map/all_to_all | solution.py:808
  87.8 23.0 %all-to-all-done.3.recv_ref = bf16[32,112,128]{2,1,0:T(8,128)(2,1)S(1)} async-done(((bf16[32,112,128]{2,1,0:T(8,128)(2,1)}), bf16[32,112,128]{2,1,0:T(8,128)(2,1)S(1)}, u32[]{:S(2)}, u32[]{:S(2)}) %all-to-all-start.3) | async-done | bytes 917536 | tf_op jit(solution)/shard_map/all_to_all | solution.py:808
  112.5 5.5 %all-to-all-start.6 = ((bf16[8,12,24,128]{3,2,1,0:T(8,128)(2,1)}), bf16[8,12,24,128]{3,2,1,0:T(8,128)(2,1)S(1)}, u32[]{:S(2)}, u32[]{:S(2)}) async-start(bf16[8,12,24,128]{3,2,1,0:T(8,128)(2,1)} %copy-done.2), calls=%async_computation.6 | async-start | bytes 1179648 | tf_op jit(solution)/shard_map/all_to_all | solution.py:812
  118.0 9.5 %filter_step.3 = bf16[32,56,128]{2,1,0:T(8,128)(2,1)} custom-call(s32[1]{0:T(128)} %bitcast.idx_ref.refs_0_, s32[1]{0:T(128)} %bitcast.1.idx_ref.lon_ref, bf16[32,112,128]{2,1,0:T(8,128)(2,1)} %copy-done, f32[192,384]{1,0:T(8,128)} %bitcast.48, f32[384,128]{1,0:T(8,128)} %constant.95.clone.post_ref, bf16[12,384,384]{2,1,0:T(8,128)(2,1)} %legendre_table.1.table_in, ...), custom_call_target="tpu_custom_call" | custom-call | flops 8000000000 | bytes 9000000 | tf_op jit(solution)/shard_map/filter_step/pallas_call | solution.py:391
  127.5 3.9 %all-to-all-start.4 = ((bf16[32,56,128]{2,1,0:T(8,128)(2,1)}), bf16[32,56,128]{2,1,0:T(8,128)(2,1)S(1)}, u32[]{:S(2)}, u32[]{:S(2)}) async-start(bf16[32,56,128]{2,1,0:T(8,128)(2,1)} %filter_step.3), calls=%async_computation.4 | async-start | bytes 917504 | tf_op jit(solution)/shard_map/all_to_all | solution.py:814
  133.2 3.1 %collective-permute-start.3 = (bf16[40,128]{1,0:T(8,128)(2,1)S(1)}, bf16[40,128]{1,0:T(8,128)(2,1)S(1)}, u32[]{:S(2)}, u32[]{:S(2)}) collective-permute-start(bf16[40,128]{1,0:T(8,128)(2,1)S(1)} %get-tuple-element.51), channel_id=1, source_target_pairs={{0,7},{1,0},{2,1},{3,2},{4,3},{5,4},{6,5},{7,6},{8,15},{9,8},{10,9... | collective-permute-start | bytes 30728 | tf_op jit(solution)/shard_map/ppermute | solution.py:819
  137.7 4.4 %collective-permute-done.2.refs_3_ = bf16[40,128]{1,0:T(8,128)(2,1)S(1)} collective-permute-done((bf16[40,128]{1,0:T(8,128)(2,1)S(1)}, bf16[40,128]{1,0:T(8,128)(2,1)S(1)}, u32[]{:S(2)}, u32[]{:S(2)}) %collective-permute-start.2) | collective-permute-done | bytes 10272 | tf_op jit(solution)/shard_map/ppermute | solution.py:818
  143.4 5.4 %collective-permute-start.5 = (bf16[400,128]{1,0:T(8,128)(2,1)}, bf16[400,128]{1,0:T(8,128)(2,1)S(1)}, u32[]{:S(2)}, u32[]{:S(2)}) collective-permute-start(bf16[400,128]{1,0:T(8,128)(2,1)} %pad_maximum_fusion.3), channel_id=1, source_target_pairs={{0,248},{8,0},{16,8},{24,16},{32,24},{40,32},{48,40},{56,48},{64,5... | collective-permute-start | bytes 307208 | tf_op jit(solution)/shard_map/ppermute | solution.py:702
  151.7 5.7 %all-to-all-start.5 = ((bf16[8,12,24,128]{3,2,1,0:T(8,128)(2,1)}), bf16[8,12,24,128]{3,2,1,0:T(8,128)(2,1)S(1)}, u32[]{:S(2)}, u32[]{:S(2)}) async-start(bf16[8,12,24,128]{3,2,1,0:T(8,128)(2,1)} %synthesis.2), calls=%async_computation.5 | async-start | bytes 1179648 | tf_op jit(solution)/shard_map/all_to_all | solution.py:815
  159.5 9.3 %conv_adjoint.1 = bf16[12,192,128]{2,1,0:T(8,128)(2,1)} custom-call(bf16[12,192,128]{2,1,0:T(8,128)(2,1)S(1)} %copy-done.11, bf16[400,128]{1,0:T(8,128)(2,1)S(1)} %collective-permute-done.4.refs_1_, bf16[400,128]{1,0:T(8,128)(2,1)S(1)} %collective-permute-done.5.refs_2_, bf16[40,128]{1,0:T(8,128)(2,1)S(1)} %collective-permute-done.2.refs_3_, ...), custom_call_target="tpu_custom_call" | custom-call | flops 12000000000 | bytes 4000000 | tf_op jit(solution)/shard_map/conv_adjoint/pallas_call | solution.py:680
  (87 shorter events, 23.1 us)
Async XLA Ops:
  3.2 6.1 %copy-start.20 = (s32[384,5]{0,1:T(8,128)S(1)}, s32[384,5]{0,1:T(8,128)}, u32[]{:S(2)}) copy-start(s32[384,5]{0,1:T(8,128)} %param.18) | copy-start | bytes 23044
  3.2 6.3 %copy-start.18 = (f32[384,5,5,9]{0,2,3,1:T(8,128)S(1)}, f32[384,5,5,9]{0,2,3,1:T(8,128)}, u32[]{:S(2)}) copy-start(f32[384,5,5,9]{0,2,3,1:T(8,128)} %param.17) | copy-start | bytes 1036804
  3.2 6.7 %copy-start.21 = (s32[768]{0:T(1024)S(1)}, s32[768]{0:T(1024)}, u32[]{:S(2)}) copy-start(s32[768]{0:T(1024)} %constant.88.clone) | copy-start | bytes 9220
  3.2 6.7 %copy-start.22 = (s32[768]{0:T(1024)S(1)}, s32[768]{0:T(1024)}, u32[]{:S(2)}) copy-start(s32[768]{0:T(1024)} %constant.87.clone) | copy-start | bytes 9220
  3.2 17.9 %all-to-all-start = ((bf16[8,336,128]{2,1,0:T(8,128)(2,1)}), bf16[8,336,128]{2,1,0:T(8,128)(2,1)S(1)}, u32[]{:S(2)}, u32[]{:S(2)}) async-start(bf16[8,336,128]{2,1,0:T(8,128)(2,1)} %start.1), calls=%async_computation | async-start | bytes 1376256 | tf_op jit(solution)/shard_map/all_to_all | solution.py:764
  9.2 2.3 %copy-start.9 = (f32[768,16]{1,0:T(8,128)S(1)}, f32[768,16]{1,0:T(8,128)}, u32[]{:S(2)}) copy-start(f32[768,16]{1,0:T(8,128)} %constant.89.clone.far_ref) | copy-start | bytes 147460
  9.9 28.3 %copy-start.12 = (bf16[16,16,25]{2,1,0:T(8,128)(2,1)}, bf16[16,16,25]{2,1,0:T(8,128)(2,1)S(1)}, u32[]{:S(2)}) copy-start(bf16[16,16,25]{2,1,0:T(8,128)(2,1)S(1)} %pad.15.clone) | copy-start | bytes 38404
  13.2 7.8 %copy-start.1 = (bf16[1,12,192,128]{3,2,1,0:T(8,128)(2,1)S(1)}, bf16[1,12,192,128]{3,2,1,0:T(8,128)(2,1)}, u32[]{:S(2)}) copy-start(bf16[1,12,192,128]{3,2,1,0:T(8,128)(2,1)} %param.16) | copy-start | bytes 1769476
  21.1 8.7 %collective-permute-start = (bf16[400,128]{1,0:T(8,128)(2,1)S(1)}, bf16[400,128]{1,0:T(8,128)(2,1)S(1)}, u32[]{:S(2)}, u32[]{:S(2)}) collective-permute-start(bf16[400,128]{1,0:T(8,128)(2,1)S(1)} %pad_maximum_fusion), channel_id=1, source_target_pairs={{0,8},{8,16},{16,24},{24,32},{32,40},{40,48},{48,56},{56,64},{64,7... | collective-permute-start | bytes 307208 | tf_op jit(solution)/shard_map/ppermute | solution.py:701
  21.3 16.9 %copy-start.7 = (bf16[4,9,48,48]{3,2,1,0:T(8,128)(2,1)S(1)}, bf16[4,9,48,48]{3,2,1,0:T(8,128)(2,1)}, u32[]{:S(2)}) copy-start(bf16[4,9,48,48]{3,2,1,0:T(8,128)(2,1)} %param.19) | copy-start | bytes 497668
  21.3 8.6 %collective-permute-start.1 = (bf16[400,128]{1,0:T(8,128)(2,1)S(1)}, bf16[400,128]{1,0:T(8,128)(2,1)S(1)}, u32[]{:S(2)}, u32[]{:S(2)}) collective-permute-start(bf16[400,128]{1,0:T(8,128)(2,1)S(1)} %pad_maximum_fusion.1), channel_id=1, source_target_pairs={{0,248},{8,0},{16,8},{24,16},{32,24},{40,32},{48,40},{56,48},{64,5... | collective-permute-start | bytes 307208 | tf_op jit(solution)/shard_map/ppermute | solution.py:702
  30.5 26.1 %all-to-all-start.1 = ((bf16[32,56,128]{2,1,0:T(8,128)(2,1)}), bf16[32,56,128]{2,1,0:T(8,128)(2,1)S(1)}, u32[]{:S(2)}, u32[]{:S(2)}) async-start(bf16[32,56,128]{2,1,0:T(8,128)(2,1)} %analysis.2), calls=%async_computation.1 | async-start | bytes 917504 | tf_op jit(solution)/shard_map/all_to_all | solution.py:797
  57.4 15.1 %all-to-all-start.2 = ((bf16[8,12,24,128]{3,2,1,0:T(8,128)(2,1)}), bf16[8,12,24,128]{3,2,1,0:T(8,128)(2,1)S(1)}, u32[]{:S(2)}, u32[]{:S(2)}) async-start(bf16[8,12,24,128]{3,2,1,0:T(8,128)(2,1)} %get-tuple-element.38), calls=%async_computation.2 | async-start | bytes 1179648 | tf_op jit(solution)/shard_map/all_to_all | solution.py:805
  75.5 35.2 %all-to-all-start.3 = ((bf16[32,112,128]{2,1,0:T(8,128)(2,1)}), bf16[32,112,128]{2,1,0:T(8,128)(2,1)S(1)}, u32[]{:S(2)}, u32[]{:S(2)}) async-start(bf16[32,112,128]{2,1,0:T(8,128)(2,1)} %analysis.3), calls=%async_computation.3 | async-start | bytes 1835008 | tf_op jit(solution)/shard_map/all_to_all | solution.py:808
  112.5 14.9 %all-to-all-start.6 = ((bf16[8,12,24,128]{3,2,1,0:T(8,128)(2,1)}), bf16[8,12,24,128]{3,2,1,0:T(8,128)(2,1)S(1)}, u32[]{:S(2)}, u32[]{:S(2)}) async-start(bf16[8,12,24,128]{3,2,1,0:T(8,128)(2,1)} %copy-done.2), calls=%async_computation.6 | async-start | bytes 1179648 | tf_op jit(solution)/shard_map/all_to_all | solution.py:812
  127.5 22.6 %all-to-all-start.4 = ((bf16[32,56,128]{2,1,0:T(8,128)(2,1)}), bf16[32,56,128]{2,1,0:T(8,128)(2,1)S(1)}, u32[]{:S(2)}, u32[]{:S(2)}) async-start(bf16[32,56,128]{2,1,0:T(8,128)(2,1)} %filter_step.3), calls=%async_computation.4 | async-start | bytes 917504 | tf_op jit(solution)/shard_map/all_to_all | solution.py:814
  131.4 1.3 copy-start.4
  133.2 10.2 %copy-start.10 = (bf16[12,192,128]{2,1,0:T(8,128)(2,1)}, bf16[12,192,128]{2,1,0:T(8,128)(2,1)S(1)}, u32[]{:S(2)}) copy-start(bf16[12,192,128]{2,1,0:T(8,128)(2,1)S(1)} %get-tuple-element.49.refs_0_) | copy-start | bytes 1769476
  133.2 4.5 %collective-permute-start.3 = (bf16[40,128]{1,0:T(8,128)(2,1)S(1)}, bf16[40,128]{1,0:T(8,128)(2,1)S(1)}, u32[]{:S(2)}, u32[]{:S(2)}) collective-permute-start(bf16[40,128]{1,0:T(8,128)(2,1)S(1)} %get-tuple-element.51), channel_id=1, source_target_pairs={{0,7},{1,0},{2,1},{3,2},{4,3},{5,4},{6,5},{7,6},{8,15},{9,8},{10,9... | collective-permute-start | bytes 30728 | tf_op jit(solution)/shard_map/ppermute | solution.py:819
  136.3 5.8 %collective-permute-start.2 = (bf16[40,128]{1,0:T(8,128)(2,1)S(1)}, bf16[40,128]{1,0:T(8,128)(2,1)S(1)}, u32[]{:S(2)}, u32[]{:S(2)}) collective-permute-start(bf16[40,128]{1,0:T(8,128)(2,1)S(1)} %get-tuple-element.50), channel_id=1, source_target_pairs={{0,1},{1,2},{2,3},{3,4},{4,5},{5,6},{6,7},{7,0},{8,9},{9,10},{10,1... | collective-permute-start | bytes 30728 | tf_op jit(solution)/shard_map/ppermute | solution.py:818
  142.8 14.7 %collective-permute-start.4 = (bf16[400,128]{1,0:T(8,128)(2,1)}, bf16[400,128]{1,0:T(8,128)(2,1)S(1)}, u32[]{:S(2)}, u32[]{:S(2)}) collective-permute-start(bf16[400,128]{1,0:T(8,128)(2,1)} %pad_maximum_fusion.2), channel_id=1, source_target_pairs={{0,8},{8,16},{16,24},{24,32},{32,40},{40,48},{48,56},{56,64},{64,7... | collective-permute-start | bytes 307208 | tf_op jit(solution)/shard_map/ppermute | solution.py:701
  143.4 14.0 %copy-start.5 = (bf16[1,12,192,128]{3,2,1,0:T(8,128)(2,1)S(1)}, bf16[1,12,192,128]{3,2,1,0:T(8,128)(2,1)}, u32[]{:S(2)}) copy-start(bf16[1,12,192,128]{3,2,1,0:T(8,128)(2,1)} %param.21) | copy-start | bytes 1769476
  143.4 14.0 %collective-permute-start.5 = (bf16[400,128]{1,0:T(8,128)(2,1)}, bf16[400,128]{1,0:T(8,128)(2,1)S(1)}, u32[]{:S(2)}, u32[]{:S(2)}) collective-permute-start(bf16[400,128]{1,0:T(8,128)(2,1)} %pad_maximum_fusion.3), channel_id=1, source_target_pairs={{0,248},{8,0},{16,8},{24,16},{32,24},{40,32},{48,40},{56,48},{64,5... | collective-permute-start | bytes 307208 | tf_op jit(solution)/shard_map/ppermute | solution.py:702
  151.7 17.1 %all-to-all-start.5 = ((bf16[8,12,24,128]{3,2,1,0:T(8,128)(2,1)}), bf16[8,12,24,128]{3,2,1,0:T(8,128)(2,1)S(1)}, u32[]{:S(2)}, u32[]{:S(2)}) async-start(bf16[8,12,24,128]{3,2,1,0:T(8,128)(2,1)} %synthesis.2), calls=%async_computation.5 | async-start | bytes 1179648 | tf_op jit(solution)/shard_map/all_to_all | solution.py:815
  (12 other events, 10.8 us)
